TPU v7x, 512 devices: a whole 4x8x8 slice. The times are simulated.
512 devices in a mesh: dp: 16 (over y, core), expert: 32 (over z, x).
Axes of the slice: x: 4, y: 8, z: 8, core: 2. Of those that a mesh axis runs over, the one named last changes fastest.
Arguments:
- tokens: bfloat16 [65536, 2048], P(('dp', 'expert')), may hold values from -6 to 6
- output_gradient: bfloat16 [65536, 2048], P(('dp', 'expert')), may hold values from -6 to 6
- selected_expert_index: int32 [65536, 8], P(('dp', 'expert')), may hold values from 0 to 95, as said below
- routing_weight_rows: float32 [65536, 8], P(('dp', 'expert')), may hold values from 0.05 to 1
- fixed_gate_up_weight: bfloat16 [32, 2048, 2048], P('expert', 'dp'), may hold values from -0.125 to 0.125
- fixed_down_weight_flipped: bfloat16 [32, 2048, 1024], P('expert', 'dp'), may hold values from -0.1875 to 0.1875
- gate_up_adapter_narrow: bfloat16 [32, 2048, 128], P('expert'), may hold values from -0.125 to 0.125
- gate_up_adapter_widen: bfloat16 [32, 128, 1024], P('expert'), may hold values from -0.75 to 0.75
- down_adapter_narrow: bfloat16 [32, 1024, 64], P('expert'), may hold values from -0.1875 to 0.1875
- down_adapter_widen: bfloat16 [32, 64, 2048], P('expert'), may hold values from -0.75 to 0.75
Outputs:
- grad_in_a: float32 [32, 2048, 128], P('expert', 'dp')
- grad_in_b: float32 [32, 128, 1024], P('expert', 'dp')
- grad_down_a: float32 [32, 1024, 64], P('expert', 'dp')
- grad_down_b: float32 [32, 64, 2048], P('expert', 'dp')
Inputs may be any that keep to these rules, and one draw needn't show every extreme that they name: `selected_expert_index`: within the 128 tokens of one device no expert is chosen more than 16 times, and some experts are chosen exactly 16 times; no token chooses an expert twice.
All inputs are finite; a program needn't handle non-finite values.
Results may differ from a plain program's by a relative error of at most 0.0059.
Values may be sent and summed in bfloat16 or wider, within the bound.
No kernel may reach another device: no remote copies, remote signals or barrier semaphores. Data moves between devices by JAX's collectives and lax.ppermute only.
A program may use at most 64 MiB of HBM per device.

v0:
```python
import math

import jax
import jax.numpy as jnp
from jax import lax
from jax.sharding import PartitionSpec as P


def slot_table(block_ids, experts, capacity):
    flat = block_ids.reshape(-1)
    onehot = (flat[:, None] == jnp.arange(experts, dtype=jnp.int32)[None, :]).astype(jnp.int32)
    before = jnp.cumsum(onehot, axis=0) - onehot
    slot_pos = jnp.sum(before * onehot, axis=1)
    dest = jnp.where(flat < experts, flat * capacity + slot_pos, -1)
    match = dest[:, None] == jnp.arange(experts * capacity, dtype=jnp.int32)[None, :]
    filled = jnp.any(match, axis=0)
    rows = jnp.arange(flat.shape[0], dtype=jnp.int32)
    source = jnp.sum(jnp.where(match, rows[:, None], 0), axis=0)
    return (source, filled)


def body(
    tokens,
    output_gradient,
    selected_expert_index,
    routing_weight_rows,
    fixed_gate_up_weight,
    fixed_down_weight_flipped,
    gate_up_adapter_narrow,
    gate_up_adapter_widen,
    down_adapter_narrow,
    down_adapter_widen,
):
    experts = lax.axis_size("expert")
    tok_rows = tokens.shape[0]
    topk = selected_expert_index.shape[1]
    capacity = tok_rows // 8
    width = fixed_down_weight_flipped.shape[2]
    model_width = tokens.shape[1]
    adapter_rank_size = down_adapter_narrow.shape[2]
    routing_factor = 0.5 / math.sqrt(tok_rows * lax.axis_size("dp") * experts)
    source, filled = slot_table(selected_expert_index, experts, capacity)
    tok_index = source // topk
    pick = source % topk
    x_send = jnp.where(filled[:, None], tokens[tok_index], jnp.zeros((), jnp.bfloat16))
    weight = routing_weight_rows[tok_index, pick]
    y_send = (weight[:, None] * output_gradient[tok_index].astype(jnp.float32)).astype(jnp.bfloat16)
    y_send = jnp.where(filled[:, None], y_send, jnp.zeros((), jnp.bfloat16))
    x_send = x_send.reshape(experts, capacity, model_width)
    y_send = y_send.reshape(experts, capacity, model_width)
    x_recv, y_recv = (
        lax.all_to_all(x_send, "expert", split_axis=0, concat_axis=0, tiled=True),
        lax.all_to_all(y_send, "expert", split_axis=0, concat_axis=0, tiled=True),
    )
    slots = experts * capacity
    expert_input_rows = x_recv.reshape(slots, model_width)
    output_cotangent_rows = y_recv.reshape(slots, model_width)
    base = jnp.dot(
        expert_input_rows,
        lax.all_gather(fixed_gate_up_weight[0], "dp", axis=0, tiled=True),
        preferred_element_type=jnp.float32,
    )
    input_adapter_lower = gate_up_adapter_narrow[0]
    input_adapter_upper = gate_up_adapter_widen[0]
    down_adapter_lower = down_adapter_narrow[0]
    down_adapter_upper = down_adapter_widen[0]
    low = jnp.dot(
        expert_input_rows, input_adapter_lower, preferred_element_type=jnp.float32
    ).astype(jnp.bfloat16)
    gate = base[:, :width] + 0.5 * jnp.dot(
        low[:, :adapter_rank_size],
        input_adapter_upper[:adapter_rank_size],
        preferred_element_type=jnp.float32,
    )
    up = base[:, width:] + 0.5 * jnp.dot(
        low[:, adapter_rank_size:],
        input_adapter_upper[adapter_rank_size:],
        preferred_element_type=jnp.float32,
    )
    sig = jax.nn.sigmoid(gate)
    silu = gate * sig
    hidden = (silu * up).astype(jnp.bfloat16)
    hlow = jnp.dot(hidden, down_adapter_lower, preferred_element_type=jnp.float32).astype(
        jnp.bfloat16
    )
    zlow = jnp.dot(
        output_cotangent_rows, down_adapter_upper.T, preferred_element_type=jnp.float32
    ).astype(jnp.bfloat16)
    dbase = jnp.dot(
        output_cotangent_rows,
        lax.all_gather(fixed_down_weight_flipped[0], "dp", axis=0, tiled=True),
        preferred_element_type=jnp.float32,
    )
    dhid = dbase + 0.5 * jnp.dot(zlow, down_adapter_lower.T, preferred_element_type=jnp.float32)
    dgate = (dhid * up * sig * (1.0 + gate * (1.0 - sig))).astype(jnp.bfloat16)
    dup = (dhid * silu).astype(jnp.bfloat16)
    vlow = jnp.concatenate(
        [
            jnp.dot(
                dgate, input_adapter_upper[:adapter_rank_size].T, preferred_element_type=jnp.float32
            ),
            jnp.dot(
                dup, input_adapter_upper[adapter_rank_size:].T, preferred_element_type=jnp.float32
            ),
        ],
        axis=1,
    ).astype(jnp.bfloat16)
    term_ia = routing_factor * jnp.dot(
        expert_input_rows.T, vlow, preferred_element_type=jnp.float32
    )
    term_ib = routing_factor * jnp.concatenate(
        [
            jnp.dot(low[:, :adapter_rank_size].T, dgate, preferred_element_type=jnp.float32),
            jnp.dot(low[:, adapter_rank_size:].T, dup, preferred_element_type=jnp.float32),
        ],
        axis=0,
    )
    term_da = routing_factor * jnp.dot(hidden.T, zlow, preferred_element_type=jnp.float32)
    term_db = routing_factor * jnp.dot(
        hlow.T, output_cotangent_rows, preferred_element_type=jnp.float32
    )
    grad_ia, grad_ib, grad_da, grad_db = (
        lax.psum_scatter(term_ia[None], "dp", scatter_dimension=1, tiled=True),
        lax.psum_scatter(term_ib[None], "dp", scatter_dimension=1, tiled=True),
        lax.psum_scatter(term_da[None], "dp", scatter_dimension=1, tiled=True),
        lax.psum_scatter(term_db[None], "dp", scatter_dimension=1, tiled=True),
    )
    return (grad_ia, grad_ib, grad_da, grad_db)


def solution(mesh):
    in_specs = (
        P(("dp", "expert"), None),
        P(("dp", "expert"), None),
        P(("dp", "expert"), None),
        P(("dp", "expert"), None),
        P("expert", "dp", None),
        P("expert", "dp", None),
        P("expert", None, None),
        P("expert", None, None),
        P("expert", None, None),
        P("expert", None, None),
    )
    out_specs = (
        P("expert", "dp", None),
        P("expert", "dp", None),
        P("expert", "dp", None),
        P("expert", "dp", None),
    )
    return jax.shard_map(body, mesh=mesh, in_specs=in_specs, out_specs=out_specs, check_vma=False)
```

profile of v0, /device:TPU:6, one launch (start us, length us, event | category | flops | bytes accessed | tf_op | source)
XLA Modules:
  0.0 481.1 jit_solution(11849060724557583329)
XLA Ops:
  9.7 9.0 %reduce-window.6 = s32[32,8,128]{2,1,0:T(8,128)S(1)} reduce-window(s32[32,8,128]{2,1,0:T(8,128)S(1)} %fusion.26, s32[]{:T(128)} %constant.24.clone.1), window={size=1x1x128 pad=0_0x0_0x127_0}, to_apply=%region_0.0 | reduce-window | flops 4161536 | bytes 262148 | tf_op jit(solution)/shard_map/reduce-window
  19.5 2.5 gather_fusion.1
  22.6 2.5 gather_fusion.2
  25.1 3.3 gather_fusion
  28.4 4.4 fusion.7
  32.8 63.9 %all_to_all.10 = bf16[32,16,2048]{2,1,0:T(8,128)(2,1)} all-to-all(bf16[32,16,2048]{2,1,0:T(8,128)(2,1)S(1)} %get-tuple-element.25), channel_id=1, replica_groups=mesh['dp'=16,'expert'=32] {'expert'}, dimensions={0} | all-to-all | bytes 4194304 | tf_op jit(solution)/shard_map/all_to_all | solution.py:53
  96.7 5.7 %all-to-all-start = ((bf16[32,16,2048]{2,1,0:T(8,128)(2,1)}), bf16[32,16,2048]{2,1,0:T(8,128)(2,1)S(1)}, u32[]{:S(2)}, u32[]{:S(2)}) async-start(bf16[32,16,2048]{2,1,0:T(8,128)(2,1)} %get-tuple-element.26), calls=%async_computation | async-start | bytes 4194304 | tf_op jit(solution)/shard_map/all_to_all | solution.py:52
  102.6 2.4 convolution_convert_fusion.4
  105.0 46.9 %all-to-all-done = bf16[32,16,2048]{2,1,0:T(8,128)(2,1)S(1)} async-done(((bf16[32,16,2048]{2,1,0:T(8,128)(2,1)}), bf16[32,16,2048]{2,1,0:T(8,128)(2,1)S(1)}, u32[]{:S(2)}, u32[]{:S(2)}) %all-to-all-start) | async-done | bytes 2097184 | tf_op jit(solution)/shard_map/all_to_all | solution.py:52
  151.9 1.9 convolution_convert_fusion
  153.8 5.2 %fusion.3 = f32[512,1024]{1,0:T(8,128)S(1)} fusion(bf16[512,2048]{1,0:T(8,128)(2,1)} %bitcast.96, bf16[1,2048,1024]{2,1,0:T(8,128)(2,1)} %all-gather.5.cloned.1.call-done), kind=kOutput, calls=%fused_computation.7 | convolution fusion | flops 2147483648 | bytes 8388608 | tf_op jit(solution)/shard_map/dot_general | solution.py:89
  159.0 1.8 multiply_add_fusion
  160.8 6.9 %fusion = f32[512,2048]{1,0:T(8,128)S(1)} fusion(bf16[512,2048]{1,0:T(8,128)(2,1)S(1)} %bitcast.93, bf16[1,2048,2048]{2,1,0:T(8,128)(2,1)} %all-gather.7.cloned.1.call-done), kind=kOutput, calls=%fused_computation.3 | convolution fusion | flops 4294967296 | bytes 14680064 | tf_op jit(solution)/shard_map/dot_general | solution.py:58
  169.3 3.0 multiply_convert_fusion
  172.3 3.6 fusion.6
  176.0 1.5 fusion.10
  178.6 1.5 convolution_bitcast_fusion
  182.6 1.7 convolution_convert_fusion.2
  184.3 1.7 convolution_convert_fusion.3
  185.9 1.7 fusion.5
  189.6 98.1 %all-reduce.3.cloned.1.call-done = f32[1,64,2048]{2,1,0:T(8,128)} async-done(((f32[1,64,2048]{2,1,0:T(8,128)}), f32[1,64,2048]{2,1,0:T(8,128)}) %all-reduce.3.cloned.1.call-update) | async-done | bytes 524304
  289.2 61.7 %reduce-scatter.11.cloned.1.call-done = f32[64,64]{1,0:T(8,128)} async-done(((f32[1024,64]{1,0:T(8,128)}), f32[64,64]{1,0:T(8,128)}) %reduce-scatter.11.cloned.1.call-update) | async-done | bytes 16400
  350.9 61.1 %reduce-scatter.9.cloned.1.call-done = f32[1,8,1024]{2,1,0:T(8,128)} async-done(((f32[1,128,1024]{2,1,0:T(8,128)}), f32[1,8,1024]{2,1,0:T(8,128)}) %reduce-scatter.9.cloned.1.call-update) | async-done | bytes 32784 | tf_op jit(solution)/shard_map/reduce_scatter | solution.py:124
  412.0 62.3 %reduce-scatter.7.cloned.1.call-done = f32[1,128,128]{2,1,0:T(8,128)} async-done(((f32[1,2048,128]{2,1,0:T(8,128)}), f32[1,128,128]{2,1,0:T(8,128)}) %reduce-scatter.7.cloned.1.call-update) | async-done | bytes 65552 | tf_op jit(solution)/shard_map/reduce_scatter | solution.py:123
  (52 shorter events, 11.9 us)
Async XLA Ops:
  7.2 15.5 %copy-start = (bf16[128,2048]{1,0:T(8,128)(2,1)S(1)}, bf16[128,2048]{1,0:T(8,128)(2,1)}, u32[]{:S(2)}) copy-start(bf16[128,2048]{1,0:T(8,128)(2,1)} %param.11) | copy-start | bytes 1572868
  7.2 12.4 %copy-start.1 = (f32[128,8]{0,1:T(8,128)S(1)}, f32[128,8]{0,1:T(8,128)}, u32[]{:S(2)}) copy-start(f32[128,8]{0,1:T(8,128)} %param.13) | copy-start | bytes 12292
  7.2 146.6 %all-gather.5.cloned.1.call-start = ((), (), s32[]{:S(2)}) async-start(), calls=%async_computation.7 | async-start | bytes 4456448 | tf_op jit(solution)/shard_map/all_gather | solution.py:91
  7.9 152.9 %all-gather.7.cloned.1.call-start = ((), (), s32[]{:S(2)}) async-start(), calls=%async_computation.8 | async-start | bytes 8912896 | tf_op jit(solution)/shard_map/all_gather | solution.py:60
  22.6 2.5 copy-start.2
  96.7 5.9 %copy-start.6 = (bf16[1,64,2048]{2,1,0:T(8,128)(2,1)S(1)}, bf16[1,64,2048]{2,1,0:T(8,128)(2,1)}, u32[]{:S(2)}) copy-start(bf16[1,64,2048]{2,1,0:T(8,128)(2,1)} %param.19) | copy-start | bytes 786436
  96.7 55.2 %all-to-all-start = ((bf16[32,16,2048]{2,1,0:T(8,128)(2,1)}), bf16[32,16,2048]{2,1,0:T(8,128)(2,1)S(1)}, u32[]{:S(2)}, u32[]{:S(2)}) async-start(bf16[32,16,2048]{2,1,0:T(8,128)(2,1)} %get-tuple-element.26), calls=%async_computation | async-start | bytes 4194304 | tf_op jit(solution)/shard_map/all_to_all | solution.py:52
  102.4 185.4 %all-reduce.3.cloned.1.call-start = ((), (), s32[]{:S(2)}) async-start(), calls=%async_computation.10 | async-start | bytes 1048576
  153.7 5.2 %copy-start.5 = (bf16[1,1024,64]{1,2,0:T(8,128)(2,1)S(1)}, bf16[1,1024,64]{1,2,0:T(8,128)(2,1)}, u32[]{:S(2)}) copy-start(bf16[1,1024,64]{1,2,0:T(8,128)(2,1)} %param.18) | copy-start | bytes 393220
  160.8 6.9 %copy-start.4 = (bf16[1,128,1024]{2,1,0:T(8,128)(2,1)S(1)}, bf16[1,128,1024]{2,1,0:T(8,128)(2,1)}, u32[]{:S(2)}) copy-start(bf16[1,128,1024]{2,1,0:T(8,128)(2,1)} %param.17) | copy-start | bytes 786436
  167.7 1.6 copy-start.3
  175.9 174.9 %reduce-scatter.11.cloned.1.call-start = ((), (), s32[]{:S(2)}) async-start(), calls=%async_computation.9 | async-start | bytes 557056
  178.6 233.4 %reduce-scatter.9.cloned.1.call-start = ((), (), s32[]{:S(2)}) async-start(), calls=%async_computation.6 | async-start | bytes 557056 | tf_op jit(solution)/shard_map/reduce_scatter | solution.py:124
  182.5 291.7 %reduce-scatter.7.cloned.1.call-start = ((), (), s32[]{:S(2)}) async-start(), calls=%async_computation.5 | async-start | bytes 1114112 | tf_op jit(solution)/shard_map/reduce_scatter | solution.py:123
Sparse Core Ops, SparseCore 0:
  10.1 49.1 all-gather.4
  61.5 57.3 all-gather.6
  176.0 111.6 all-reduce.2
  291.2 59.6 reduce-scatter.10
  354.1 57.8 reduce-scatter.8
  415.5 58.7 reduce-scatter.6
where the time goes:
time: 482 us; the launch traced here: 481 us
  waiting for transfers between devices  332 us (69%)
  blocking collectives  63.9 us (13%)
  matrix products  34.8 us (7%)
  other arithmetic  15.1 us (3%)
  between operations  15 us (3%)
  local copies, waits for them, and re-layouts  14.6 us (3%)
  starting transfers between devices  6.12 us (1%)
    unnamed x8, waiting for transfers between devices  161 us
    all_to_all x1, blocking collectives, body(): lax.all_to_all(y_send, 'expert', split_axis=0, concat_axis=0, tiled=True)  63.9 us
    reduce_scatter x1, waiting for transfers between devices, body(): lax.psum_scatter(term_ia[None], 'dp', scatter_dimension=1, tiled=True)  62.3 us
    reduce_scatter x1, waiting for transfers between devices, body(): lax.psum_scatter(term_ib[None], 'dp', scatter_dimension=1, tiled=True)  61.1 us
    all_to_all x1, waiting for transfers between devices, body(): lax.all_to_all(x_send, 'expert', split_axis=0, concat_axis=0, tiled=True)  46.9 us
  transfers between devices with their start and end apart: 7, of which 5 were waited for; matrix products, arithmetic and copies ran while one was open for 10% of the time, Pallas kernels for 0%

commit v1 on v0

v1 whole, which is shorter than its diff:
```python
import functools
import math

import jax
import jax.numpy as jnp
from jax import lax
from jax.experimental import pallas as pl
from jax.experimental.pallas import tpu as pltpu
from jax.sharding import PartitionSpec as P

F32 = jnp.float32
BF16 = jnp.bfloat16
LANES = 128


def dot_nt(a, b):
    return lax.dot_general(a, b, (((1,), (1,)), ((), ())), preferred_element_type=F32)


def dot_nn(a, b):
    return lax.dot_general(a, b, (((1,), (0,)), ((), ())), preferred_element_type=F32)


def slot_ranks(sel, experts):
    topk, toks = sel.shape
    ids = lax.broadcasted_iota(jnp.int32, (experts, toks), 0)
    chosen = jnp.zeros((experts, toks), F32)
    for k in range(topk):
        chosen += jnp.where(sel[k : k + 1, :] == ids, 1.0, 0.0)
    earlier = lax.broadcasted_iota(jnp.int32, (toks, toks), 0) < lax.broadcasted_iota(
        jnp.int32, (toks, toks), 1
    )
    before = dot_nn(chosen.astype(BF16), jnp.where(earlier, 1.0, 0.0).astype(BF16))
    return jnp.where(chosen > 0.0, before, -1.0)


def pack_x_kernel(cap, sel_ref, tok_ref, out_ref, rank_s):
    step = pl.program_id(0)

    @pl.when(step == 0)
    def _():
        rank_s[...] = slot_ranks(sel_ref[...], rank_s.shape[0])

    rank = rank_s[pl.ds(pl.multiple_of(step * 8, 8), 8), :]
    slot = lax.broadcasted_iota(jnp.int32, (cap, rank.shape[1]), 0).astype(F32)
    onehot = jnp.concatenate(
        [jnp.where(rank[e : e + 1, :] == slot, 1.0, 0.0) for e in range(8)], axis=0
    )
    out_ref[...] = dot_nn(onehot.astype(BF16), tok_ref[...]).astype(BF16)


def pack_y_kernel(cap, sel_ref, wgt_ref, tok_ref, out_ref, rank_s, wgt_s):
    step = pl.program_id(0)

    @pl.when(step == 0)
    def _():
        sel = sel_ref[...]
        rank_s[...] = slot_ranks(sel, rank_s.shape[0])
        ids = lax.broadcasted_iota(jnp.int32, rank_s.shape, 0)
        total = jnp.zeros(rank_s.shape, F32)
        for k in range(sel.shape[0]):
            total += jnp.where(sel[k : k + 1, :] == ids, wgt_ref[k : k + 1, :], 0.0)
        wgt_s[...] = total

    rows = pl.ds(pl.multiple_of(step * 8, 8), 8)
    rank = rank_s[rows, :]
    wgt = wgt_s[rows, :]
    slot = lax.broadcasted_iota(jnp.int32, (cap, rank.shape[1]), 0).astype(F32)
    taken = [rank[e : e + 1, :] == slot for e in range(8)]
    onehot = jnp.concatenate([jnp.where(m, 1.0, 0.0) for m in taken], axis=0)
    weight = jnp.concatenate(
        [
            jnp.sum(jnp.where(taken[e], wgt[e : e + 1, :], 0.0), axis=1, keepdims=True)
            for e in range(8)
        ],
        axis=0,
    )
    out_ref[...] = (weight * dot_nn(onehot.astype(BF16), tok_ref[...])).astype(BF16)


def pack_rows(sel_t, wgt_t, tok, experts, cap):
    toks, width = tok.shape
    topk = sel_t.shape[0]
    steps = experts // 8
    whole = lambda shape: pl.BlockSpec(shape, lambda i: (0, 0))
    ranks = pltpu.VMEM((experts, toks), F32)
    common = dict(
        grid=(steps,),
        out_shape=jax.ShapeDtypeStruct((experts * cap, width), BF16),
        out_specs=pl.BlockSpec((8 * cap, width), lambda i: (i, 0)),
        cost_estimate=pl.CostEstimate(
            flops=2 * experts * cap * toks * width,
            bytes_accessed=2 * width * (toks + experts * cap),
            transcendentals=0,
        ),
        compiler_params=pltpu.CompilerParams(vmem_limit_bytes=16 * 2**20),
    )
    if wgt_t is None:
        return pl.pallas_call(
            functools.partial(pack_x_kernel, cap),
            in_specs=[whole((topk, toks)), whole((toks, width))],
            scratch_shapes=[ranks],
            name="pack_x",
            **common,
        )(sel_t, tok)
    return pl.pallas_call(
        functools.partial(pack_y_kernel, cap),
        in_specs=[whole((topk, toks)), whole((topk, toks)), whole((toks, width))],
        scratch_shapes=[ranks, ranks],
        name="pack_y",
        **common,
    )(sel_t, wgt_t, tok)


def tail_kernel(
    core_ref,
    y_ref,
    wd_ref,
    dw_ref,
    dn_ref,
    g1_ref,
    g2_ref,
    hid_ref,
    hlow_t_ref,
    low_t_ref,
    win_ref,
    x_hbm,
    keep_ref,
    send_ref,
    x_s,
    zt_s,
    z_s,
    vt_s,
    inb_s,
    dna_s,
    db_s,
    x_sem,
):
    step = pl.program_id(0)
    steps = pl.num_programs(0)
    rank = zt_s.shape[0]
    fetch_x = pltpu.make_async_copy(x_hbm, x_s, x_sem)

    @pl.when(step == 0)
    def _():
        fetch_x.start()
        zt = dot_nt(dw_ref[...], y_ref[...])
        zt_s[...] = zt.astype(BF16)
        z_s[...] = zt.T.astype(BF16)
        db_s[...] = dot_nn(hlow_t_ref[...], y_ref[...])
        vt_s[...] = jnp.zeros_like(vt_s)

    dhid = dot_nn(y_ref[...], wd_ref[...]) + 0.5 * dot_nt(z_s[...], dn_ref[...])
    dgate = (dhid * g1_ref[...]).astype(BF16)
    dup = (dhid * g2_ref[...]).astype(BF16)
    vt_s[:rank, :] += dot_nt(win_ref[:rank, :], dgate)
    vt_s[rank:, :] += dot_nt(win_ref[rank:, :], dup)
    inb_s[step, :rank, :] = dot_nn(low_t_ref[:rank, :], dgate)
    inb_s[step, rank:, :] = dot_nn(low_t_ref[rank:, :], dup)
    dna_s[step] = dot_nn(zt_s[...], hid_ref[...])

    @pl.when(step == steps - 1)
    def _():
        fetch_x.wait()
        even = core_ref[0] == 0
        ina = dot_nn(vt_s[...].astype(BF16), x_s[...])
        cols = inb_s.shape[2] // LANES
        width = db_s.shape[1] // 2
        half = rank // 2
        left = lax.broadcasted_iota(jnp.int32, (half, LANES), 1) < LANES // 2
        upper = lax.broadcasted_iota(jnp.int32, (8, LANES), 0) < 4
        for t in range(keep_ref.shape[0]):
            d = dna_s[t // cols][:, (t % cols) * LANES : (t % cols + 1) * LANES]
            top, low = d[:half], d[half:]
            middle = (
                jnp.where(left, top, pltpu.roll(low, LANES // 2, 1)),
                jnp.where(left, pltpu.roll(top, LANES // 2, 1), low),
            )
            last = ([], [])
            for b in range(width // LANES):
                p = db_s[8 * t : 8 * t + 8, b * LANES : (b + 1) * LANES]
                q = db_s[8 * t : 8 * t + 8, width + b * LANES : width + (b + 1) * LANES]
                last[0].append(jnp.where(upper, p, pltpu.roll(q, 4, 0)))
                last[1].append(jnp.where(upper, pltpu.roll(p, 4, 0), q))
            both = []
            for c in range(2):
                j = 2 * t + c
                rows = [ina[:, j * LANES : (j + 1) * LANES]]
                for s in range(inb_s.shape[0]):
                    for b in range(cols):
                        rows.append(inb_s[s, 8 * j : 8 * j + 8, b * LANES : (b + 1) * LANES])
                both.append(jnp.concatenate(rows + [middle[c]] + last[c], axis=0))
            keep_ref[t] = jnp.where(even, both[0], both[1]).astype(BF16)
            send_ref[t] = jnp.where(even, both[1], both[0]).astype(BF16)


def tail(core, y, wd, dw, dn, g1, g2, hidden, hlow_t, low_t, win, x, parts):
    slots, width = y.shape
    units = wd.shape[1]
    rank = dw.shape[0]
    block = 256
    steps = units // block
    rows = (2 * rank * units + units * rank + rank * width) // (parts * LANES) + width // parts
    whole = lambda a: pl.BlockSpec(a.shape, lambda i: (0, 0))
    cols = lambda a: pl.BlockSpec((a.shape[0], block), lambda i: (0, i))
    out = jax.ShapeDtypeStruct((parts // 2, rows, LANES), BF16)
    out_spec = pl.BlockSpec(out.shape, lambda i: (0, 0, 0))
    return pl.pallas_call(
        tail_kernel,
        grid=(steps,),
        in_specs=[
            pl.BlockSpec(memory_space=pltpu.SMEM),
            whole(y),
            cols(wd),
            whole(dw),
            pl.BlockSpec((block, rank), lambda i: (i, 0)),
            cols(g1),
            cols(g2),
            cols(hidden),
            whole(hlow_t),
            whole(low_t),
            cols(win),
            pl.BlockSpec(memory_space=pl.ANY),
        ],
        out_shape=(out, out),
        out_specs=(out_spec, out_spec),
        scratch_shapes=[
            pltpu.VMEM((slots, width), BF16),
            pltpu.VMEM((rank, slots), BF16),
            pltpu.VMEM((slots, rank), BF16),
            pltpu.VMEM((2 * rank, slots), F32),
            pltpu.VMEM((steps, 2 * rank, block), F32),
            pltpu.VMEM((steps, rank, block), F32),
            pltpu.VMEM((rank, width), F32),
            pltpu.SemaphoreType.DMA,
        ],
        cost_estimate=pl.CostEstimate(
            flops=2 * slots * width * (units + 4 * rank),
            bytes_accessed=2 * width * (2 * slots + units) + 10 * slots * units,
            transcendentals=0,
        ),
        compiler_params=pltpu.CompilerParams(vmem_limit_bytes=40 * 2**20),
        name="gradients",
    )(core, y, wd, dw, dn, g1, g2, hidden, hlow_t, low_t, win, x)


def finish_kernel(factor, parts_ref, ina_ref, inb_ref, dna_ref, dnb_ref):
    total = parts_ref[0].astype(F32)
    for i in range(1, parts_ref.shape[0]):
        total += parts_ref[i].astype(F32)
    total *= factor
    width = ina_ref.shape[1]
    ina_ref[0] = total[:width].T
    at = width
    for b in range(inb_ref.shape[2] // LANES):
        inb_ref[0, :, b * LANES : (b + 1) * LANES] = total[at : at + 8]
        at += 8
    half = dna_ref.shape[2] // 2
    d = total[at : at + half]
    at += half
    both = jnp.concatenate([d, pltpu.roll(d, LANES // 2, 1)], axis=0)
    dna_ref[0] = both.T[: dna_ref.shape[1]]
    reach = dnb_ref.shape[2] // 2
    for b in range(reach // LANES):
        e = total[at : at + 8]
        at += 8
        dnb_ref[0, :, b * LANES : (b + 1) * LANES] = e[:4]
        dnb_ref[0, :, reach + b * LANES : reach + (b + 1) * LANES] = e[4:]


def finish(parts, factor, shapes):
    return pl.pallas_call(
        functools.partial(finish_kernel, factor),
        out_shape=tuple(jax.ShapeDtypeStruct(s, F32) for s in shapes),
        name="sum_parts",
    )(parts)


def body(
    tokens,
    output_gradient,
    selected_expert_index,
    routing_weight_rows,
    fixed_gate_up_weight,
    fixed_down_weight_flipped,
    gate_up_adapter_narrow,
    gate_up_adapter_widen,
    down_adapter_narrow,
    down_adapter_widen,
):
    experts = lax.axis_size("expert")
    groups = lax.axis_size("dp")
    tok_rows, model_width = tokens.shape
    cap = tok_rows // 8
    width = fixed_down_weight_flipped.shape[2]
    rank = down_adapter_narrow.shape[2]
    slots = experts * cap
    factor = 0.5 / math.sqrt(tok_rows * groups * experts)
    sel_t = selected_expert_index.T
    wgt_t = routing_weight_rows.T

    w_gate_up = lax.all_gather(fixed_gate_up_weight[0], "dp", axis=0, tiled=True)
    w_down = lax.all_gather(fixed_down_weight_flipped[0], "dp", axis=0, tiled=True)

    x_send = pack_rows(sel_t, None, tokens, experts, cap).reshape(experts, cap, model_width)
    x = lax.all_to_all(x_send, "expert", 0, 0, tiled=True)
    y_send = pack_rows(sel_t, wgt_t, output_gradient, experts, cap)
    y_send, x = lax.optimization_barrier((y_send, x))
    y = lax.all_to_all(
        y_send.reshape(experts, cap, model_width), "expert", 0, 0, tiled=True
    ).reshape(slots, model_width)
    x = x.reshape(slots, model_width)

    narrow = gate_up_adapter_narrow[0]
    widen = gate_up_adapter_widen[0]
    down_narrow = down_adapter_narrow[0]
    down_widen = down_adapter_widen[0]
    base = jnp.dot(x, w_gate_up, preferred_element_type=F32)
    low = jnp.dot(x, narrow, preferred_element_type=F32).astype(BF16)
    gate = base[:, :width] + 0.5 * jnp.dot(low[:, :rank], widen[:rank], preferred_element_type=F32)
    up = base[:, width:] + 0.5 * jnp.dot(low[:, rank:], widen[rank:], preferred_element_type=F32)
    sig = jax.nn.sigmoid(gate)
    silu = gate * sig
    hidden = (silu * up).astype(BF16)
    g_gate = up * sig * (1.0 + gate * (1.0 - sig))
    hlow_t = lax.dot_general(
        down_narrow, hidden, (((0,), (1,)), ((), ())), preferred_element_type=F32
    ).astype(BF16)

    core = (lax.axis_index("dp") % 2).astype(jnp.int32).reshape(1)
    keep, send = tail(
        core, y, w_down, down_widen, down_narrow, g_gate, silu, hidden, hlow_t, low.T, widen, x, groups
    )
    other = lax.ppermute(send, "dp", [(i, i ^ 1) for i in range(groups)])
    pair = (keep.astype(F32) + other.astype(F32)).astype(BF16)
    lines = [[2 * i + c for i in range(groups // 2)] for c in range(2)]
    parts = lax.all_to_all(pair, "dp", 0, 0, tiled=True, axis_index_groups=lines)
    shapes = (
        (1, model_width // groups, 2 * rank),
        (1, 2 * rank // groups, width),
        (1, width // groups, rank),
        (1, rank // groups, model_width),
    )
    return finish(parts, factor, shapes)


def solution(mesh):
    in_specs = (
        P(("dp", "expert"), None),
        P(("dp", "expert"), None),
        P(("dp", "expert"), None),
        P(("dp", "expert"), None),
        P("expert", "dp", None),
        P("expert", "dp", None),
        P("expert", None, None),
        P("expert", None, None),
        P("expert", None, None),
        P("expert", None, None),
    )
    out_specs = (
        P("expert", "dp", None),
        P("expert", "dp", None),
        P("expert", "dp", None),
        P("expert", "dp", None),
    )
    return jax.shard_map(body, mesh=mesh, in_specs=in_specs, out_specs=out_specs, check_vma=False)
```

time: 482 us -> 187 us (0.39)
  waiting for transfers between devices: 332 us -> 85.4 us
  blocking collectives: 63.9 us -> 26.2 us
  matrix products: 34.8 us -> 12.4 us
  starting transfers between devices: 6.12 us -> 22 us
  other arithmetic: 15.1 us -> 0.16 us
  Pallas kernels: 0 us -> 14.6 us
    unnamed x8 -> x2, waiting for transfers between devices: 161 us -> 1.38 us
    reduce_scatter x2 -> x0, waiting for transfers between devices: 123 us -> none  [the longest x1 62.3 us: body(): lax.psum_scatter(term_ia[None], 'dp', scatter_dimension=1, tiled=True)]
    all_to_all x1, blocking collectives: 63.9 us -> 26.2 us  [body(): lax.all_to_all(pair, 'dp', 0, 0, tiled=True, axis_index_groups=lines)]
    all_gather x1, waiting for transfers between devices: 0.02 us -> 22.8 us  [body(): lax.all_gather(fixed_down_weight_flipped[0], 'dp', axis=0, tiled=True)]
    dot_general x14 -> x5, matrix products: 34.8 us -> 12.4 us  [the longest x1 6.92 us: body(): base = jnp.dot(x, w_gate_up, preferred_element_type=F32)]
    pallas_call x0 -> x4, Pallas kernels: none -> 14.6 us  [the longest x1 9.98 us: tail(): pl.pallas_call(tail_kernel, grid=(steps,), in_specs=[pl.BlockSpec(memory_...]
    all_to_all x1 -> x2, starting transfers between devices: 5.7 us -> 20 us  [the longest x1 13.6 us: body(): x = lax.all_to_all(x_send, 'expert', 0, 0, tiled=True)]
    all_to_all x1 -> x2, waiting for transfers between devices: 46.9 us -> 59.3 us  [the longest x1 46.3 us: body(): x = lax.all_to_all(x_send, 'expert', 0, 0, tiled=True)]
  transfers between devices with their start and end apart: 7 -> 5, of which waited for: 5 -> 4; matrix products, arithmetic and copies ran while one was open for 10% -> 7% of each run, Pallas kernels for 0% -> 1%
where the time goes in v1:
time: 187 us; the launch traced here: 186 us
  waiting for transfers between devices  85.4 us (46%)
  blocking collectives  26.2 us (14%)
  starting transfers between devices  22 us (12%)
  Pallas kernels  14.6 us (8%)
  between operations  14.3 us (8%)
  matrix products  12.4 us (7%)
  local copies, waits for them, and re-layouts  10.8 us (6%)
    all_to_all x1, waiting for transfers between devices, body(): x = lax.all_to_all(x_send, 'expert', 0, 0, tiled=True)  46.3 us
    all_to_all x1, blocking collectives, body(): lax.all_to_all(pair, 'dp', 0, 0, tiled=True, axis_index_groups=lines)  26.2 us
    all_gather x1, waiting for transfers between devices, body(): lax.all_gather(fixed_down_weight_flipped[0], 'dp', axis=0, tiled=True)  22.8 us
    all_to_all x1, starting transfers between devices, body(): x = lax.all_to_all(x_send, 'expert', 0, 0, tiled=True)  13.6 us
    all_to_all x1, waiting for transfers between devices, body(): lax.all_to_all(y_send.reshape(experts, cap, model_width), 'expert', 0, 0,...  13 us
    unnamed x35, local copies, waits for them, and re-layouts  10.8 us
    pallas_call x1, Pallas kernels, tail(): pl.pallas_call(tail_kernel, grid=(steps,), in_specs=[pl.BlockSpec(memory_...  9.98 us
    dot_general x1, matrix products, body(): base = jnp.dot(x, w_gate_up, preferred_element_type=F32)  6.92 us
  transfers between devices with their start and end apart: 5, of which 4 were waited for; matrix products, arithmetic and copies ran while one was open for 7% of the time, Pallas kernels for 1%

profile of v1, /device:TPU:6, one launch (start us, length us, event | category | flops | bytes accessed | tf_op | source)
XLA Modules:
  0.0 185.9 jit_solution(2674777032405131351)
XLA Ops:
  7.9 1.0 copy-done.8
  9.6 1.3 pack_x.1
  11.0 1.3 copy-done.2
  12.3 13.6 %all-to-all-start = ((bf16[32,16,2048]{2,1,0:T(8,128)(2,1)}), bf16[32,16,2048]{2,1,0:T(8,128)(2,1)S(1)}, u32[]{:S(2)}, u32[]{:S(2)}) async-start(bf16[32,16,2048]{2,1,0:T(8,128)(2,1)} %bitcast.38), calls=%async_computation | async-start | bytes 4194304 | tf_op jit(solution)/shard_map/all_to_all | solution.py:306
  26.6 1.4 pack_y.1
  28.1 1.3 copy-done.1
  29.4 46.3 %all-to-all-done = bf16[32,16,2048]{2,1,0:T(8,128)(2,1)S(1)} async-done(((bf16[32,16,2048]{2,1,0:T(8,128)(2,1)}), bf16[32,16,2048]{2,1,0:T(8,128)(2,1)S(1)}, u32[]{:S(2)}, u32[]{:S(2)}) %all-to-all-start) | async-done | bytes 2097184 | tf_op jit(solution)/shard_map/all_to_all | solution.py:306
  75.7 6.5 %all-to-all-start.1 = ((bf16[32,16,2048]{2,1,0:T(8,128)(2,1)}), bf16[32,16,2048]{2,1,0:T(8,128)(2,1)}, u32[]{:S(2)}, u32[]{:S(2)}) async-start(bf16[32,16,2048]{2,1,0:T(8,128)(2,1)} %bitcast.37), calls=%async_computation.1 | async-start | bytes 4194304 | tf_op jit(solution)/shard_map/all_to_all | solution.py:309
  82.3 0.8 convolution_convert_fusion
  83.2 6.9 %fusion = f32[512,2048]{1,0:T(8,128)S(1)} fusion(bf16[512,2048]{1,0:T(8,128)(2,1)S(1)} %bitcast.35, bf16[1,2048,2048]{2,1,0:T(8,128)(2,1)} %all-gather.7.cloned.1.call-done), kind=kOutput, calls=%fused_computation | convolution fusion | flops 4294967296 | bytes 14680064 | tf_op jit(solution)/shard_map/dot_general | solution.py:318
  90.6 3.2 %multiply_convert_fusion = (bf16[512,1024]{1,0:T(8,128)(2,1)S(1)}, f32[512,1024]{1,0:T(8,128)}, f32[512,1024]{1,0:T(8,128)}) fusion(f32[512,1024]{1,0:T(8,128)S(1)} %slice_add_fusion, bf16[1,128,1024]{2,1,0:T(8,128)(2,1)S(1)} %copy-done.7, bf16[512,128]{0,1:T(8,128)(2,1)S(1)} %convolution_convert_fusion, f32[512,2048]{1,0:T(8,128)S(1)} %fusion), kind=kOutput, calls=%fused_computation.4 | convolution fusion | flops 73924608 | bytes 9633792 | tf_op jit(solution)/shard_map/dot_general | solution.py:321
  93.8 1.1 fusion.3.hlow_t_ref
  94.9 1.0 copy-done.3
  95.9 22.8 %all-gather.5.cloned.1.call-done = bf16[1,2048,1024]{2,1,0:T(8,128)(2,1)} async-done(((bf16[1,128,1024]{2,1,0:T(8,128)(2,1)}), bf16[1,2048,1024]{2,1,0:T(8,128)(2,1)}) %all-gather.5.cloned.1.call-update) | async-done | bytes 4194320 | tf_op jit(solution)/shard_map/all_gather | solution.py:303
  118.7 13.0 %all-to-all-done.1 = bf16[32,16,2048]{2,1,0:T(8,128)(2,1)} async-done(((bf16[32,16,2048]{2,1,0:T(8,128)(2,1)}), bf16[32,16,2048]{2,1,0:T(8,128)(2,1)}, u32[]{:S(2)}, u32[]{:S(2)}) %all-to-all-start.1) | async-done | bytes 2097184 | tf_op jit(solution)/shard_map/all_to_all | solution.py:309
  131.7 1.2 copy-done.4
  132.9 1.6 copy-done.5
  134.5 1.6 copy-done.6
  136.1 0.8 copy-done.11
  136.9 10.0 %gradients.1 = (bf16[8,288,128]{2,1,0:T(8,128)(2,1)S(1)}, bf16[8,288,128]{2,1,0:T(8,128)(2,1)S(1)}) custom-call(s32[1]{0:T(128)} %bitcast.core_ref, bf16[512,2048]{1,0:T(8,128)(2,1)} %bitcast.5.y_ref, bf16[2048,1024]{1,0:T(8,128)(2,1)} %bitcast.46, bf16[64,2048]{1,0:T(8,128)(2,1)S(1)} %bitcast.42, bf16[1024,64]{1,0:T(8,128)(2,1)S(1)} %bitcast.39, ...), custom_call_target="tpu_custom_call" | custom-call | flops 2684354560 | bytes 13631488 | tf_op jit(solution)/shard_map/gradients/pallas_call | solution.py:208
  146.9 1.9 %collective-permute-start = (bf16[8,288,128]{2,1,0:T(8,128)(2,1)S(1)}, bf16[8,288,128]{2,1,0:T(8,128)(2,1)S(1)}, u32[]{:S(2)}, u32[]{:S(2)}) collective-permute-start(bf16[8,288,128]{2,1,0:T(8,128)(2,1)S(1)} %get-tuple-element.11), channel_id=1, source_target_pairs={{0,32},{32,0},{64,96},{96,64},{128,160},{160,128},{192,224},{224,1... | collective-permute-start | bytes 1769480 | tf_op jit(solution)/shard_map/ppermute | solution.py:334
  148.9 2.0 %collective-permute-done = bf16[8,288,128]{2,1,0:T(8,128)(2,1)S(1)} collective-permute-done((bf16[8,288,128]{2,1,0:T(8,128)(2,1)S(1)}, bf16[8,288,128]{2,1,0:T(8,128)(2,1)S(1)}, u32[]{:S(2)}, u32[]{:S(2)}) %collective-permute-start) | collective-permute-done | bytes 589856 | tf_op jit(solution)/shard_map/ppermute | solution.py:334
  151.0 26.2 %all_to_all.15.parts_ref = bf16[8,288,128]{2,1,0:T(8,128)(2,1)} all-to-all(bf16[8,288,128]{2,1,0:T(8,128)(2,1)S(1)} %add_convert_fusion), channel_id=1, replica_groups={{0,64,128,192,256,320,384,448},{32,96,160,224,288,352,416,480},{1,65,12..., dimensions={0} | all-to-all | bytes 1179648 | tf_op jit(solution)/shard_map/all_to_all | solution.py:337
  177.2 1.8 sum_parts.1
  (34 shorter events, 3.0 us)
Async XLA Ops:
  7.2 75.2 %copy-start = (bf16[1,2048,128]{2,1,0:T(8,128)(2,1)S(1)}, bf16[1,2048,128]{2,1,0:T(8,128)(2,1)}, u32[]{:S(2)}) copy-start(bf16[1,2048,128]{2,1,0:T(8,128)(2,1)} %param.16) | copy-start | bytes 1572868
  7.2 76.0 %all-gather.7.cloned.1.call-start = ((), (), s32[]{:S(2)}) async-start(), calls=%async_computation.4 | async-start | bytes 8912896 | tf_op jit(solution)/shard_map/all_gather | solution.py:302
  7.9 1.0 copy-start.8
  9.0 0.7 copy-start.12
  11.0 1.3 copy-start.2
  12.3 14.3 %copy-start.9 = (bf16[128,2048]{1,0:T(8,128)(2,1)S(1)}, bf16[128,2048]{1,0:T(8,128)(2,1)}, u32[]{:S(2)}) copy-start(bf16[128,2048]{1,0:T(8,128)(2,1)} %tok_ref.2) | copy-start | bytes 1572868
  12.3 14.3 %copy-start.13 = (s32[128,8]{0,1:T(8,128)S(1)}, s32[128,8]{0,1:T(8,128)}, u32[]{:S(2)}) copy-start(s32[128,8]{0,1:T(8,128)} %param.12) | copy-start | bytes 12292
  12.3 14.3 %copy-start.14 = (f32[128,8]{0,1:T(8,128)S(1)}, f32[128,8]{0,1:T(8,128)}, u32[]{:S(2)}) copy-start(f32[128,8]{0,1:T(8,128)} %param.13) | copy-start | bytes 12292
  12.3 63.4 %all-to-all-start = ((bf16[32,16,2048]{2,1,0:T(8,128)(2,1)}), bf16[32,16,2048]{2,1,0:T(8,128)(2,1)S(1)}, u32[]{:S(2)}, u32[]{:S(2)}) async-start(bf16[32,16,2048]{2,1,0:T(8,128)(2,1)} %bitcast.38), calls=%async_computation | async-start | bytes 4194304 | tf_op jit(solution)/shard_map/all_to_all | solution.py:306
  25.8 92.8 %all-gather.5.cloned.1.call-start = ((), (), s32[]{:S(2)}) async-start(), calls=%async_computation.3 | async-start | bytes 4456448 | tf_op jit(solution)/shard_map/all_gather | solution.py:303
  28.1 1.3 copy-start.1
  75.7 6.5 %copy-start.15 = (bf16[1,1024,64]{1,2,0:T(8,128)(2,1)S(1)}, bf16[1,1024,64]{1,2,0:T(8,128)(2,1)}, u32[]{:S(2)}) copy-start(bf16[1,1024,64]{1,2,0:T(8,128)(2,1)} %param.18) | copy-start | bytes 393220
  75.7 56.0 %all-to-all-start.1 = ((bf16[32,16,2048]{2,1,0:T(8,128)(2,1)}), bf16[32,16,2048]{2,1,0:T(8,128)(2,1)}, u32[]{:S(2)}, u32[]{:S(2)}) async-start(bf16[32,16,2048]{2,1,0:T(8,128)(2,1)} %bitcast.37), calls=%async_computation.1 | async-start | bytes 4194304 | tf_op jit(solution)/shard_map/all_to_all | solution.py:309
  83.2 7.0 %copy-start.7 = (bf16[1,128,1024]{2,1,0:T(8,128)(2,1)S(1)}, bf16[1,128,1024]{2,1,0:T(8,128)(2,1)}, u32[]{:S(2)}) copy-start(bf16[1,128,1024]{2,1,0:T(8,128)(2,1)} %param.17) | copy-start | bytes 786436
  90.6 3.2 %copy-start.16 = (bf16[1,1024,64]{1,2,0:T(8,128)(2,1)S(1)}, bf16[1,1024,64]{1,2,0:T(8,128)(2,1)}, u32[]{:S(2)}) copy-start(bf16[1,1024,64]{1,2,0:T(8,128)(2,1)} %param.18) | copy-start | bytes 393220
  90.6 41.1 %copy-start.10 = (bf16[1,64,2048]{2,1,0:T(8,128)(2,1)S(1)}, bf16[1,64,2048]{2,1,0:T(8,128)(2,1)}, u32[]{:S(2)}) copy-start(bf16[1,64,2048]{2,1,0:T(8,128)(2,1)} %param.19) | copy-start | bytes 786436
  94.9 1.0 copy-start.3
  131.7 1.2 copy-start.4
  132.9 1.6 copy-start.5
  134.5 1.6 copy-start.6
  136.1 0.8 copy-start.11
  146.9 3.9 %collective-permute-start = (bf16[8,288,128]{2,1,0:T(8,128)(2,1)S(1)}, bf16[8,288,128]{2,1,0:T(8,128)(2,1)S(1)}, u32[]{:S(2)}, u32[]{:S(2)}) collective-permute-start(bf16[8,288,128]{2,1,0:T(8,128)(2,1)S(1)} %get-tuple-element.11), channel_id=1, source_target_pairs={{0,32},{32,0},{64,96},{96,64},{128,160},{160,128},{192,224},{224,1... | collective-permute-start | bytes 1769480 | tf_op jit(solution)/shard_map/ppermute | solution.py:334
Sparse Core Ops, SparseCore 0:
  10.1 62.8 all-gather.6
  75.1 43.5 all-gather.4

commit v2 on v1

v2 whole, which is shorter than its diff:
```python
import functools
import math

import jax
import jax.numpy as jnp
from jax import lax
from jax.experimental import pallas as pl
from jax.experimental.pallas import tpu as pltpu
from jax.sharding import PartitionSpec as P

F32 = jnp.float32
BF16 = jnp.bfloat16
LANES = 128
VMEM = 58 * 2**20


def dot_nt(a, b):
    return lax.dot_general(a, b, (((1,), (1,)), ((), ())), preferred_element_type=F32)


def dot_nn(a, b):
    return lax.dot_general(a, b, (((1,), (0,)), ((), ())), preferred_element_type=F32)


def slot_ranks(sel, experts):
    topk, toks = sel.shape
    ids = lax.broadcasted_iota(jnp.int32, (experts, toks), 0)
    chosen = jnp.zeros((experts, toks), F32)
    for k in range(topk):
        chosen += jnp.where(sel[k : k + 1, :] == ids, 1.0, 0.0)
    earlier = lax.broadcasted_iota(jnp.int32, (toks, toks), 0) < lax.broadcasted_iota(
        jnp.int32, (toks, toks), 1
    )
    before = dot_nn(chosen.astype(BF16), jnp.where(earlier, 1.0, 0.0).astype(BF16))
    return jnp.where(chosen > 0.0, before, -1.0)


def pack_kernel(cap, sel_ref, wgt_ref, tok_ref, cot_ref, out_ref, rank_s, wgt_s):
    step = pl.program_id(0)
    group = out_ref.shape[0]
    width = out_ref.shape[2]

    @pl.when(step == 0)
    def _():
        sel = sel_ref[...]
        rank_s[...] = slot_ranks(sel, rank_s.shape[0])
        ids = lax.broadcasted_iota(jnp.int32, rank_s.shape, 0)
        total = jnp.zeros(rank_s.shape, F32)
        for k in range(sel.shape[0]):
            total += jnp.where(sel[k : k + 1, :] == ids, wgt_ref[k : k + 1, :], 0.0)
        wgt_s[...] = total

    rows = pl.ds(pl.multiple_of(step * group, group), group)
    rank = rank_s[rows, :]
    wgt = wgt_s[rows, :]
    slot = lax.broadcasted_iota(jnp.int32, (cap, rank.shape[1]), 0).astype(F32)
    taken = [rank[e : e + 1, :] == slot for e in range(group)]
    onehot = jnp.concatenate([jnp.where(m, 1.0, 0.0) for m in taken], axis=0).astype(BF16)
    weight = jnp.concatenate(
        [
            jnp.sum(jnp.where(taken[e], wgt[e : e + 1, :], 0.0), axis=1, keepdims=True)
            for e in range(group)
        ],
        axis=0,
    )
    x = dot_nn(onehot, tok_ref[...]).astype(BF16)
    y = (weight * dot_nn(onehot, cot_ref[...])).astype(BF16)
    out_ref[:, :cap, :] = x.reshape(group, cap, width)
    out_ref[:, cap:, :] = y.reshape(group, cap, width)


def pack_rows(sel_t, wgt_t, tok, cot, experts, cap):
    toks, width = tok.shape
    group = 8
    whole = lambda a: pl.BlockSpec(a.shape, lambda i: (0, 0))
    ranks = pltpu.VMEM((experts, toks), F32)
    return pl.pallas_call(
        functools.partial(pack_kernel, cap),
        grid=(experts // group,),
        in_specs=[whole(sel_t), whole(wgt_t), whole(tok), whole(cot)],
        out_shape=jax.ShapeDtypeStruct((experts, 2 * cap, width), BF16),
        out_specs=pl.BlockSpec((group, 2 * cap, width), lambda i: (i, 0, 0)),
        scratch_shapes=[ranks, ranks],
        cost_estimate=pl.CostEstimate(
            flops=4 * experts * cap * toks * width,
            bytes_accessed=4 * width * (toks + experts * cap),
            transcendentals=0,
        ),
        compiler_params=pltpu.CompilerParams(vmem_limit_bytes=VMEM),
        name="pack_rows",
    )(sel_t, wgt_t, tok, cot)


def gradients_kernel(
    core_ref,
    x_ref,
    wg_ref,
    wu_ref,
    wd_ref,
    narrow_ref,
    dw_ref,
    dnt_ref,
    win_ref,
    rows_hbm,
    keep_ref,
    send_ref,
    y_s,
    low_s,
    lowt_s,
    z_s,
    zt_s,
    vt_s,
    hlt_s,
    inb_s,
    dna_s,
    y_sem,
):
    step = pl.program_id(0)
    steps = pl.num_programs(0)
    rank = zt_s.shape[0]
    slots = low_s.shape[0]
    cap, width = x_ref.shape[1:]
    fetch_y = pltpu.make_async_copy(rows_hbm.at[:, pl.ds(cap, cap), :], y_s, y_sem)
    x = x_ref[...].reshape(slots, width)

    @pl.when(step == 0)
    def _():
        fetch_y.start()
        low = dot_nn(x, narrow_ref[...])
        low_s[...] = low.astype(BF16)
        lowt_s[...] = low.T.astype(BF16)
        vt_s[...] = jnp.zeros_like(vt_s)
        hlt_s[...] = jnp.zeros_like(hlt_s)

    win = win_ref[...]
    first = lax.broadcasted_iota(jnp.int32, win.shape, 0) < rank
    zero = jnp.zeros_like(win)
    low = low_s[...]
    gate = dot_nn(x, wg_ref[...]) + 0.5 * dot_nn(low, jnp.where(first, win, zero))
    up = dot_nn(x, wu_ref[...]) + 0.5 * dot_nn(low, jnp.where(first, zero, win))

    @pl.when(step == 0)
    def _():
        fetch_y.wait()
        z = dot_nt(y_s[...].reshape(slots, width), dw_ref[...])
        z_s[...] = z.astype(BF16)
        zt_s[...] = z.T.astype(BF16)

    dhid = dot_nn(y_s[...].reshape(slots, width), wd_ref[...])
    dhid += 0.5 * dot_nn(z_s[...], dnt_ref[...])
    sig = jax.nn.sigmoid(gate)
    silu = gate * sig
    hidden = (silu * up).astype(BF16)
    dgate = (dhid * up * sig * (1.0 + gate * (1.0 - sig))).astype(BF16)
    dup = (dhid * silu).astype(BF16)
    hlt_s[...] += dot_nt(dnt_ref[...], hidden)
    dna_s[step] = dot_nn(zt_s[...], hidden)
    vt_s[:rank, :] += dot_nt(win[:rank, :], dgate)
    vt_s[rank:, :] += dot_nt(win[rank:, :], dup)
    inb_s[step, :rank, :] = dot_nn(lowt_s[:rank, :], dgate)
    inb_s[step, rank:, :] = dot_nn(lowt_s[rank:, :], dup)

    @pl.when(step == steps - 1)
    def _():
        even = core_ref[0] == 0
        ina = dot_nn(vt_s[...].astype(BF16), x)
        dnb = dot_nn(hlt_s[...].astype(BF16), y_s[...].reshape(slots, width))
        cols = inb_s.shape[2] // LANES
        reach = width // 2
        half = rank // 2
        left = lax.broadcasted_iota(jnp.int32, (half, LANES), 1) < LANES // 2
        upper = lax.broadcasted_iota(jnp.int32, (8, LANES), 0) < 4
        for t in range(keep_ref.shape[0]):
            d = dna_s[t // cols][:, (t % cols) * LANES : (t % cols + 1) * LANES]
            top, low = d[:half], d[half:]
            middle = (
                jnp.where(left, top, pltpu.roll(low, LANES // 2, 1)),
                jnp.where(left, pltpu.roll(top, LANES // 2, 1), low),
            )
            last = ([], [])
            for b in range(reach // LANES):
                p = dnb[8 * t : 8 * t + 8, b * LANES : (b + 1) * LANES]
                q = dnb[8 * t : 8 * t + 8, reach + b * LANES : reach + (b + 1) * LANES]
                last[0].append(jnp.where(upper, p, pltpu.roll(q, 4, 0)))
                last[1].append(jnp.where(upper, pltpu.roll(p, 4, 0), q))
            both = []
            for c in range(2):
                j = 2 * t + c
                rows = [ina[:, j * LANES : (j + 1) * LANES]]
                for s in range(inb_s.shape[0]):
                    for b in range(cols):
                        rows.append(inb_s[s, 8 * j : 8 * j + 8, b * LANES : (b + 1) * LANES])
                both.append(jnp.concatenate(rows + [middle[c]] + last[c], axis=0))
            keep_ref[t] = jnp.where(even, both[0], both[1]).astype(BF16)
            send_ref[t] = jnp.where(even, both[1], both[0]).astype(BF16)


def gradients(core, rows, weights, narrow, win, dnt, dw, parts):
    sources, pair, width = rows.shape
    cap = pair // 2
    slots = sources * cap
    rank, units = dnt.shape
    block = 256
    steps = units // block
    lines = (2 * rank * units + units * rank + rank * width) // (parts * LANES) + width // parts
    whole = lambda a: pl.BlockSpec(a.shape, lambda i: (0, 0))
    cols = lambda a, at: pl.BlockSpec((a.shape[0], block), lambda i: (0, at * steps + i))
    out = jax.ShapeDtypeStruct((parts // 2, lines, LANES), BF16)
    out_spec = pl.BlockSpec(out.shape, lambda i: (0, 0, 0))
    return pl.pallas_call(
        gradients_kernel,
        grid=(steps,),
        in_specs=[
            pl.BlockSpec(memory_space=pltpu.SMEM),
            pl.BlockSpec((sources, cap, width), lambda i: (0, 0, 0)),
            cols(weights, 0),
            cols(weights, 1),
            cols(weights, 2),
            whole(narrow),
            whole(dw),
            cols(dnt, 0),
            cols(win, 0),
            pl.BlockSpec(memory_space=pl.ANY),
        ],
        out_shape=(out, out),
        out_specs=(out_spec, out_spec),
        scratch_shapes=[
            pltpu.VMEM((sources, cap, width), BF16),
            pltpu.VMEM((slots, 2 * rank), BF16),
            pltpu.VMEM((2 * rank, slots), BF16),
            pltpu.VMEM((slots, rank), BF16),
            pltpu.VMEM((rank, slots), BF16),
            pltpu.VMEM((2 * rank, slots), F32),
            pltpu.VMEM((rank, slots), F32),
            pltpu.VMEM((steps, 2 * rank, block), F32),
            pltpu.VMEM((steps, rank, block), F32),
            pltpu.SemaphoreType.DMA,
        ],
        cost_estimate=pl.CostEstimate(
            flops=2 * slots * width * (3 * units + 6 * rank),
            bytes_accessed=2 * width * (2 * slots + 3 * units),
            transcendentals=slots * units,
        ),
        compiler_params=pltpu.CompilerParams(vmem_limit_bytes=VMEM),
        name="gradients",
    )(core, rows, weights, weights, weights, narrow, dw, dnt, win, rows)


def finish_kernel(factor, parts_ref, ina_ref, inb_ref, dna_ref, dnb_ref):
    total = parts_ref[0].astype(F32)
    for i in range(1, parts_ref.shape[0]):
        total += parts_ref[i].astype(F32)
    total *= factor
    width = ina_ref.shape[1]
    ina_ref[0] = total[:width].T
    at = width
    for b in range(inb_ref.shape[2] // LANES):
        inb_ref[0, :, b * LANES : (b + 1) * LANES] = total[at : at + 8]
        at += 8
    half = dna_ref.shape[2] // 2
    d = total[at : at + half]
    at += half
    both = jnp.concatenate([d, pltpu.roll(d, LANES // 2, 1)], axis=0)
    dna_ref[0] = both.T[: dna_ref.shape[1]]
    reach = dnb_ref.shape[2] // 2
    for b in range(reach // LANES):
        e = total[at : at + 8]
        at += 8
        dnb_ref[0, :, b * LANES : (b + 1) * LANES] = e[:4]
        dnb_ref[0, :, reach + b * LANES : reach + (b + 1) * LANES] = e[4:]


def finish(parts, factor, shapes):
    return pl.pallas_call(
        functools.partial(finish_kernel, factor),
        out_shape=tuple(jax.ShapeDtypeStruct(s, F32) for s in shapes),
        name="sum_parts",
    )(parts)


def body(
    tokens,
    output_gradient,
    selected_expert_index,
    routing_weight_rows,
    fixed_gate_up_weight,
    fixed_down_weight_flipped,
    gate_up_adapter_narrow,
    gate_up_adapter_widen,
    down_adapter_narrow,
    down_adapter_widen,
):
    experts = lax.axis_size("expert")
    groups = lax.axis_size("dp")
    tok_rows, model_width = tokens.shape
    cap = tok_rows // 8
    width = fixed_down_weight_flipped.shape[2]
    rank = down_adapter_narrow.shape[2]
    factor = 0.5 / math.sqrt(tok_rows * groups * experts)
    weights = jnp.concatenate([fixed_gate_up_weight[0], fixed_down_weight_flipped[0]], axis=1)
    weights = lax.all_gather(weights, "dp", axis=0, tiled=True)
    rows = pack_rows(
        selected_expert_index.T, routing_weight_rows.T, tokens, output_gradient, experts, cap
    )
    rows = lax.all_to_all(rows, "expert", 0, 0, tiled=True)
    core = (lax.axis_index("dp") % 2).astype(jnp.int32).reshape(1)
    keep, send = gradients(
        core,
        rows,
        weights,
        gate_up_adapter_narrow[0],
        gate_up_adapter_widen[0],
        down_adapter_narrow[0].T,
        down_adapter_widen[0],
        groups,
    )
    other = lax.ppermute(send, "dp", [(i, i ^ 1) for i in range(groups)])
    pair = (keep.astype(F32) + other.astype(F32)).astype(BF16)
    lines = [[2 * i + c for i in range(groups // 2)] for c in range(2)]
    parts = lax.all_to_all(pair, "dp", 0, 0, tiled=True, axis_index_groups=lines)
    shapes = (
        (1, model_width // groups, 2 * rank),
        (1, 2 * rank // groups, width),
        (1, width // groups, rank),
        (1, rank // groups, model_width),
    )
    return finish(parts, factor, shapes)


def solution(mesh):
    in_specs = (
        P(("dp", "expert"), None),
        P(("dp", "expert"), None),
        P(("dp", "expert"), None),
        P(("dp", "expert"), None),
        P("expert", "dp", None),
        P("expert", "dp", None),
        P("expert", None, None),
        P("expert", None, None),
        P("expert", None, None),
        P("expert", None, None),
    )
    out_specs = (
        P("expert", "dp", None),
        P("expert", "dp", None),
        P("expert", "dp", None),
        P("expert", "dp", None),
    )
    return jax.shard_map(body, mesh=mesh, in_specs=in_specs, out_specs=out_specs, check_vma=False)
```

time: 187 us -> 182 us (0.973)
  waiting for transfers between devices: 85.4 us -> 97.9 us
  matrix products: 12.4 us -> 0 us
  local copies, waits for them, and re-layouts: 10.8 us -> 0 us
  Pallas kernels: 14.6 us -> 24.9 us
  starting transfers between devices: 22 us -> 15.4 us
  other arithmetic: 0.16 us -> 3.29 us
    all_to_all x2 -> x1, waiting for transfers between devices: 59.3 us -> 95.7 us  [body(): rows = lax.all_to_all(rows, 'expert', 0, 0, tiled=True)]
    all_gather x2 -> x1, waiting for transfers between devices: 22.8 us -> 0.01 us  [body(): weights = lax.all_gather(weights, 'dp', axis=0, tiled=True)]
    dot_general x5 -> x0, matrix products: 12.4 us -> none  [the longest x1 6.92 us: body(): base = jnp.dot(x, w_gate_up, preferred_element_type=F32)]
    unnamed x35 -> x0, local copies, waits for them, and re-layouts: 10.8 us -> none
    pallas_call x3 -> x2, Pallas kernels: 12.7 us -> 23.1 us  [the longest x1 18.4 us: gradients(): pl.pallas_call(gradients_kernel, grid=(steps,), in_specs=[pl.BlockSpec(me...]
    all_to_all x2 -> x1, starting transfers between devices: 20 us -> 13.5 us  [body(): rows = lax.all_to_all(rows, 'expert', 0, 0, tiled=True)]
    concatenate x0 -> x1, other arithmetic: none -> 2.07 us  [body(): jnp.concatenate([fixed_gate_up_weight[0], fixed_down_weight_flipped[0]],...]
  transfers between devices with their start and end apart: 5 -> 3, of which waited for: 4 -> 2; matrix products, arithmetic and copies ran while one was open for 7% -> 0% of each run, Pallas kernels for 1% -> 3%
where the time goes in v2:
time: 182 us
  waiting for transfers between devices  97.9 us (54%)
  blocking collectives  26.2 us (14%)
  Pallas kernels  24.9 us (14%)
  starting transfers between devices  15.4 us (8%)
  between operations  14.1 us (8%)
  other arithmetic  3.29 us (2%)
    all_to_all x1, waiting for transfers between devices, body(): rows = lax.all_to_all(rows, 'expert', 0, 0, tiled=True)  95.7 us
    all_to_all x1, blocking collectives, body(): lax.all_to_all(pair, 'dp', 0, 0, tiled=True, axis_index_groups=lines)  26.2 us
    pallas_call x1, Pallas kernels, gradients(): pl.pallas_call(gradients_kernel, grid=(steps,), in_specs=[pl.BlockSpec(me...  18.4 us
    all_to_all x1, starting transfers between devices, body(): rows = lax.all_to_all(rows, 'expert', 0, 0, tiled=True)  13.5 us
    pallas_call x1, Pallas kernels, pack_rows(): pl.pallas_call(functools.partial(pack_kernel, cap), grid=(experts // grou...  4.73 us
  transfers between devices with their start and end apart: 3, of which 2 were waited for; matrix products, arithmetic and copies ran while one was open for 0% of the time, Pallas kernels for 3%

profile of v2, /device:TPU:6, one launch (start us, length us, event | category | flops | bytes accessed | tf_op | source)
XLA Modules:
  0.0 181.8 jit_solution(11088221307324902919)
XLA Ops:
  7.2 0.0 all-gather.2.cloned.1.call-start
  7.2 2.1 %pad_maximum_fusion = bf16[128,3072]{1,0:T(8,128)(2,1)} fusion(bf16[128,1024]{1,0:T(8,128)(2,1)} %bitcast.15, bf16[128,2048]{1,0:T(8,128)(2,1)} %bitcast.12), kind=kLoop, calls=%fused_computation.1 | loop fusion | flops 1572864 | bytes 1572864 | tf_op jit(solution)/shard_map/concatenate | solution.py:300
  9.3 0.0 all-gather.2.cloned.1.call-update
  9.3 4.7 %pack_rows.1 = bf16[32,32,2048]{2,1,0:T(8,128)(2,1)} custom-call(s32[8,128]{1,0:T(8,128)} %bitcast.17, f32[8,128]{1,0:T(8,128)} %bitcast.18, bf16[128,2048]{1,0:T(8,128)(2,1)} %tok_ref.1, bf16[128,2048]{1,0:T(8,128)(2,1)} %cot_ref.1), custom_call_target="tpu_custom_call" | custom-call | flops 536870912 | bytes 5242880 | tf_op jit(solution)/shard_map/pack_rows/pallas_call | solution.py:77
  14.0 13.5 %all-to-all-start = ((bf16[32,32,2048]{2,1,0:T(8,128)(2,1)}), bf16[32,32,2048]{2,1,0:T(8,128)(2,1)}, u32[]{:S(2)}, u32[]{:S(2)}) async-start(bf16[32,32,2048]{2,1,0:T(8,128)(2,1)} %pack_rows.1), calls=%async_computation | async-start | bytes 8388608 | tf_op jit(solution)/shard_map/all_to_all | solution.py:305
  27.5 95.7 %all-to-all-done.x_ref.rows_hbm = bf16[32,32,2048]{2,1,0:T(8,128)(2,1)} async-done(((bf16[32,32,2048]{2,1,0:T(8,128)(2,1)}), bf16[32,32,2048]{2,1,0:T(8,128)(2,1)}, u32[]{:S(2)}, u32[]{:S(2)}) %all-to-all-start) | async-done | bytes 4194336 | tf_op jit(solution)/shard_map/all_to_all | solution.py:305
  123.2 0.0 all-gather.2.cloned.1.call-done.wg_ref.wu_ref.wd_ref
  123.3 18.4 %gradients.1 = (bf16[8,288,128]{2,1,0:T(8,128)(2,1)}, bf16[8,288,128]{2,1,0:T(8,128)(2,1)}) custom-call(s32[1]{0:T(128)} %bitcast.core_ref, bf16[32,32,2048]{2,1,0:T(8,128)(2,1)} %all-to-all-done.x_ref.rows_hbm, bf16[2048,3072]{1,0:T(8,128)(2,1)} %all-gather.2.cloned.1.call-done.wg_ref.wu_ref.wd_ref, ...), custom_call_target="tpu_custom_call" | custom-call | flops 7247757312 | bytes 16777216 | tf_op jit(solution)/shard_map/gradients/pallas_call | solution.py:210
  141.6 1.9 %collective-permute-start = (bf16[8,288,128]{2,1,0:T(8,128)(2,1)}, bf16[8,288,128]{2,1,0:T(8,128)(2,1)S(1)}, u32[]{:S(2)}, u32[]{:S(2)}) collective-permute-start(bf16[8,288,128]{2,1,0:T(8,128)(2,1)} %get-tuple-element.7), channel_id=1, source_target_pairs={{0,32},{32,0},{64,96},{96,64},{128,160},{160,128},{192,224},{224,1... | collective-permute-start | bytes 1769480 | tf_op jit(solution)/shard_map/ppermute | solution.py:317
  143.6 2.2 %collective-permute-done = bf16[8,288,128]{2,1,0:T(8,128)(2,1)S(1)} collective-permute-done((bf16[8,288,128]{2,1,0:T(8,128)(2,1)}, bf16[8,288,128]{2,1,0:T(8,128)(2,1)S(1)}, u32[]{:S(2)}, u32[]{:S(2)}) %collective-permute-start) | collective-permute-done | bytes 589856 | tf_op jit(solution)/shard_map/ppermute | solution.py:317
  145.7 1.2 add_convert_fusion
  147.0 26.2 %all_to_all.10.parts_ref = bf16[8,288,128]{2,1,0:T(8,128)(2,1)} all-to-all(bf16[8,288,128]{2,1,0:T(8,128)(2,1)S(1)} %add_convert_fusion), channel_id=1, replica_groups={{0,64,128,192,256,320,384,448},{32,96,160,224,288,352,416,480},{1,65,12..., dimensions={0} | all-to-all | bytes 1179648 | tf_op jit(solution)/shard_map/all_to_all | solution.py:320
  173.2 1.8 %sum_parts.1 = (f32[1,128,128]{2,1,0:T(8,128)}, f32[1,8,1024]{2,1,0:T(8,128)}, f32[1,64,64]{2,1,0:T(8,128)}, f32[1,4,2048]{2,1,0:T(4,128)}) custom-call(bf16[8,288,128]{2,1,0:T(8,128)(2,1)} %all_to_all.10.parts_ref), custom_call_target="tpu_custom_call" | custom-call | tf_op jit(solution)/shard_map/sum_parts/pallas_call | solution.py:274
Async XLA Ops:
  7.2 116.1 %all-gather.2.cloned.1.call-start = ((), (), s32[]{:S(2)}) async-start(), calls=%async_computation.2 | async-start | bytes 13369344 | tf_op jit(solution)/shard_map/all_gather | solution.py:301
  14.0 109.2 %all-to-all-start = ((bf16[32,32,2048]{2,1,0:T(8,128)(2,1)}), bf16[32,32,2048]{2,1,0:T(8,128)(2,1)}, u32[]{:S(2)}, u32[]{:S(2)}) async-start(bf16[32,32,2048]{2,1,0:T(8,128)(2,1)} %pack_rows.1), calls=%async_computation | async-start | bytes 8388608 | tf_op jit(solution)/shard_map/all_to_all | solution.py:305
  141.6 4.1 %collective-permute-start = (bf16[8,288,128]{2,1,0:T(8,128)(2,1)}, bf16[8,288,128]{2,1,0:T(8,128)(2,1)S(1)}, u32[]{:S(2)}, u32[]{:S(2)}) collective-permute-start(bf16[8,288,128]{2,1,0:T(8,128)(2,1)} %get-tuple-element.7), channel_id=1, source_target_pairs={{0,32},{32,0},{64,96},{96,64},{128,160},{160,128},{192,224},{224,1... | collective-permute-start | bytes 1769480 | tf_op jit(solution)/shard_map/ppermute | solution.py:317
Sparse Core Ops, SparseCore 0:
  10.1 82.5 all-gather.1

commit v3 on v2

v3 whole, which is shorter than its diff:
```python
import functools
import math

import jax
import jax.numpy as jnp
from jax import lax
from jax.experimental import pallas as pl
from jax.experimental.pallas import tpu as pltpu
from jax.sharding import PartitionSpec as P

F32 = jnp.float32
BF16 = jnp.bfloat16
LANES = 128
VMEM = 44 * 2**20


def in_hbm(*arrays):
    return [pltpu.with_memory_space_constraint(a, pltpu.HBM) for a in arrays]


def dot_nt(a, b):
    return lax.dot_general(a, b, (((1,), (1,)), ((), ())), preferred_element_type=F32)


def dot_nn(a, b):
    return lax.dot_general(a, b, (((1,), (0,)), ((), ())), preferred_element_type=F32)


def slot_ranks(sel, experts):
    topk, toks = sel.shape
    ids = lax.broadcasted_iota(jnp.int32, (experts, toks), 0)
    chosen = jnp.zeros((experts, toks), F32)
    for k in range(topk):
        chosen += jnp.where(sel[k : k + 1, :] == ids, 1.0, 0.0)
    earlier = lax.broadcasted_iota(jnp.int32, (toks, toks), 0) < lax.broadcasted_iota(
        jnp.int32, (toks, toks), 1
    )
    before = dot_nn(chosen.astype(BF16), jnp.where(earlier, 1.0, 0.0).astype(BF16))
    return jnp.where(chosen > 0.0, before, -1.0)


def pack_kernel(
    cap, sel_hbm, wgt_hbm, tok_hbm, cot_hbm, out_hbm, sel_s, wgt_s, tok_s, cot_s, out_s, hot_s, row_s, sems
):
    experts, _, width = out_s.shape
    cols = width // 4

    def fetch(src, dst, i):
        copy = pltpu.make_async_copy(src, dst, sems.at[i])
        copy.start()
        return copy

    first = [fetch(sel_hbm, sel_s, 0), fetch(wgt_hbm, wgt_s, 1)]
    tok_in = fetch(tok_hbm, tok_s, 2)
    cot_in = fetch(cot_hbm, cot_s, 3)
    for copy in first:
        copy.wait()
    sel = sel_s[...]
    rank = slot_ranks(sel, experts)
    ids = lax.broadcasted_iota(jnp.int32, rank.shape, 0)
    wgt = jnp.zeros(rank.shape, F32)
    for k in range(sel.shape[0]):
        wgt += jnp.where(sel[k : k + 1, :] == ids, wgt_s[k : k + 1, :], 0.0)
    slot = lax.broadcasted_iota(jnp.int32, (cap, rank.shape[1]), 0).astype(F32)
    for e in range(experts):
        taken = rank[e : e + 1, :] == slot
        rows = pl.ds(e * cap, cap)
        hot_s[rows, :] = jnp.where(taken, 1.0, 0.0).astype(BF16)
        weight = jnp.sum(jnp.where(taken, wgt[e : e + 1, :], 0.0), axis=1, keepdims=True)
        row_s[rows, :] = jnp.broadcast_to(weight, (cap, LANES))
    tok_in.wait()
    cot_in.wait()
    copies = []
    for i in range(width // cols):
        at = pl.ds(i * cols, cols)
        x = dot_nn(hot_s[...], tok_s[:, at]).astype(BF16)
        out_s[:, :cap, at] = x.reshape(experts, cap, cols)
        y = dot_nn(hot_s[...], cot_s[:, at])
        y = (jnp.concatenate([row_s[...]] * (cols // LANES), axis=1) * y).astype(BF16)
        out_s[:, cap:, at] = y.reshape(experts, cap, cols)
        copies.append(fetch(out_s.at[:, :, at], out_hbm.at[:, :, at], 4 + i))
    for copy in copies:
        copy.wait()


def pack_rows(sel_t, wgt_t, tok, cot, experts, cap):
    toks, width = tok.shape
    like = lambda a: pltpu.VMEM(a.shape, a.dtype)
    out = pltpu.HBM((experts, 2 * cap, width), BF16)
    return pl.pallas_call(
        functools.partial(pack_kernel, cap),
        in_specs=[pl.BlockSpec(memory_space=pltpu.HBM)] * 4,
        out_shape=out,
        out_specs=pl.BlockSpec(memory_space=pltpu.HBM),
        scratch_shapes=[
            like(sel_t),
            like(wgt_t),
            like(tok),
            like(cot),
            pltpu.VMEM(out.shape, BF16),
            pltpu.VMEM((experts * cap, toks), BF16),
            pltpu.VMEM((experts * cap, LANES), F32),
            pltpu.SemaphoreType.DMA((8,)),
        ],
        cost_estimate=pl.CostEstimate(
            flops=4 * experts * cap * toks * width,
            bytes_accessed=4 * width * (toks + experts * cap),
            transcendentals=0,
        ),
        compiler_params=pltpu.CompilerParams(vmem_limit_bytes=VMEM),
        name="pack_rows",
    )(*in_hbm(sel_t, wgt_t, tok, cot))


def gather_weights(shards):
    groups = lax.axis_size("dp")
    chips = groups // 2
    core = lax.axis_index("dp") % 2
    swap = lambda a: lax.ppermute(a, "dp", [(i, i ^ 1) for i in range(groups)])
    ring = lambda a, way: lax.ppermute(a, "dp", [(i, (i + 2 * way(i)) % groups) for i in range(groups)])
    up = down = jnp.concatenate(shards, axis=1)
    held = [up]
    for _ in range(1, chips // 2):
        up = ring(up, lambda i: 1)
        down = ring(down, lambda i: -1)
        held += [up, down]
    held.append(ring(jnp.where(core == 0, up, down), lambda i: 1 if i % 2 == 0 else -1))
    return held + [swap(a) for a in held]


def piece_rows(chips, lines, chip, core):
    starts = [chip]
    for hop in range(1, chips // 2):
        starts += [chip - hop, chip + hop]
    starts.append(chip + chips // 2)
    return [
        pl.multiple_of((2 * lax.rem(at + chips, chips) + part) * lines, lines)
        for part in (core, 1 - core)
        for at in starts
    ]


def gradients_kernel(
    block,
    chips,
    place_ref,
    rows_hbm,
    narrow_hbm,
    dw_hbm,
    dnt_hbm,
    win_hbm,
    *refs,
):
    pieces, refs = refs[: 2 * chips], refs[2 * chips :]
    keep_ref, send_ref, x_s, y_s, w_s, narrow_s, dw_s, dnt_s, win_s = refs[:9]
    hid_s, dgate_s, dup_s, inb_s, dna_s, dnb_s, ina_s, sems = refs[9:]
    sources, pair, width = rows_hbm.shape
    cap = pair // 2
    slots = sources * cap
    rank, units = dnt_s.shape
    deeper = x_s.shape[2]
    steps = units // block
    used = iter(range(sems.shape[0]))

    def fetch(src, dst):
        copy = pltpu.make_async_copy(src, dst, sems.at[next(used)])
        copy.start()
        return copy

    def columns(part, step):
        return pl.ds(part * units + step * block, block)

    firsts = piece_rows(chips, pieces[0].shape[0], place_ref[0], place_ref[1])
    cols_in = {}

    def fetch_columns(part, step):
        at = columns(part, step)
        cols_in[part, step] = [
            fetch(piece.at[:, at], w_s.at[pl.ds(first, piece.shape[0]), at])
            for piece, first in zip(pieces, firsts)
        ]

    def wait_columns(part, step):
        for copy in cols_in[part, step]:
            copy.wait()

    x_in = fetch(rows_hbm.at[:, pl.ds(0, cap), :], x_s.at[:, :, pl.ds(0, width)])
    narrow_in = fetch(narrow_hbm, narrow_s)
    fetch_columns(0, 0)
    win_in = fetch(win_hbm, win_s)
    fetch_columns(1, 0)
    y_in = fetch(rows_hbm.at[:, pl.ds(cap, cap), :], y_s.at[:, :, pl.ds(0, width)])
    dw_in = fetch(dw_hbm, dw_s)
    dnt_in = fetch(dnt_hbm, dnt_s)

    def times(rows_ref, part, step):
        return dot_nn(rows_ref[...].reshape(slots, deeper), w_s[:, columns(part, step)])

    for step in range(steps):
        at = pl.ds(step * block, block)
        if step == 0:
            x_in.wait()
            narrow_in.wait()
            x = x_s[:, :, :width].reshape(slots, width)
            low_f = dot_nn(x, narrow_s[...])
            low = low_f.astype(BF16)
            low_t = low_f.T.astype(BF16)
            x_s[:, :, width:] = low.reshape(sources, cap, 2 * rank)
            win_in.wait()
            win = (0.5 * win_s[...].astype(F32)).astype(BF16)
            zero = jnp.zeros((rank, units), BF16)
            w_s[width:, :units] = jnp.concatenate([win[:rank], zero], axis=0)
            w_s[width:, units : 2 * units] = jnp.concatenate([zero, win[rank:]], axis=0)
        wait_columns(0, step)
        fetch_columns(2, step)
        gate = times(x_s, 0, step)
        wait_columns(1, step)
        if step + 1 < steps:
            fetch_columns(0, step + 1)
        up = times(x_s, 1, step)
        if step == 0:
            y_in.wait()
            dw_in.wait()
            dnt_in.wait()
            y = y_s[:, :, :width].reshape(slots, width)
            z_f = dot_nt(y, dw_s[...])
            z = z_f.astype(BF16)
            z_t = z_f.T.astype(BF16)
            z = jnp.concatenate([z, jnp.zeros_like(z)], axis=1)
            y_s[:, :, width:] = z.reshape(sources, cap, 2 * rank)
            dnt = (0.5 * dnt_s[...].astype(F32)).astype(BF16)
            w_s[width:, 2 * units :] = jnp.concatenate([dnt, zero], axis=0)
        wait_columns(2, step)
        if step + 1 < steps:
            fetch_columns(1, step + 1)
        dhid = times(y_s, 2, step)
        sig = jax.nn.sigmoid(gate)
        silu = gate * sig
        hid_s[:, at] = (silu * up).astype(BF16)
        dgate_s[:, at] = (dhid * up * sig * (1.0 + gate * (1.0 - sig))).astype(BF16)
        dup_s[:, at] = (dhid * silu).astype(BF16)

    hlow_t = dot_nt(dnt_s[...], hid_s[...]).astype(BF16)
    vlow_t = jnp.concatenate(
        [dot_nt(win_s[:rank, :], dgate_s[...]), dot_nt(win_s[rank:, :], dup_s[...])], axis=0
    ).astype(BF16)
    dna_s[...] = dot_nn(z_t, hid_s[...])
    inb_s[:rank, :] = dot_nn(low_t[:rank, :], dgate_s[...])
    inb_s[rank:, :] = dot_nn(low_t[rank:, :], dup_s[...])
    dnb_s[...] = dot_nn(hlow_t, y_s[:, :, :width].reshape(slots, width))
    ina_s[...] = dot_nn(vlow_t, x_s[:, :, :width].reshape(slots, width))

    even = place_ref[1] == 0
    reach = width // 2
    half = rank // 2
    left = lax.broadcasted_iota(jnp.int32, (half, LANES), 1) < LANES // 2
    upper = lax.broadcasted_iota(jnp.int32, (8, LANES), 0) < 4
    for t in range(keep_ref.shape[0]):
        d = dna_s[:, t * LANES : (t + 1) * LANES]
        top, bottom = d[:half], d[half:]
        middle = (
            jnp.where(left, top, pltpu.roll(bottom, LANES // 2, 1)),
            jnp.where(left, pltpu.roll(top, LANES // 2, 1), bottom),
        )
        last = ([], [])
        for b in range(reach // LANES):
            p = dnb_s[8 * t : 8 * t + 8, b * LANES : (b + 1) * LANES]
            q = dnb_s[8 * t : 8 * t + 8, reach + b * LANES : reach + (b + 1) * LANES]
            last[0].append(jnp.where(upper, p, pltpu.roll(q, 4, 0)))
            last[1].append(jnp.where(upper, pltpu.roll(p, 4, 0), q))
        both = []
        for c in range(2):
            j = 2 * t + c
            lines = [ina_s[:, j * LANES : (j + 1) * LANES]]
            for b in range(units // LANES):
                lines.append(inb_s[8 * j : 8 * j + 8, b * LANES : (b + 1) * LANES])
            both.append(jnp.concatenate(lines + [middle[c]] + last[c], axis=0))
        keep_ref[t] = jnp.where(even, both[0], both[1]).astype(BF16)
        send_ref[t] = jnp.where(even, both[1], both[0]).astype(BF16)


def gradients(place, rows, pieces, narrow, win, dnt, dw, parts):
    sources, pair, width = rows.shape
    cap = pair // 2
    slots = sources * cap
    rank, units = dnt.shape
    block = 512
    lines = (2 * rank * units + units * rank + rank * width) // (parts * LANES) + width // parts
    out = pltpu.VMEM((parts // 2, lines, LANES), BF16)
    out_spec = pl.BlockSpec(memory_space=pltpu.VMEM)
    acts = pltpu.VMEM((sources, cap, width + 2 * rank), BF16)
    hidden = pltpu.VMEM((slots, units), BF16)
    like = lambda a: pltpu.VMEM(a.shape, a.dtype)
    return pl.pallas_call(
        functools.partial(gradients_kernel, block, parts // 2),
        in_specs=[pl.BlockSpec(memory_space=pltpu.SMEM)]
        + [pl.BlockSpec(memory_space=pltpu.HBM)] * 5
        + [pl.BlockSpec(memory_space=pl.ANY)] * len(pieces),
        out_shape=(out, out),
        out_specs=(out_spec, out_spec),
        scratch_shapes=[
            acts,
            acts,
            pltpu.VMEM((width + 2 * rank, 3 * units), BF16),
            like(narrow),
            like(dw),
            like(dnt),
            like(win),
            hidden,
            hidden,
            hidden,
            pltpu.VMEM((2 * rank, units), F32),
            pltpu.VMEM((rank, units), F32),
            pltpu.VMEM((rank, width), F32),
            pltpu.VMEM((2 * rank, width), F32),
            pltpu.SemaphoreType.DMA((6 + 3 * len(pieces) * (units // block),)),
        ],
        cost_estimate=pl.CostEstimate(
            flops=2 * slots * width * (3 * units + 6 * rank),
            bytes_accessed=2 * width * (2 * slots + 3 * units),
            transcendentals=slots * units,
        ),
        compiler_params=pltpu.CompilerParams(vmem_limit_bytes=VMEM),
        name="gradients",
    )(place, *in_hbm(rows, narrow, dw, dnt, win, *pieces))


def finish_kernel(factor, parts_ref, ina_ref, inb_ref, dna_ref, dnb_ref):
    total = parts_ref[0].astype(F32)
    for i in range(1, parts_ref.shape[0]):
        total += parts_ref[i].astype(F32)
    total *= factor
    width = ina_ref.shape[1]
    ina_ref[0] = total[:width].T
    at = width
    for b in range(inb_ref.shape[2] // LANES):
        inb_ref[0, :, b * LANES : (b + 1) * LANES] = total[at : at + 8]
        at += 8
    half = dna_ref.shape[2] // 2
    d = total[at : at + half]
    at += half
    both = jnp.concatenate([d, pltpu.roll(d, LANES // 2, 1)], axis=0)
    dna_ref[0] = both.T[: dna_ref.shape[1]]
    reach = dnb_ref.shape[2] // 2
    for b in range(reach // LANES):
        e = total[at : at + 8]
        at += 8
        dnb_ref[0, :, b * LANES : (b + 1) * LANES] = e[:4]
        dnb_ref[0, :, reach + b * LANES : reach + (b + 1) * LANES] = e[4:]


def finish(parts, factor, shapes):
    return pl.pallas_call(
        functools.partial(finish_kernel, factor),
        out_shape=tuple(jax.ShapeDtypeStruct(s, F32) for s in shapes),
        name="sum_parts",
    )(parts)


def body(
    tokens,
    output_gradient,
    selected_expert_index,
    routing_weight_rows,
    fixed_gate_up_weight,
    fixed_down_weight_flipped,
    gate_up_adapter_narrow,
    gate_up_adapter_widen,
    down_adapter_narrow,
    down_adapter_widen,
):
    experts = lax.axis_size("expert")
    groups = lax.axis_size("dp")
    tok_rows, model_width = tokens.shape
    cap = tok_rows // 8
    width = fixed_down_weight_flipped.shape[2]
    rank = down_adapter_narrow.shape[2]
    factor = 0.5 / math.sqrt(tok_rows * groups * experts)
    pieces = gather_weights([fixed_gate_up_weight[0], fixed_down_weight_flipped[0]])
    rows = pack_rows(
        selected_expert_index.T, routing_weight_rows.T, tokens, output_gradient, experts, cap
    )
    rows = lax.all_to_all(rows, "expert", 0, 0, tiled=True)
    index = lax.axis_index("dp").astype(jnp.int32)
    place = jnp.stack([index // 2, index % 2])
    keep, send = gradients(
        place,
        rows,
        pieces,
        gate_up_adapter_narrow[0],
        gate_up_adapter_widen[0],
        down_adapter_narrow[0].T,
        down_adapter_widen[0],
        groups,
    )
    other = lax.ppermute(send, "dp", [(i, i ^ 1) for i in range(groups)])
    pair = (keep.astype(F32) + other.astype(F32)).astype(BF16)
    lines = [[2 * i + c for i in range(groups // 2)] for c in range(2)]
    parts = lax.all_to_all(pair, "dp", 0, 0, tiled=True, axis_index_groups=lines)
    shapes = (
        (1, model_width // groups, 2 * rank),
        (1, 2 * rank // groups, width),
        (1, width // groups, rank),
        (1, rank // groups, model_width),
    )
    return finish(parts, factor, shapes)


def solution(mesh):
    in_specs = (
        P(("dp", "expert"), None),
        P(("dp", "expert"), None),
        P(("dp", "expert"), None),
        P(("dp", "expert"), None),
        P("expert", "dp", None),
        P("expert", "dp", None),
        P("expert", None, None),
        P("expert", None, None),
        P("expert", None, None),
        P("expert", None, None),
    )
    out_specs = (
        P("expert", "dp", None),
        P("expert", "dp", None),
        P("expert", "dp", None),
        P("expert", "dp", None),
    )
    return jax.shard_map(body, mesh=mesh, in_specs=in_specs, out_specs=out_specs, check_vma=False)
```

time: 182 us -> 164 us (0.901)
  waiting for transfers between devices: 97.9 us -> 56.2 us
  starting transfers between devices: 15.4 us -> 56.5 us
  between operations: 14.1 us -> 0.97 us
  other arithmetic: 3.29 us -> 0.37 us
  Pallas kernels: 24.9 us -> 22.5 us
    all_to_all x1, waiting for transfers between devices: 95.7 us -> 9.84 us  [body(): rows = lax.all_to_all(rows, 'expert', 0, 0, tiled=True)]
    ppermute x0 -> x15, waiting for transfers between devices: none -> 44.4 us  [the longest x7 41.9 us: gather_weights(): lax.ppermute(a, 'dp', [(i, (i + 2 * way(i)) % groups) for i in range(grou...]
    ppermute x0 -> x15, starting transfers between devices: none -> 41 us  [the longest x7 24.2 us: gather_weights(): lax.ppermute(a, 'dp', [(i, (i + 2 * way(i)) % groups) for i in range(grou...]
    pallas_call x2, Pallas kernels: 23.1 us -> 20.7 us  [the longest x1 16.9 us: gradients(): pl.pallas_call(functools.partial(gradients_kernel, block, parts // 2), in...]
    concatenate x1, other arithmetic: 2.07 us -> 0.06 us  [gather_weights(): up = down = jnp.concatenate(shards, axis=1)]
  transfers between devices with their start and end apart: 3 -> 17, of which waited for: 2 -> 8; matrix products, arithmetic and copies ran while one was open for 0% -> 0% of each run, Pallas kernels for 3% -> 0%
where the time goes in v3:
time: 164 us; the launch traced here: 163 us
  starting transfers between devices  56.5 us (34%)
  waiting for transfers between devices  56.2 us (34%)
  blocking collectives  26.2 us (16%)
  Pallas kernels  22.5 us (14%)
    ppermute x7, waiting for transfers between devices, gather_weights(): lax.ppermute(a, 'dp', [(i, (i + 2 * way(i)) % groups) for i in range(grou...  41.9 us
    all_to_all x1, blocking collectives, body(): lax.all_to_all(pair, 'dp', 0, 0, tiled=True, axis_index_groups=lines)  26.2 us
    ppermute x7, starting transfers between devices, gather_weights(): lax.ppermute(a, 'dp', [(i, (i + 2 * way(i)) % groups) for i in range(grou...  24.2 us
    pallas_call x1, Pallas kernels, gradients(): pl.pallas_call(functools.partial(gradients_kernel, block, parts // 2), in...  16.9 us
    ppermute x8, starting transfers between devices, gather_weights(): swap = lambda a: lax.ppermute(a, 'dp', [(i, i ^ 1) for i in range(groups)])  16.8 us
    all_to_all x1, starting transfers between devices, body(): rows = lax.all_to_all(rows, 'expert', 0, 0, tiled=True)  13.6 us
    all_to_all x1, waiting for transfers between devices, body(): rows = lax.all_to_all(rows, 'expert', 0, 0, tiled=True)  9.84 us
    pallas_call x1, Pallas kernels, pack_rows(): pl.pallas_call(functools.partial(pack_kernel, cap), in_specs=[pl.BlockSpe...  3.78 us
  transfers between devices with their start and end apart: 17, of which 8 were waited for; matrix products, arithmetic and copies ran while one was open for 0% of the time, Pallas kernels for 0%

profile of v3, /device:TPU:6, one launch (start us, length us, event | category | flops | bytes accessed | tf_op | source)
XLA Modules:
  0.0 162.8 jit_solution(5942325168265058950)
XLA Ops:
  0.6 3.8 %pack_rows.1 = bf16[32,32,2048]{2,1,0:T(8,128)(2,1)} custom-call(s32[8,128]{1,0:T(8,128)} %bitcast.14, f32[8,128]{1,0:T(8,128)} %bitcast.15, bf16[128,2048]{1,0:T(8,128)(2,1)} %tok_hbm.1, bf16[128,2048]{1,0:T(8,128)(2,1)} %cot_hbm.1), custom_call_target="tpu_custom_call" | custom-call | flops 536870912 | bytes 5242880 | tf_op jit(solution)/shard_map/pack_rows/pallas_call | solution.py:90
  4.4 13.6 %all-to-all-start = ((bf16[32,32,2048]{2,1,0:T(8,128)(2,1)}), bf16[32,32,2048]{2,1,0:T(8,128)(2,1)}, u32[]{:S(2)}, u32[]{:S(2)}) async-start(bf16[32,32,2048]{2,1,0:T(8,128)(2,1)} %pack_rows.1), calls=%async_computation | async-start | bytes 8388608 | tf_op jit(solution)/shard_map/all_to_all | solution.py:383
  18.2 3.5 %collective-permute-start = (bf16[128,3072]{1,0:T(8,128)(2,1)S(1)}, bf16[128,3072]{1,0:T(8,128)(2,1)S(1)}, u32[]{:S(2)}, u32[]{:S(2)}) collective-permute-start(bf16[128,3072]{1,0:T(8,128)(2,1)S(1)} %pad_maximum_fusion.refs_0_), channel_id=1, source_target_pairs={{0,64},{32,96},{64,128},{96,160},{128,192},{160,224},{192,256},{22... | collective-permute-start | bytes 2359304 | tf_op jit(solution)/shard_map/ppermute | solution.py:120
  21.6 3.8 %collective-permute-start.1 = (bf16[128,3072]{1,0:T(8,128)(2,1)S(1)}, bf16[128,3072]{1,0:T(8,128)(2,1)S(1)}, u32[]{:S(2)}, u32[]{:S(2)}) collective-permute-start(bf16[128,3072]{1,0:T(8,128)(2,1)S(1)} %pad_maximum_fusion.refs_0_), channel_id=1, source_target_pairs={{0,448},{32,480},{64,0},{96,32},{128,64},{160,96},{192,128},{224,1... | collective-permute-start | bytes 2359304 | tf_op jit(solution)/shard_map/ppermute | solution.py:120
  25.5 15.0 %collective-permute-done.refs_1_ = bf16[128,3072]{1,0:T(8,128)(2,1)S(1)} collective-permute-done((bf16[128,3072]{1,0:T(8,128)(2,1)S(1)}, bf16[128,3072]{1,0:T(8,128)(2,1)S(1)}, u32[]{:S(2)}, u32[]{:S(2)}) %collective-permute-start) | collective-permute-done | bytes 786464 | tf_op jit(solution)/shard_map/ppermute | solution.py:120
  42.5 5.1 %collective-permute-start.3 = (bf16[128,3072]{1,0:T(8,128)(2,1)S(1)}, bf16[128,3072]{1,0:T(8,128)(2,1)}, u32[]{:S(2)}, u32[]{:S(2)}) collective-permute-start(bf16[128,3072]{1,0:T(8,128)(2,1)S(1)} %collective-permute-done.1.refs_2_), channel_id=1, source_target_pairs={{0,448},{32,480},{64,0},{96,32},{128,64},{160,96},{192,128},{224,1... | collective-permute-start | bytes 2359304 | tf_op jit(solution)/shard_map/ppermute | solution.py:120
  47.6 14.3 %collective-permute-done.2.refs_3_ = bf16[128,3072]{1,0:T(8,128)(2,1)} collective-permute-done((bf16[128,3072]{1,0:T(8,128)(2,1)S(1)}, bf16[128,3072]{1,0:T(8,128)(2,1)}, u32[]{:S(2)}, u32[]{:S(2)}) %collective-permute-start.2) | collective-permute-done | bytes 786464 | tf_op jit(solution)/shard_map/ppermute | solution.py:120
  63.8 5.1 %collective-permute-start.5 = (bf16[128,3072]{1,0:T(8,128)(2,1)}, bf16[128,3072]{1,0:T(8,128)(2,1)S(1)}, u32[]{:S(2)}, u32[]{:S(2)}) collective-permute-start(bf16[128,3072]{1,0:T(8,128)(2,1)} %collective-permute-done.3.refs_4_), channel_id=1, source_target_pairs={{0,448},{32,480},{64,0},{96,32},{128,64},{160,96},{192,128},{224,1... | collective-permute-start | bytes 2359304 | tf_op jit(solution)/shard_map/ppermute | solution.py:120
  69.0 1.9 %collective-permute-start.7 = (bf16[128,3072]{1,0:T(8,128)(2,1)S(1)}, bf16[128,3072]{1,0:T(8,128)(2,1)}, u32[]{:S(2)}, u32[]{:S(2)}) collective-permute-start(bf16[128,3072]{1,0:T(8,128)(2,1)S(1)} %pad_maximum_fusion.refs_0_), channel_id=1, source_target_pairs={{0,32},{32,0},{64,96},{96,64},{128,160},{160,128},{192,224},{224,1... | collective-permute-start | bytes 2359304 | tf_op jit(solution)/shard_map/ppermute | solution.py:119
  70.9 2.4 %collective-permute-start.8 = (bf16[128,3072]{1,0:T(8,128)(2,1)S(1)}, bf16[128,3072]{1,0:T(8,128)(2,1)S(1)}, u32[]{:S(2)}, u32[]{:S(2)}) collective-permute-start(bf16[128,3072]{1,0:T(8,128)(2,1)S(1)} %collective-permute-done.refs_1_), channel_id=1, source_target_pairs={{0,32},{32,0},{64,96},{96,64},{128,160},{160,128},{192,224},{224,1... | collective-permute-start | bytes 2359304 | tf_op jit(solution)/shard_map/ppermute | solution.py:119
  73.3 1.9 %collective-permute-start.9 = (bf16[128,3072]{1,0:T(8,128)(2,1)}, bf16[128,3072]{1,0:T(8,128)(2,1)S(1)}, u32[]{:S(2)}, u32[]{:S(2)}) collective-permute-start(bf16[128,3072]{1,0:T(8,128)(2,1)} %copy-done.6), channel_id=1, source_target_pairs={{0,32},{32,0},{64,96},{96,64},{128,160},{160,128},{192,224},{224,1... | collective-permute-start | bytes 2359304 | tf_op jit(solution)/shard_map/ppermute | solution.py:119
  75.3 7.2 %collective-permute-done.4.refs_5_ = bf16[128,3072]{1,0:T(8,128)(2,1)S(1)} collective-permute-done((bf16[128,3072]{1,0:T(8,128)(2,1)}, bf16[128,3072]{1,0:T(8,128)(2,1)S(1)}, u32[]{:S(2)}, u32[]{:S(2)}) %collective-permute-start.4) | collective-permute-done | bytes 786464 | tf_op jit(solution)/shard_map/ppermute | solution.py:120
  83.9 2.8 %collective-permute-start.6 = (bf16[128,3072]{1,0:T(8,128)(2,1)S(1)}, bf16[128,3072]{1,0:T(8,128)(2,1)}, u32[]{:S(2)}, u32[]{:S(2)}) collective-permute-start(bf16[128,3072]{1,0:T(8,128)(2,1)S(1)} %broadcast_select_fusion), channel_id=1, source_target_pairs={{0,64},{32,480},{64,128},{96,32},{128,192},{160,96},{192,256},{224... | collective-permute-start | bytes 2359304 | tf_op jit(solution)/shard_map/ppermute | solution.py:120
  86.7 1.9 %collective-permute-start.10 = (bf16[128,3072]{1,0:T(8,128)(2,1)}, bf16[128,3072]{1,0:T(8,128)(2,1)}, u32[]{:S(2)}, u32[]{:S(2)}) collective-permute-start(bf16[128,3072]{1,0:T(8,128)(2,1)} %collective-permute-done.2.refs_3_), channel_id=1, source_target_pairs={{0,32},{32,0},{64,96},{96,64},{128,160},{160,128},{192,224},{224,1... | collective-permute-start | bytes 2359304 | tf_op jit(solution)/shard_map/ppermute | solution.py:119
  88.6 2.4 %collective-permute-start.11 = (bf16[128,3072]{1,0:T(8,128)(2,1)}, bf16[128,3072]{1,0:T(8,128)(2,1)}, u32[]{:S(2)}, u32[]{:S(2)}) collective-permute-start(bf16[128,3072]{1,0:T(8,128)(2,1)} %collective-permute-done.3.refs_4_), channel_id=1, source_target_pairs={{0,32},{32,0},{64,96},{96,64},{128,160},{160,128},{192,224},{224,1... | collective-permute-start | bytes 2359304 | tf_op jit(solution)/shard_map/ppermute | solution.py:119
  91.0 1.9 %collective-permute-start.12 = (bf16[128,3072]{1,0:T(8,128)(2,1)S(1)}, bf16[128,3072]{1,0:T(8,128)(2,1)}, u32[]{:S(2)}, u32[]{:S(2)}) collective-permute-start(bf16[128,3072]{1,0:T(8,128)(2,1)S(1)} %collective-permute-done.4.refs_5_), channel_id=1, source_target_pairs={{0,32},{32,0},{64,96},{96,64},{128,160},{160,128},{192,224},{224,1... | collective-permute-start | bytes 2359304 | tf_op jit(solution)/shard_map/ppermute | solution.py:119
  93.0 2.4 %collective-permute-start.13 = (bf16[128,3072]{1,0:T(8,128)(2,1)S(1)}, bf16[128,3072]{1,0:T(8,128)(2,1)}, u32[]{:S(2)}, u32[]{:S(2)}) collective-permute-start(bf16[128,3072]{1,0:T(8,128)(2,1)S(1)} %collective-permute-done.5.refs_6_), channel_id=1, source_target_pairs={{0,32},{32,0},{64,96},{96,64},{128,160},{160,128},{192,224},{224,1... | collective-permute-start | bytes 2359304 | tf_op jit(solution)/shard_map/ppermute | solution.py:119
  95.4 4.0 %collective-permute-done.6.refs_7_ = bf16[128,3072]{1,0:T(8,128)(2,1)} collective-permute-done((bf16[128,3072]{1,0:T(8,128)(2,1)S(1)}, bf16[128,3072]{1,0:T(8,128)(2,1)}, u32[]{:S(2)}, u32[]{:S(2)}) %collective-permute-start.6) | collective-permute-done | bytes 786464 | tf_op jit(solution)/shard_map/ppermute | solution.py:120
  101.5 2.5 %collective-permute-done.14.refs_15_ = bf16[128,3072]{1,0:T(8,128)(2,1)} collective-permute-done((bf16[128,3072]{1,0:T(8,128)(2,1)}, bf16[128,3072]{1,0:T(8,128)(2,1)}, u32[]{:S(2)}, u32[]{:S(2)}) %collective-permute-start.14) | collective-permute-done | bytes 786464 | tf_op jit(solution)/shard_map/ppermute | solution.py:119
  104.0 9.8 %all-to-all-done.rows_hbm = bf16[32,32,2048]{2,1,0:T(8,128)(2,1)} async-done(((bf16[32,32,2048]{2,1,0:T(8,128)(2,1)}), bf16[32,32,2048]{2,1,0:T(8,128)(2,1)}, u32[]{:S(2)}, u32[]{:S(2)}) %all-to-all-start) | async-done | bytes 4194336 | tf_op jit(solution)/shard_map/all_to_all | solution.py:383
  113.8 16.9 %gradients.1 = (bf16[8,288,128]{2,1,0:T(8,128)(2,1)S(1)}, bf16[8,288,128]{2,1,0:T(8,128)(2,1)S(1)}) custom-call(s32[2]{0:T(128)S(1)} %pad_add_fusion.place_ref, bf16[32,32,2048]{2,1,0:T(8,128)(2,1)} %all-to-all-done.rows_hbm, bf16[2048,128]{1,0:T(8,128)(2,1)} %bitcast.16, bf16[64,2048]{1,0:T(8,128)(2,1)} %bitcast.17, bf16[64,1024]{1,0:T(8,128)(2,1)} %bitcast.19, ...), custom_call_target="tpu_custom_call" | custom-call | flops 7247757312 | bytes 16777216 | tf_op jit(solution)/shard_map/gradients/pallas_call | solution.py:294
  130.7 1.9 %collective-permute-start.15 = (bf16[8,288,128]{2,1,0:T(8,128)(2,1)S(1)}, bf16[8,288,128]{2,1,0:T(8,128)(2,1)S(1)}, u32[]{:S(2)}, u32[]{:S(2)}) collective-permute-start(bf16[8,288,128]{2,1,0:T(8,128)(2,1)S(1)} %get-tuple-element.7), channel_id=1, source_target_pairs={{0,32},{32,0},{64,96},{96,64},{128,160},{160,128},{192,224},{224,1... | collective-permute-start | bytes 1769480 | tf_op jit(solution)/shard_map/ppermute | solution.py:396
  132.7 2.0 %collective-permute-done.15 = bf16[8,288,128]{2,1,0:T(8,128)(2,1)S(1)} collective-permute-done((bf16[8,288,128]{2,1,0:T(8,128)(2,1)S(1)}, bf16[8,288,128]{2,1,0:T(8,128)(2,1)S(1)}, u32[]{:S(2)}, u32[]{:S(2)}) %collective-permute-start.15) | collective-permute-done | bytes 589856 | tf_op jit(solution)/shard_map/ppermute | solution.py:396
  134.8 26.2 %all_to_all.10.parts_ref = bf16[8,288,128]{2,1,0:T(8,128)(2,1)} all-to-all(bf16[8,288,128]{2,1,0:T(8,128)(2,1)S(1)} %add_convert_fusion), channel_id=1, replica_groups={{0,64,128,192,256,320,384,448},{32,96,160,224,288,352,416,480},{1,65,12..., dimensions={0} | all-to-all | bytes 1179648 | tf_op jit(solution)/shard_map/all_to_all | solution.py:399
  (36 shorter events, 9.3 us)
Async XLA Ops:
  4.4 13.6 %copy-start.3 = (bf16[1,128,2048]{2,1,0:T(8,128)(2,1)S(1)}, bf16[1,128,2048]{2,1,0:T(8,128)(2,1)}, u32[]{:S(2)}) copy-start(bf16[1,128,2048]{2,1,0:T(8,128)(2,1)} %param.14) | copy-start | bytes 1572868
  4.4 13.6 %copy-start.4 = (bf16[1,128,1024]{2,1,0:T(8,128)(2,1)S(1)}, bf16[1,128,1024]{2,1,0:T(8,128)(2,1)}, u32[]{:S(2)}) copy-start(bf16[1,128,1024]{2,1,0:T(8,128)(2,1)} %param.15) | copy-start | bytes 786436
  4.4 109.4 %all-to-all-start = ((bf16[32,32,2048]{2,1,0:T(8,128)(2,1)}), bf16[32,32,2048]{2,1,0:T(8,128)(2,1)}, u32[]{:S(2)}, u32[]{:S(2)}) async-start(bf16[32,32,2048]{2,1,0:T(8,128)(2,1)} %pack_rows.1), calls=%async_computation | async-start | bytes 8388608 | tf_op jit(solution)/shard_map/all_to_all | solution.py:383
  18.1 95.7 %copy-start.2 = (bf16[128,3072]{1,0:T(8,128)(2,1)}, bf16[128,3072]{1,0:T(8,128)(2,1)S(1)}, u32[]{:S(2)}) copy-start(bf16[128,3072]{1,0:T(8,128)(2,1)S(1)} %pad_maximum_fusion.refs_0_) | copy-start | bytes 2359300
  18.2 22.4 %collective-permute-start = (bf16[128,3072]{1,0:T(8,128)(2,1)S(1)}, bf16[128,3072]{1,0:T(8,128)(2,1)S(1)}, u32[]{:S(2)}, u32[]{:S(2)}) collective-permute-start(bf16[128,3072]{1,0:T(8,128)(2,1)S(1)} %pad_maximum_fusion.refs_0_), channel_id=1, source_target_pairs={{0,64},{32,96},{64,128},{96,160},{128,192},{160,224},{192,256},{22... | collective-permute-start | bytes 2359304 | tf_op jit(solution)/shard_map/ppermute | solution.py:120
  21.6 20.8 %collective-permute-start.1 = (bf16[128,3072]{1,0:T(8,128)(2,1)S(1)}, bf16[128,3072]{1,0:T(8,128)(2,1)S(1)}, u32[]{:S(2)}, u32[]{:S(2)}) collective-permute-start(bf16[128,3072]{1,0:T(8,128)(2,1)S(1)} %pad_maximum_fusion.refs_0_), channel_id=1, source_target_pairs={{0,448},{32,480},{64,0},{96,32},{128,64},{160,96},{192,128},{224,1... | collective-permute-start | bytes 2359304 | tf_op jit(solution)/shard_map/ppermute | solution.py:120
  40.5 73.3 %copy-start.5 = (bf16[128,3072]{1,0:T(8,128)(2,1)}, bf16[128,3072]{1,0:T(8,128)(2,1)S(1)}, u32[]{:S(2)}) copy-start(bf16[128,3072]{1,0:T(8,128)(2,1)S(1)} %collective-permute-done.refs_1_) | copy-start | bytes 2359300
  40.5 21.4 %collective-permute-start.2 = (bf16[128,3072]{1,0:T(8,128)(2,1)S(1)}, bf16[128,3072]{1,0:T(8,128)(2,1)}, u32[]{:S(2)}, u32[]{:S(2)}) collective-permute-start(bf16[128,3072]{1,0:T(8,128)(2,1)S(1)} %collective-permute-done.refs_1_), channel_id=1, source_target_pairs={{0,64},{32,96},{64,128},{96,160},{128,192},{160,224},{192,256},{22... | collective-permute-start | bytes 2359304 | tf_op jit(solution)/shard_map/ppermute | solution.py:120
  42.4 21.4 %copy-start.6 = (bf16[128,3072]{1,0:T(8,128)(2,1)}, bf16[128,3072]{1,0:T(8,128)(2,1)S(1)}, u32[]{:S(2)}) copy-start(bf16[128,3072]{1,0:T(8,128)(2,1)S(1)} %collective-permute-done.1.refs_2_) | copy-start | bytes 2359300
  42.5 21.4 %collective-permute-start.3 = (bf16[128,3072]{1,0:T(8,128)(2,1)S(1)}, bf16[128,3072]{1,0:T(8,128)(2,1)}, u32[]{:S(2)}, u32[]{:S(2)}) collective-permute-start(bf16[128,3072]{1,0:T(8,128)(2,1)S(1)} %collective-permute-done.1.refs_2_), channel_id=1, source_target_pairs={{0,448},{32,480},{64,0},{96,32},{128,64},{160,96},{192,128},{224,1... | collective-permute-start | bytes 2359304 | tf_op jit(solution)/shard_map/ppermute | solution.py:120
  61.9 20.6 %collective-permute-start.4 = (bf16[128,3072]{1,0:T(8,128)(2,1)}, bf16[128,3072]{1,0:T(8,128)(2,1)S(1)}, u32[]{:S(2)}, u32[]{:S(2)}) collective-permute-start(bf16[128,3072]{1,0:T(8,128)(2,1)} %collective-permute-done.2.refs_3_), channel_id=1, source_target_pairs={{0,64},{32,96},{64,128},{96,160},{128,192},{160,224},{192,256},{22... | collective-permute-start | bytes 2359304 | tf_op jit(solution)/shard_map/ppermute | solution.py:120
  63.8 19.9 %collective-permute-start.5 = (bf16[128,3072]{1,0:T(8,128)(2,1)}, bf16[128,3072]{1,0:T(8,128)(2,1)S(1)}, u32[]{:S(2)}, u32[]{:S(2)}) collective-permute-start(bf16[128,3072]{1,0:T(8,128)(2,1)} %collective-permute-done.3.refs_4_), channel_id=1, source_target_pairs={{0,448},{32,480},{64,0},{96,32},{128,64},{160,96},{192,128},{224,1... | collective-permute-start | bytes 2359304 | tf_op jit(solution)/shard_map/ppermute | solution.py:120
  69.0 19.6 %collective-permute-start.7 = (bf16[128,3072]{1,0:T(8,128)(2,1)S(1)}, bf16[128,3072]{1,0:T(8,128)(2,1)}, u32[]{:S(2)}, u32[]{:S(2)}) collective-permute-start(bf16[128,3072]{1,0:T(8,128)(2,1)S(1)} %pad_maximum_fusion.refs_0_), channel_id=1, source_target_pairs={{0,32},{32,0},{64,96},{96,64},{128,160},{160,128},{192,224},{224,1... | collective-permute-start | bytes 2359304 | tf_op jit(solution)/shard_map/ppermute | solution.py:119
  70.9 20.1 %collective-permute-start.8 = (bf16[128,3072]{1,0:T(8,128)(2,1)S(1)}, bf16[128,3072]{1,0:T(8,128)(2,1)S(1)}, u32[]{:S(2)}, u32[]{:S(2)}) collective-permute-start(bf16[128,3072]{1,0:T(8,128)(2,1)S(1)} %collective-permute-done.refs_1_), channel_id=1, source_target_pairs={{0,32},{32,0},{64,96},{96,64},{128,160},{160,128},{192,224},{224,1... | collective-permute-start | bytes 2359304 | tf_op jit(solution)/shard_map/ppermute | solution.py:119
  73.3 19.6 %collective-permute-start.9 = (bf16[128,3072]{1,0:T(8,128)(2,1)}, bf16[128,3072]{1,0:T(8,128)(2,1)S(1)}, u32[]{:S(2)}, u32[]{:S(2)}) collective-permute-start(bf16[128,3072]{1,0:T(8,128)(2,1)} %copy-done.6), channel_id=1, source_target_pairs={{0,32},{32,0},{64,96},{96,64},{128,160},{160,128},{192,224},{224,1... | collective-permute-start | bytes 2359304 | tf_op jit(solution)/shard_map/ppermute | solution.py:119
  82.5 31.3 %copy-start = (bf16[128,3072]{1,0:T(8,128)(2,1)}, bf16[128,3072]{1,0:T(8,128)(2,1)S(1)}, u32[]{:S(2)}) copy-start(bf16[128,3072]{1,0:T(8,128)(2,1)S(1)} %collective-permute-done.4.refs_5_) | copy-start | bytes 2359300
  83.8 30.0 %copy-start.1 = (bf16[128,3072]{1,0:T(8,128)(2,1)}, bf16[128,3072]{1,0:T(8,128)(2,1)S(1)}, u32[]{:S(2)}) copy-start(bf16[128,3072]{1,0:T(8,128)(2,1)S(1)} %collective-permute-done.5.refs_6_) | copy-start | bytes 2359300
  83.9 15.6 %collective-permute-start.6 = (bf16[128,3072]{1,0:T(8,128)(2,1)S(1)}, bf16[128,3072]{1,0:T(8,128)(2,1)}, u32[]{:S(2)}, u32[]{:S(2)}) collective-permute-start(bf16[128,3072]{1,0:T(8,128)(2,1)S(1)} %broadcast_select_fusion), channel_id=1, source_target_pairs={{0,64},{32,480},{64,128},{96,32},{128,192},{160,96},{192,256},{224... | collective-permute-start | bytes 2359304 | tf_op jit(solution)/shard_map/ppermute | solution.py:120
  86.7 14.8 %collective-permute-start.10 = (bf16[128,3072]{1,0:T(8,128)(2,1)}, bf16[128,3072]{1,0:T(8,128)(2,1)}, u32[]{:S(2)}, u32[]{:S(2)}) collective-permute-start(bf16[128,3072]{1,0:T(8,128)(2,1)} %collective-permute-done.2.refs_3_), channel_id=1, source_target_pairs={{0,32},{32,0},{64,96},{96,64},{128,160},{160,128},{192,224},{224,1... | collective-permute-start | bytes 2359304 | tf_op jit(solution)/shard_map/ppermute | solution.py:119
  88.6 12.9 %collective-permute-start.11 = (bf16[128,3072]{1,0:T(8,128)(2,1)}, bf16[128,3072]{1,0:T(8,128)(2,1)}, u32[]{:S(2)}, u32[]{:S(2)}) collective-permute-start(bf16[128,3072]{1,0:T(8,128)(2,1)} %collective-permute-done.3.refs_4_), channel_id=1, source_target_pairs={{0,32},{32,0},{64,96},{96,64},{128,160},{160,128},{192,224},{224,1... | collective-permute-start | bytes 2359304 | tf_op jit(solution)/shard_map/ppermute | solution.py:119
  91.0 10.4 %collective-permute-start.12 = (bf16[128,3072]{1,0:T(8,128)(2,1)S(1)}, bf16[128,3072]{1,0:T(8,128)(2,1)}, u32[]{:S(2)}, u32[]{:S(2)}) collective-permute-start(bf16[128,3072]{1,0:T(8,128)(2,1)S(1)} %collective-permute-done.4.refs_5_), channel_id=1, source_target_pairs={{0,32},{32,0},{64,96},{96,64},{128,160},{160,128},{192,224},{224,1... | collective-permute-start | bytes 2359304 | tf_op jit(solution)/shard_map/ppermute | solution.py:119
  93.0 8.5 %collective-permute-start.13 = (bf16[128,3072]{1,0:T(8,128)(2,1)S(1)}, bf16[128,3072]{1,0:T(8,128)(2,1)}, u32[]{:S(2)}, u32[]{:S(2)}) collective-permute-start(bf16[128,3072]{1,0:T(8,128)(2,1)S(1)} %collective-permute-done.5.refs_6_), channel_id=1, source_target_pairs={{0,32},{32,0},{64,96},{96,64},{128,160},{160,128},{192,224},{224,1... | collective-permute-start | bytes 2359304 | tf_op jit(solution)/shard_map/ppermute | solution.py:119
  99.4 4.5 %collective-permute-start.14 = (bf16[128,3072]{1,0:T(8,128)(2,1)}, bf16[128,3072]{1,0:T(8,128)(2,1)}, u32[]{:S(2)}, u32[]{:S(2)}) collective-permute-start(bf16[128,3072]{1,0:T(8,128)(2,1)} %collective-permute-done.6.refs_7_), channel_id=1, source_target_pairs={{0,32},{32,0},{64,96},{96,64},{128,160},{160,128},{192,224},{224,1... | collective-permute-start | bytes 2359304 | tf_op jit(solution)/shard_map/ppermute | solution.py:119
  130.7 3.9 %collective-permute-start.15 = (bf16[8,288,128]{2,1,0:T(8,128)(2,1)S(1)}, bf16[8,288,128]{2,1,0:T(8,128)(2,1)S(1)}, u32[]{:S(2)}, u32[]{:S(2)}) collective-permute-start(bf16[8,288,128]{2,1,0:T(8,128)(2,1)S(1)} %get-tuple-element.7), channel_id=1, source_target_pairs={{0,32},{32,0},{64,96},{96,64},{128,160},{160,128},{192,224},{224,1... | collective-permute-start | bytes 1769480 | tf_op jit(solution)/shard_map/ppermute | solution.py:396
  (2 other events, 14.9 us)

commit v4 on v3

--- a/solution.py
+++ b/solution.py
@@ -11,11 +11,16 @@
 F32 = jnp.float32
 BF16 = jnp.bfloat16
 LANES = 128
+BLOCK = 512
 VMEM = 44 * 2**20
 
 
 def in_hbm(*arrays):
     return [pltpu.with_memory_space_constraint(a, pltpu.HBM) for a in arrays]
+
+
+def in_vmem(*arrays):
+    return [pltpu.with_memory_space_constraint(a, pltpu.VMEM) for a in arrays]
 
 
 def dot_nt(a, b):
@@ -43,7 +48,7 @@
     cap, sel_hbm, wgt_hbm, tok_hbm, cot_hbm, out_hbm, sel_s, wgt_s, tok_s, cot_s, out_s, hot_s, row_s, sems
 ):
     experts, _, width = out_s.shape
-    cols = width // 4
+    cols = width // 8
 
     def fetch(src, dst, i):
         copy = pltpu.make_async_copy(src, dst, sems.at[i])
@@ -100,7 +105,7 @@
             pltpu.VMEM(out.shape, BF16),
             pltpu.VMEM((experts * cap, toks), BF16),
             pltpu.VMEM((experts * cap, LANES), F32),
-            pltpu.SemaphoreType.DMA((8,)),
+            pltpu.SemaphoreType.DMA((12,)),
         ],
         cost_estimate=pl.CostEstimate(
             flops=4 * experts * cap * toks * width,
@@ -110,6 +115,15 @@
         compiler_params=pltpu.CompilerParams(vmem_limit_bytes=VMEM),
         name="pack_rows",
     )(*in_hbm(sel_t, wgt_t, tok, cot))
+
+
+def column_blocks(gate_up, down):
+    units = down.shape[1]
+    cut = lambda a, first: a[:, first : first + BLOCK]
+    blocks = []
+    for at in range(0, units, BLOCK):
+        blocks += [cut(gate_up, at), cut(gate_up, units + at), cut(down, at)]
+    return blocks
 
 
 def gather_weights(shards):
@@ -141,25 +155,23 @@
 
 
 def gradients_kernel(
-    block,
     chips,
     place_ref,
     rows_hbm,
-    narrow_hbm,
-    dw_hbm,
-    dnt_hbm,
-    win_hbm,
+    narrow_s,
+    dw_s,
+    dnt_s,
+    win_s,
     *refs,
 ):
     pieces, refs = refs[: 2 * chips], refs[2 * chips :]
-    keep_ref, send_ref, x_s, y_s, w_s, narrow_s, dw_s, dnt_s, win_s = refs[:9]
-    hid_s, dgate_s, dup_s, inb_s, dna_s, dnb_s, ina_s, sems = refs[9:]
-    sources, pair, width = rows_hbm.shape
-    cap = pair // 2
-    slots = sources * cap
+    keep_ref, send_ref, x_rows, y_rows, x_s, y_s, w_s = refs[:7]
+    hid_s, dgate_s, dup_s, inb_s, dna_s, dnb_s, ina_s, sems = refs[7:]
+    slots = x_rows.shape[0]
+    cap, width = x_s.shape[1:]
     rank, units = dnt_s.shape
-    deeper = x_s.shape[2]
-    steps = units // block
+    steps = units // BLOCK
+    firsts = piece_rows(chips, pieces[0].shape[0], place_ref[0], place_ref[1])
     used = iter(range(sems.shape[0]))
 
     def fetch(src, dst):
@@ -167,73 +179,54 @@
         copy.start()
         return copy
 
-    def columns(part, step):
-        return pl.ds(part * units + step * block, block)
-
-    firsts = piece_rows(chips, pieces[0].shape[0], place_ref[0], place_ref[1])
-    cols_in = {}
-
-    def fetch_columns(part, step):
-        at = columns(part, step)
-        cols_in[part, step] = [
-            fetch(piece.at[:, at], w_s.at[pl.ds(first, piece.shape[0]), at])
-            for piece, first in zip(pieces, firsts)
+    def fetch_blocks(first, last):
+        at = pl.ds(first * BLOCK, (last - first) * BLOCK)
+        return [
+            fetch(piece.at[:, at], w_s.at[pl.ds(row, piece.shape[0]), at])
+            for piece, row in zip(pieces, firsts)
         ]
 
-    def wait_columns(part, step):
-        for copy in cols_in[part, step]:
+    def wait(copies):
+        for copy in copies:
             copy.wait()
 
-    x_in = fetch(rows_hbm.at[:, pl.ds(0, cap), :], x_s.at[:, :, pl.ds(0, width)])
-    narrow_in = fetch(narrow_hbm, narrow_s)
-    fetch_columns(0, 0)
-    win_in = fetch(win_hbm, win_s)
-    fetch_columns(1, 0)
-    y_in = fetch(rows_hbm.at[:, pl.ds(cap, cap), :], y_s.at[:, :, pl.ds(0, width)])
-    dw_in = fetch(dw_hbm, dw_s)
-    dnt_in = fetch(dnt_hbm, dnt_s)
-
-    def times(rows_ref, part, step):
-        return dot_nn(rows_ref[...].reshape(slots, deeper), w_s[:, columns(part, step)])
-
+    def block(i):
+        return w_s[:, i * BLOCK : (i + 1) * BLOCK]
+
+    x_in = [fetch(rows_hbm.at[:, pl.ds(0, cap), :], x_s)]
+    y_in = [fetch(rows_hbm.at[:, pl.ds(cap, cap), :], y_s)]
+    y_in += fetch_blocks(0, 1)
+    u_in = fetch_blocks(1, 3)
+    wait(x_in)
+    zero = jnp.zeros((rank, BLOCK), BF16)
     for step in range(steps):
-        at = pl.ds(step * block, block)
-        if step == 0:
-            x_in.wait()
-            narrow_in.wait()
-            x = x_s[:, :, :width].reshape(slots, width)
-            low_f = dot_nn(x, narrow_s[...])
-            low = low_f.astype(BF16)
-            low_t = low_f.T.astype(BF16)
-            x_s[:, :, width:] = low.reshape(sources, cap, 2 * rank)
-            win_in.wait()
-            win = (0.5 * win_s[...].astype(F32)).astype(BF16)
-            zero = jnp.zeros((rank, units), BF16)
-            w_s[width:, :units] = jnp.concatenate([win[:rank], zero], axis=0)
-            w_s[width:, units : 2 * units] = jnp.concatenate([zero, win[rank:]], axis=0)
-        wait_columns(0, step)
-        fetch_columns(2, step)
-        gate = times(x_s, 0, step)
-        wait_columns(1, step)
-        if step + 1 < steps:
-            fetch_columns(0, step + 1)
-        up = times(x_s, 1, step)
-        if step == 0:
-            y_in.wait()
-            dw_in.wait()
-            dnt_in.wait()
-            y = y_s[:, :, :width].reshape(slots, width)
-            z_f = dot_nt(y, dw_s[...])
-            z = z_f.astype(BF16)
-            z_t = z_f.T.astype(BF16)
-            z = jnp.concatenate([z, jnp.zeros_like(z)], axis=1)
-            y_s[:, :, width:] = z.reshape(sources, cap, 2 * rank)
-            dnt = (0.5 * dnt_s[...].astype(F32)).astype(BF16)
-            w_s[width:, 2 * units :] = jnp.concatenate([dnt, zero], axis=0)
-        wait_columns(2, step)
-        if step + 1 < steps:
-            fetch_columns(1, step + 1)
-        dhid = times(y_s, 2, step)
+        at = slice(step * BLOCK, (step + 1) * BLOCK)
+        win = (0.5 * win_s[:, at].astype(F32)).astype(BF16)
+        dnt = (0.5 * dnt_s[:, at].astype(F32)).astype(BF16)
+        extra = [[win[:rank], zero], [zero, win[rank:]], [dnt, zero]]
+        for part in range(3):
+            i = 3 * step + part
+            w_s[width:, i * BLOCK : (i + 1) * BLOCK] = jnp.concatenate(extra[part], axis=0)
+    x_rows[:, :width] = x_s[...].reshape(slots, width)
+    low = dot_nn(x_rows[:, :width], narrow_s[...])
+    low_t = low.T.astype(BF16)
+    x_rows[:, width:] = low.astype(BF16)
+    rest = fetch_blocks(3, 6)
+    wait(y_in)
+    y_rows[:, :width] = y_s[...].reshape(slots, width)
+    z = dot_nt(y_rows[:, :width], dw_s[...])
+    z_t = z.T.astype(BF16)
+    z = z.astype(BF16)
+    y_rows[:, width:] = jnp.concatenate([z, jnp.zeros_like(z)], axis=1)
+    vals = [dot_nn(x_rows[...], block(0))]
+    wait(u_in)
+    vals += [dot_nn(x_rows[...], block(1)), dot_nn(y_rows[...], block(2))]
+    wait(rest)
+    for i in range(3, 6):
+        vals.append(dot_nn(y_rows[...] if i % 3 == 2 else x_rows[...], block(i)))
+    for step in range(steps):
+        at = pl.ds(step * BLOCK, BLOCK)
+        gate, up, dhid = vals[3 * step : 3 * step + 3]
         sig = jax.nn.sigmoid(gate)
         silu = gate * sig
         hid_s[:, at] = (silu * up).astype(BF16)
@@ -247,8 +240,8 @@
     dna_s[...] = dot_nn(z_t, hid_s[...])
     inb_s[:rank, :] = dot_nn(low_t[:rank, :], dgate_s[...])
     inb_s[rank:, :] = dot_nn(low_t[rank:, :], dup_s[...])
-    dnb_s[...] = dot_nn(hlow_t, y_s[:, :, :width].reshape(slots, width))
-    ina_s[...] = dot_nn(vlow_t, x_s[:, :, :width].reshape(slots, width))
+    dnb_s[...] = dot_nn(hlow_t, y_rows[:, :width])
+    ina_s[...] = dot_nn(vlow_t, x_rows[:, :width])
 
     even = place_ref[1] == 0
     reach = width // 2
@@ -284,28 +277,26 @@
     cap = pair // 2
     slots = sources * cap
     rank, units = dnt.shape
-    block = 512
     lines = (2 * rank * units + units * rank + rank * width) // (parts * LANES) + width // parts
     out = pltpu.VMEM((parts // 2, lines, LANES), BF16)
     out_spec = pl.BlockSpec(memory_space=pltpu.VMEM)
-    acts = pltpu.VMEM((sources, cap, width + 2 * rank), BF16)
+    acts = pltpu.VMEM((sources, cap, width), BF16)
+    deep = pltpu.VMEM((slots, width + 2 * rank), BF16)
     hidden = pltpu.VMEM((slots, units), BF16)
-    like = lambda a: pltpu.VMEM(a.shape, a.dtype)
     return pl.pallas_call(
-        functools.partial(gradients_kernel, block, parts // 2),
+        functools.partial(gradients_kernel, parts // 2),
         in_specs=[pl.BlockSpec(memory_space=pltpu.SMEM)]
-        + [pl.BlockSpec(memory_space=pltpu.HBM)] * 5
+        + [pl.BlockSpec(memory_space=pl.ANY)]
+        + [pl.BlockSpec(memory_space=pltpu.VMEM)] * 4
         + [pl.BlockSpec(memory_space=pl.ANY)] * len(pieces),
         out_shape=(out, out),
         out_specs=(out_spec, out_spec),
         scratch_shapes=[
+            deep,
+            deep,
             acts,
             acts,
             pltpu.VMEM((width + 2 * rank, 3 * units), BF16),
-            like(narrow),
-            like(dw),
-            like(dnt),
-            like(win),
             hidden,
             hidden,
             hidden,
@@ -313,7 +304,7 @@
             pltpu.VMEM((rank, units), F32),
             pltpu.VMEM((rank, width), F32),
             pltpu.VMEM((2 * rank, width), F32),
-            pltpu.SemaphoreType.DMA((6 + 3 * len(pieces) * (units // block),)),
+            pltpu.SemaphoreType.DMA((6 + 3 * len(pieces) * (units // BLOCK),)),
         ],
         cost_estimate=pl.CostEstimate(
             flops=2 * slots * width * (3 * units + 6 * rank),
@@ -322,7 +313,7 @@
         ),
         compiler_params=pltpu.CompilerParams(vmem_limit_bytes=VMEM),
         name="gradients",
-    )(place, *in_hbm(rows, narrow, dw, dnt, win, *pieces))
+    )(place, *in_hbm(rows), *in_vmem(narrow, dw, dnt, win), *in_hbm(*pieces))
 
 
 def finish_kernel(factor, parts_ref, ina_ref, inb_ref, dna_ref, dnb_ref):
@@ -354,7 +345,7 @@
         functools.partial(finish_kernel, factor),
         out_shape=tuple(jax.ShapeDtypeStruct(s, F32) for s in shapes),
         name="sum_parts",
-    )(parts)
+    )(*in_vmem(parts))
 
 
 def body(
@@ -376,7 +367,7 @@
     width = fixed_down_weight_flipped.shape[2]
     rank = down_adapter_narrow.shape[2]
     factor = 0.5 / math.sqrt(tok_rows * groups * experts)
-    pieces = gather_weights([fixed_gate_up_weight[0], fixed_down_weight_flipped[0]])
+    pieces = gather_weights(column_blocks(fixed_gate_up_weight[0], fixed_down_weight_flipped[0]))
     rows = pack_rows(
         selected_expert_index.T, routing_weight_rows.T, tokens, output_gradient, experts, cap
     )

time: 164 us -> 161 us (0.982)
  Pallas kernels: 22.5 us -> 20.4 us
where the time goes in v4:
time: 161 us
  starting transfers between devices  56.8 us (35%)
  waiting for transfers between devices  55.8 us (35%)
  blocking collectives  26.1 us (16%)
  Pallas kernels  20.4 us (13%)
    ppermute x7, waiting for transfers between devices, gather_weights(): lax.ppermute(a, 'dp', [(i, (i + 2 * way(i)) % groups) for i in range(grou...  41.7 us
    all_to_all x1, blocking collectives, body(): lax.all_to_all(pair, 'dp', 0, 0, tiled=True, axis_index_groups=lines)  26.1 us
    ppermute x7, starting transfers between devices, gather_weights(): lax.ppermute(a, 'dp', [(i, (i + 2 * way(i)) % groups) for i in range(grou...  24.2 us
    ppermute x8, starting transfers between devices, gather_weights(): swap = lambda a: lax.ppermute(a, 'dp', [(i, i ^ 1) for i in range(groups)])  17.1 us
    pallas_call x1, Pallas kernels, gradients(): pl.pallas_call(functools.partial(gradients_kernel, parts // 2), in_specs=...  15.9 us
    all_to_all x1, starting transfers between devices, body(): rows = lax.all_to_all(rows, 'expert', 0, 0, tiled=True)  13.6 us
    all_to_all x1, waiting for transfers between devices, body(): rows = lax.all_to_all(rows, 'expert', 0, 0, tiled=True)  9.78 us
    pallas_call x1, Pallas kernels, pack_rows(): pl.pallas_call(functools.partial(pack_kernel, cap), in_specs=[pl.BlockSpe...  3.68 us
  transfers between devices with their start and end apart: 17, of which 8 were waited for; matrix products, arithmetic and copies ran while one was open for 0% of the time, Pallas kernels for 0%

profile of v4, /device:TPU:6, one launch (start us, length us, event | category | flops | bytes accessed | tf_op | source)
XLA Modules:
  0.0 160.6 jit_solution(4700117349486869501)
XLA Ops:
  0.6 3.7 %pack_rows.1 = bf16[32,32,2048]{2,1,0:T(8,128)(2,1)} custom-call(s32[8,128]{1,0:T(8,128)} %bitcast.22, f32[8,128]{1,0:T(8,128)} %bitcast.23, bf16[128,2048]{1,0:T(8,128)(2,1)} %tok_hbm.1, bf16[128,2048]{1,0:T(8,128)(2,1)} %cot_hbm.1), custom_call_target="tpu_custom_call" | custom-call | flops 536870912 | bytes 5242880 | tf_op jit(solution)/shard_map/pack_rows/pallas_call | solution.py:95
  4.3 13.6 %all-to-all-start = ((bf16[32,32,2048]{2,1,0:T(8,128)(2,1)}), bf16[32,32,2048]{2,1,0:T(8,128)(2,1)}, u32[]{:S(2)}, u32[]{:S(2)}) async-start(bf16[32,32,2048]{2,1,0:T(8,128)(2,1)} %pack_rows.1), calls=%async_computation | async-start | bytes 8388608 | tf_op jit(solution)/shard_map/all_to_all | solution.py:374
  18.1 3.5 %collective-permute-start = (bf16[128,3072]{1,0:T(8,128)(2,1)S(1)}, bf16[128,3072]{1,0:T(8,128)(2,1)S(1)}, u32[]{:S(2)}, u32[]{:S(2)}) collective-permute-start(bf16[128,3072]{1,0:T(8,128)(2,1)S(1)} %slice_dynamic-update-slice_fusion.refs_0_), channel_id=1, source_target_pairs={{0,64},{32,96},{64,128},{96,160},{128,192},{160,224},{192,256},{22... | collective-permute-start | bytes 2359304 | tf_op jit(solution)/shard_map/ppermute | solution.py:134
  21.6 3.8 %collective-permute-start.1 = (bf16[128,3072]{1,0:T(8,128)(2,1)S(1)}, bf16[128,3072]{1,0:T(8,128)(2,1)S(1)}, u32[]{:S(2)}, u32[]{:S(2)}) collective-permute-start(bf16[128,3072]{1,0:T(8,128)(2,1)S(1)} %slice_dynamic-update-slice_fusion.refs_0_), channel_id=1, source_target_pairs={{0,448},{32,480},{64,0},{96,32},{128,64},{160,96},{192,128},{224,1... | collective-permute-start | bytes 2359304 | tf_op jit(solution)/shard_map/ppermute | solution.py:134
  25.4 15.0 %collective-permute-done.refs_1_ = bf16[128,3072]{1,0:T(8,128)(2,1)S(1)} collective-permute-done((bf16[128,3072]{1,0:T(8,128)(2,1)S(1)}, bf16[128,3072]{1,0:T(8,128)(2,1)S(1)}, u32[]{:S(2)}, u32[]{:S(2)}) %collective-permute-start) | collective-permute-done | bytes 786464 | tf_op jit(solution)/shard_map/ppermute | solution.py:134
  42.4 5.1 %collective-permute-start.3 = (bf16[128,3072]{1,0:T(8,128)(2,1)S(1)}, bf16[128,3072]{1,0:T(8,128)(2,1)}, u32[]{:S(2)}, u32[]{:S(2)}) collective-permute-start(bf16[128,3072]{1,0:T(8,128)(2,1)S(1)} %collective-permute-done.1.refs_2_), channel_id=1, source_target_pairs={{0,448},{32,480},{64,0},{96,32},{128,64},{160,96},{192,128},{224,1... | collective-permute-start | bytes 2359304 | tf_op jit(solution)/shard_map/ppermute | solution.py:134
  47.5 14.3 %collective-permute-done.2.refs_3_ = bf16[128,3072]{1,0:T(8,128)(2,1)} collective-permute-done((bf16[128,3072]{1,0:T(8,128)(2,1)S(1)}, bf16[128,3072]{1,0:T(8,128)(2,1)}, u32[]{:S(2)}, u32[]{:S(2)}) %collective-permute-start.2) | collective-permute-done | bytes 786464 | tf_op jit(solution)/shard_map/ppermute | solution.py:134
  63.8 5.1 %collective-permute-start.5 = (bf16[128,3072]{1,0:T(8,128)(2,1)}, bf16[128,3072]{1,0:T(8,128)(2,1)S(1)}, u32[]{:S(2)}, u32[]{:S(2)}) collective-permute-start(bf16[128,3072]{1,0:T(8,128)(2,1)} %collective-permute-done.3.refs_4_), channel_id=1, source_target_pairs={{0,448},{32,480},{64,0},{96,32},{128,64},{160,96},{192,128},{224,1... | collective-permute-start | bytes 2359304 | tf_op jit(solution)/shard_map/ppermute | solution.py:134
  68.9 1.9 %collective-permute-start.7 = (bf16[128,3072]{1,0:T(8,128)(2,1)S(1)}, bf16[128,3072]{1,0:T(8,128)(2,1)}, u32[]{:S(2)}, u32[]{:S(2)}) collective-permute-start(bf16[128,3072]{1,0:T(8,128)(2,1)S(1)} %slice_dynamic-update-slice_fusion.refs_0_), channel_id=1, source_target_pairs={{0,32},{32,0},{64,96},{96,64},{128,160},{160,128},{192,224},{224,1... | collective-permute-start | bytes 2359304 | tf_op jit(solution)/shard_map/ppermute | solution.py:133
  70.9 2.5 %collective-permute-start.8 = (bf16[128,3072]{1,0:T(8,128)(2,1)}, bf16[128,3072]{1,0:T(8,128)(2,1)S(1)}, u32[]{:S(2)}, u32[]{:S(2)}) collective-permute-start(bf16[128,3072]{1,0:T(8,128)(2,1)} %copy-done.9), channel_id=1, source_target_pairs={{0,32},{32,0},{64,96},{96,64},{128,160},{160,128},{192,224},{224,1... | collective-permute-start | bytes 2359304 | tf_op jit(solution)/shard_map/ppermute | solution.py:133
  75.4 7.0 %collective-permute-done.4.refs_5_ = bf16[128,3072]{1,0:T(8,128)(2,1)S(1)} collective-permute-done((bf16[128,3072]{1,0:T(8,128)(2,1)}, bf16[128,3072]{1,0:T(8,128)(2,1)S(1)}, u32[]{:S(2)}, u32[]{:S(2)}) %collective-permute-start.4) | collective-permute-done | bytes 786464 | tf_op jit(solution)/shard_map/ppermute | solution.py:134
  83.8 2.8 %collective-permute-start.6 = (bf16[128,3072]{1,0:T(8,128)(2,1)S(1)}, bf16[128,3072]{1,0:T(8,128)(2,1)}, u32[]{:S(2)}, u32[]{:S(2)}) collective-permute-start(bf16[128,3072]{1,0:T(8,128)(2,1)S(1)} %broadcast_select_fusion), channel_id=1, source_target_pairs={{0,64},{32,480},{64,128},{96,32},{128,192},{160,96},{192,256},{224... | collective-permute-start | bytes 2359304 | tf_op jit(solution)/shard_map/ppermute | solution.py:134
  86.6 1.9 %collective-permute-start.10 = (bf16[128,3072]{1,0:T(8,128)(2,1)}, bf16[128,3072]{1,0:T(8,128)(2,1)}, u32[]{:S(2)}, u32[]{:S(2)}) collective-permute-start(bf16[128,3072]{1,0:T(8,128)(2,1)} %collective-permute-done.2.refs_3_), channel_id=1, source_target_pairs={{0,32},{32,0},{64,96},{96,64},{128,160},{160,128},{192,224},{224,1... | collective-permute-start | bytes 2359304 | tf_op jit(solution)/shard_map/ppermute | solution.py:133
  88.6 2.4 %collective-permute-start.11 = (bf16[128,3072]{1,0:T(8,128)(2,1)}, bf16[128,3072]{1,0:T(8,128)(2,1)}, u32[]{:S(2)}, u32[]{:S(2)}) collective-permute-start(bf16[128,3072]{1,0:T(8,128)(2,1)} %collective-permute-done.3.refs_4_), channel_id=1, source_target_pairs={{0,32},{32,0},{64,96},{96,64},{128,160},{160,128},{192,224},{224,1... | collective-permute-start | bytes 2359304 | tf_op jit(solution)/shard_map/ppermute | solution.py:133
  91.0 1.9 %collective-permute-start.12 = (bf16[128,3072]{1,0:T(8,128)(2,1)S(1)}, bf16[128,3072]{1,0:T(8,128)(2,1)}, u32[]{:S(2)}, u32[]{:S(2)}) collective-permute-start(bf16[128,3072]{1,0:T(8,128)(2,1)S(1)} %collective-permute-done.4.refs_5_), channel_id=1, source_target_pairs={{0,32},{32,0},{64,96},{96,64},{128,160},{160,128},{192,224},{224,1... | collective-permute-start | bytes 2359304 | tf_op jit(solution)/shard_map/ppermute | solution.py:133
  93.0 2.4 %collective-permute-start.13 = (bf16[128,3072]{1,0:T(8,128)(2,1)S(1)}, bf16[128,3072]{1,0:T(8,128)(2,1)}, u32[]{:S(2)}, u32[]{:S(2)}) collective-permute-start(bf16[128,3072]{1,0:T(8,128)(2,1)S(1)} %collective-permute-done.5.refs_6_), channel_id=1, source_target_pairs={{0,32},{32,0},{64,96},{96,64},{128,160},{160,128},{192,224},{224,1... | collective-permute-start | bytes 2359304 | tf_op jit(solution)/shard_map/ppermute | solution.py:133
  95.4 4.0 %collective-permute-done.6.refs_7_ = bf16[128,3072]{1,0:T(8,128)(2,1)} collective-permute-done((bf16[128,3072]{1,0:T(8,128)(2,1)S(1)}, bf16[128,3072]{1,0:T(8,128)(2,1)}, u32[]{:S(2)}, u32[]{:S(2)}) %collective-permute-start.6) | collective-permute-done | bytes 786464 | tf_op jit(solution)/shard_map/ppermute | solution.py:134
  99.4 2.1 %collective-permute-start.14 = (bf16[128,3072]{1,0:T(8,128)(2,1)}, bf16[128,3072]{1,0:T(8,128)(2,1)}, u32[]{:S(2)}, u32[]{:S(2)}) collective-permute-start(bf16[128,3072]{1,0:T(8,128)(2,1)} %collective-permute-done.6.refs_7_), channel_id=1, source_target_pairs={{0,32},{32,0},{64,96},{96,64},{128,160},{160,128},{192,224},{224,1... | collective-permute-start | bytes 2359304 | tf_op jit(solution)/shard_map/ppermute | solution.py:133
  101.6 2.3 %collective-permute-done.14.refs_15_ = bf16[128,3072]{1,0:T(8,128)(2,1)} collective-permute-done((bf16[128,3072]{1,0:T(8,128)(2,1)}, bf16[128,3072]{1,0:T(8,128)(2,1)}, u32[]{:S(2)}, u32[]{:S(2)}) %collective-permute-start.14) | collective-permute-done | bytes 786464 | tf_op jit(solution)/shard_map/ppermute | solution.py:133
  103.9 9.8 %all-to-all-done.rows_hbm = bf16[32,32,2048]{2,1,0:T(8,128)(2,1)} async-done(((bf16[32,32,2048]{2,1,0:T(8,128)(2,1)}), bf16[32,32,2048]{2,1,0:T(8,128)(2,1)}, u32[]{:S(2)}, u32[]{:S(2)}) %all-to-all-start) | async-done | bytes 4194336 | tf_op jit(solution)/shard_map/all_to_all | solution.py:374
  113.7 15.9 %gradients.1 = (bf16[8,288,128]{2,1,0:T(8,128)(2,1)S(1)}, bf16[8,288,128]{2,1,0:T(8,128)(2,1)S(1)}) custom-call(s32[2]{0:T(128)S(1)} %pad_add_fusion.place_ref, bf16[32,32,2048]{2,1,0:T(8,128)(2,1)} %all-to-all-done.rows_hbm, bf16[2048,128]{1,0:T(8,128)(2,1)S(1)} %bitcast.12, bf16[64,2048]{1,0:T(8,128)(2,1)S(1)} %bitcast.13, bf16[64,1024]{1,0:T(8,128)(2,1)S(1)} %bitcast.15, ...), custom_call_target="tpu_custom_call" | custom-call | flops 7247757312 | bytes 16777216 | tf_op jit(solution)/shard_map/gradients/pallas_call | solution.py:286
  129.6 1.9 %collective-permute-start.15 = (bf16[8,288,128]{2,1,0:T(8,128)(2,1)S(1)}, bf16[8,288,128]{2,1,0:T(8,128)(2,1)S(1)}, u32[]{:S(2)}, u32[]{:S(2)}) collective-permute-start(bf16[8,288,128]{2,1,0:T(8,128)(2,1)S(1)} %get-tuple-element.7), channel_id=1, source_target_pairs={{0,32},{32,0},{64,96},{96,64},{128,160},{160,128},{192,224},{224,1... | collective-permute-start | bytes 1769480 | tf_op jit(solution)/shard_map/ppermute | solution.py:387
  131.6 2.0 %collective-permute-done.15 = bf16[8,288,128]{2,1,0:T(8,128)(2,1)S(1)} collective-permute-done((bf16[8,288,128]{2,1,0:T(8,128)(2,1)S(1)}, bf16[8,288,128]{2,1,0:T(8,128)(2,1)S(1)}, u32[]{:S(2)}, u32[]{:S(2)}) %collective-permute-start.15) | collective-permute-done | bytes 589856 | tf_op jit(solution)/shard_map/ppermute | solution.py:387
  133.7 26.1 %all_to_all.10.parts_ref = bf16[8,288,128]{2,1,0:T(8,128)(2,1)S(1)} all-to-all(bf16[8,288,128]{2,1,0:T(8,128)(2,1)S(1)} %add_convert_fusion), channel_id=1, replica_groups={{0,64,128,192,256,320,384,448},{32,96,160,224,288,352,416,480},{1,65,12..., dimensions={0} | all-to-all | bytes 1179648 | tf_op jit(solution)/shard_map/all_to_all | solution.py:390
  (49 shorter events, 8.3 us)
Async XLA Ops:
  4.3 109.4 %all-to-all-start = ((bf16[32,32,2048]{2,1,0:T(8,128)(2,1)}), bf16[32,32,2048]{2,1,0:T(8,128)(2,1)}, u32[]{:S(2)}, u32[]{:S(2)}) async-start(bf16[32,32,2048]{2,1,0:T(8,128)(2,1)} %pack_rows.1), calls=%async_computation | async-start | bytes 8388608 | tf_op jit(solution)/shard_map/all_to_all | solution.py:374
  18.1 65.7 %copy-start.8 = (bf16[128,3072]{1,0:T(8,128)(2,1)}, bf16[128,3072]{1,0:T(8,128)(2,1)S(1)}, u32[]{:S(2)}) copy-start(bf16[128,3072]{1,0:T(8,128)(2,1)S(1)} %slice_dynamic-update-slice_fusion.refs_0_) | copy-start | bytes 2359300
  18.1 22.4 %collective-permute-start = (bf16[128,3072]{1,0:T(8,128)(2,1)S(1)}, bf16[128,3072]{1,0:T(8,128)(2,1)S(1)}, u32[]{:S(2)}, u32[]{:S(2)}) collective-permute-start(bf16[128,3072]{1,0:T(8,128)(2,1)S(1)} %slice_dynamic-update-slice_fusion.refs_0_), channel_id=1, source_target_pairs={{0,64},{32,96},{64,128},{96,160},{128,192},{160,224},{192,256},{22... | collective-permute-start | bytes 2359304 | tf_op jit(solution)/shard_map/ppermute | solution.py:134
  21.6 20.8 %collective-permute-start.1 = (bf16[128,3072]{1,0:T(8,128)(2,1)S(1)}, bf16[128,3072]{1,0:T(8,128)(2,1)S(1)}, u32[]{:S(2)}, u32[]{:S(2)}) collective-permute-start(bf16[128,3072]{1,0:T(8,128)(2,1)S(1)} %slice_dynamic-update-slice_fusion.refs_0_), channel_id=1, source_target_pairs={{0,448},{32,480},{64,0},{96,32},{128,64},{160,96},{192,128},{224,1... | collective-permute-start | bytes 2359304 | tf_op jit(solution)/shard_map/ppermute | solution.py:134
  40.5 23.3 %copy-start.9 = (bf16[128,3072]{1,0:T(8,128)(2,1)}, bf16[128,3072]{1,0:T(8,128)(2,1)S(1)}, u32[]{:S(2)}) copy-start(bf16[128,3072]{1,0:T(8,128)(2,1)S(1)} %collective-permute-done.refs_1_) | copy-start | bytes 2359300
  40.5 21.4 %collective-permute-start.2 = (bf16[128,3072]{1,0:T(8,128)(2,1)S(1)}, bf16[128,3072]{1,0:T(8,128)(2,1)}, u32[]{:S(2)}, u32[]{:S(2)}) collective-permute-start(bf16[128,3072]{1,0:T(8,128)(2,1)S(1)} %collective-permute-done.refs_1_), channel_id=1, source_target_pairs={{0,64},{32,96},{64,128},{96,160},{128,192},{160,224},{192,256},{22... | collective-permute-start | bytes 2359304 | tf_op jit(solution)/shard_map/ppermute | solution.py:134
  42.4 21.4 %copy-start.10 = (bf16[128,3072]{1,0:T(8,128)(2,1)}, bf16[128,3072]{1,0:T(8,128)(2,1)S(1)}, u32[]{:S(2)}) copy-start(bf16[128,3072]{1,0:T(8,128)(2,1)S(1)} %collective-permute-done.1.refs_2_) | copy-start | bytes 2359300
  42.4 21.4 %collective-permute-start.3 = (bf16[128,3072]{1,0:T(8,128)(2,1)S(1)}, bf16[128,3072]{1,0:T(8,128)(2,1)}, u32[]{:S(2)}, u32[]{:S(2)}) collective-permute-start(bf16[128,3072]{1,0:T(8,128)(2,1)S(1)} %collective-permute-done.1.refs_2_), channel_id=1, source_target_pairs={{0,448},{32,480},{64,0},{96,32},{128,64},{160,96},{192,128},{224,1... | collective-permute-start | bytes 2359304 | tf_op jit(solution)/shard_map/ppermute | solution.py:134
  61.8 20.6 %collective-permute-start.4 = (bf16[128,3072]{1,0:T(8,128)(2,1)}, bf16[128,3072]{1,0:T(8,128)(2,1)S(1)}, u32[]{:S(2)}, u32[]{:S(2)}) collective-permute-start(bf16[128,3072]{1,0:T(8,128)(2,1)} %collective-permute-done.2.refs_3_), channel_id=1, source_target_pairs={{0,64},{32,96},{64,128},{96,160},{128,192},{160,224},{192,256},{22... | collective-permute-start | bytes 2359304 | tf_op jit(solution)/shard_map/ppermute | solution.py:134
  63.8 19.9 %collective-permute-start.5 = (bf16[128,3072]{1,0:T(8,128)(2,1)}, bf16[128,3072]{1,0:T(8,128)(2,1)S(1)}, u32[]{:S(2)}, u32[]{:S(2)}) collective-permute-start(bf16[128,3072]{1,0:T(8,128)(2,1)} %collective-permute-done.3.refs_4_), channel_id=1, source_target_pairs={{0,448},{32,480},{64,0},{96,32},{128,64},{160,96},{192,128},{224,1... | collective-permute-start | bytes 2359304 | tf_op jit(solution)/shard_map/ppermute | solution.py:134
  68.9 19.6 %collective-permute-start.7 = (bf16[128,3072]{1,0:T(8,128)(2,1)S(1)}, bf16[128,3072]{1,0:T(8,128)(2,1)}, u32[]{:S(2)}, u32[]{:S(2)}) collective-permute-start(bf16[128,3072]{1,0:T(8,128)(2,1)S(1)} %slice_dynamic-update-slice_fusion.refs_0_), channel_id=1, source_target_pairs={{0,32},{32,0},{64,96},{96,64},{128,160},{160,128},{192,224},{224,1... | collective-permute-start | bytes 2359304 | tf_op jit(solution)/shard_map/ppermute | solution.py:133
  70.9 42.8 %copy-start = (bf16[1,2048,128]{2,1,0:T(8,128)(2,1)S(1)}, bf16[1,2048,128]{2,1,0:T(8,128)(2,1)}, u32[]{:S(2)}) copy-start(bf16[1,2048,128]{2,1,0:T(8,128)(2,1)} %param.16) | copy-start | bytes 1572868
  70.9 42.8 %copy-start.1 = (bf16[1,64,2048]{2,1,0:T(8,128)(2,1)S(1)}, bf16[1,64,2048]{2,1,0:T(8,128)(2,1)}, u32[]{:S(2)}) copy-start(bf16[1,64,2048]{2,1,0:T(8,128)(2,1)} %param.19) | copy-start | bytes 786436
  70.9 42.8 %copy-start.2 = (bf16[1,128,1024]{2,1,0:T(8,128)(2,1)S(1)}, bf16[1,128,1024]{2,1,0:T(8,128)(2,1)}, u32[]{:S(2)}) copy-start(bf16[1,128,1024]{2,1,0:T(8,128)(2,1)} %param.17) | copy-start | bytes 786436
  70.9 42.8 %copy-start.3 = (bf16[1,1024,64]{1,2,0:T(8,128)(2,1)S(1)}, bf16[1,1024,64]{1,2,0:T(8,128)(2,1)}, u32[]{:S(2)}) copy-start(bf16[1,1024,64]{1,2,0:T(8,128)(2,1)} %param.18) | copy-start | bytes 393220
  70.9 20.1 %collective-permute-start.8 = (bf16[128,3072]{1,0:T(8,128)(2,1)}, bf16[128,3072]{1,0:T(8,128)(2,1)S(1)}, u32[]{:S(2)}, u32[]{:S(2)}) collective-permute-start(bf16[128,3072]{1,0:T(8,128)(2,1)} %copy-done.9), channel_id=1, source_target_pairs={{0,32},{32,0},{64,96},{96,64},{128,160},{160,128},{192,224},{224,1... | collective-permute-start | bytes 2359304 | tf_op jit(solution)/shard_map/ppermute | solution.py:133
  73.5 19.5 %collective-permute-start.9 = (bf16[128,3072]{1,0:T(8,128)(2,1)}, bf16[128,3072]{1,0:T(8,128)(2,1)S(1)}, u32[]{:S(2)}, u32[]{:S(2)}) collective-permute-start(bf16[128,3072]{1,0:T(8,128)(2,1)} %copy-done.10), channel_id=1, source_target_pairs={{0,32},{32,0},{64,96},{96,64},{128,160},{160,128},{192,224},{224,1... | collective-permute-start | bytes 2359304 | tf_op jit(solution)/shard_map/ppermute | solution.py:133
  83.8 15.6 %collective-permute-start.6 = (bf16[128,3072]{1,0:T(8,128)(2,1)S(1)}, bf16[128,3072]{1,0:T(8,128)(2,1)}, u32[]{:S(2)}, u32[]{:S(2)}) collective-permute-start(bf16[128,3072]{1,0:T(8,128)(2,1)S(1)} %broadcast_select_fusion), channel_id=1, source_target_pairs={{0,64},{32,480},{64,128},{96,32},{128,192},{160,96},{192,256},{224... | collective-permute-start | bytes 2359304 | tf_op jit(solution)/shard_map/ppermute | solution.py:134
  86.6 15.0 %collective-permute-start.10 = (bf16[128,3072]{1,0:T(8,128)(2,1)}, bf16[128,3072]{1,0:T(8,128)(2,1)}, u32[]{:S(2)}, u32[]{:S(2)}) collective-permute-start(bf16[128,3072]{1,0:T(8,128)(2,1)} %collective-permute-done.2.refs_3_), channel_id=1, source_target_pairs={{0,32},{32,0},{64,96},{96,64},{128,160},{160,128},{192,224},{224,1... | collective-permute-start | bytes 2359304 | tf_op jit(solution)/shard_map/ppermute | solution.py:133
  88.6 13.0 %collective-permute-start.11 = (bf16[128,3072]{1,0:T(8,128)(2,1)}, bf16[128,3072]{1,0:T(8,128)(2,1)}, u32[]{:S(2)}, u32[]{:S(2)}) collective-permute-start(bf16[128,3072]{1,0:T(8,128)(2,1)} %collective-permute-done.3.refs_4_), channel_id=1, source_target_pairs={{0,32},{32,0},{64,96},{96,64},{128,160},{160,128},{192,224},{224,1... | collective-permute-start | bytes 2359304 | tf_op jit(solution)/shard_map/ppermute | solution.py:133
  91.0 10.6 %collective-permute-start.12 = (bf16[128,3072]{1,0:T(8,128)(2,1)S(1)}, bf16[128,3072]{1,0:T(8,128)(2,1)}, u32[]{:S(2)}, u32[]{:S(2)}) collective-permute-start(bf16[128,3072]{1,0:T(8,128)(2,1)S(1)} %collective-permute-done.4.refs_5_), channel_id=1, source_target_pairs={{0,32},{32,0},{64,96},{96,64},{128,160},{160,128},{192,224},{224,1... | collective-permute-start | bytes 2359304 | tf_op jit(solution)/shard_map/ppermute | solution.py:133
  93.0 8.6 %collective-permute-start.13 = (bf16[128,3072]{1,0:T(8,128)(2,1)S(1)}, bf16[128,3072]{1,0:T(8,128)(2,1)}, u32[]{:S(2)}, u32[]{:S(2)}) collective-permute-start(bf16[128,3072]{1,0:T(8,128)(2,1)S(1)} %collective-permute-done.5.refs_6_), channel_id=1, source_target_pairs={{0,32},{32,0},{64,96},{96,64},{128,160},{160,128},{192,224},{224,1... | collective-permute-start | bytes 2359304 | tf_op jit(solution)/shard_map/ppermute | solution.py:133
  99.4 4.5 %collective-permute-start.14 = (bf16[128,3072]{1,0:T(8,128)(2,1)}, bf16[128,3072]{1,0:T(8,128)(2,1)}, u32[]{:S(2)}, u32[]{:S(2)}) collective-permute-start(bf16[128,3072]{1,0:T(8,128)(2,1)} %collective-permute-done.6.refs_7_), channel_id=1, source_target_pairs={{0,32},{32,0},{64,96},{96,64},{128,160},{160,128},{192,224},{224,1... | collective-permute-start | bytes 2359304 | tf_op jit(solution)/shard_map/ppermute | solution.py:133
  129.6 3.9 %collective-permute-start.15 = (bf16[8,288,128]{2,1,0:T(8,128)(2,1)S(1)}, bf16[8,288,128]{2,1,0:T(8,128)(2,1)S(1)}, u32[]{:S(2)}, u32[]{:S(2)}) collective-permute-start(bf16[8,288,128]{2,1,0:T(8,128)(2,1)S(1)} %get-tuple-element.7), channel_id=1, source_target_pairs={{0,32},{32,0},{64,96},{96,64},{128,160},{160,128},{192,224},{224,1... | collective-permute-start | bytes 1769480 | tf_op jit(solution)/shard_map/ppermute | solution.py:387
  (6 other events, 59.9 us)

commit v5 on v4

--- a/solution.py
+++ b/solution.py
@@ -154,19 +154,56 @@
     ]
 
 
+def first_kernel(chips, place_ref, win_ref, *refs):
+    pieces, (out_ref, sems) = refs[: 2 * chips], refs[2 * chips :]
+    firsts = piece_rows(chips, pieces[0].shape[0], place_ref[0], place_ref[1])
+    copies = []
+    for i, (piece, row) in enumerate(zip(pieces, firsts)):
+        rows = pl.ds(row, piece.shape[0])
+        copies.append(
+            pltpu.make_async_copy(piece.at[:, pl.ds(0, BLOCK)], out_ref.at[rows, :], sems.at[i])
+        )
+        copies[-1].start()
+    rank = win_ref.shape[0] // 2
+    depth = out_ref.shape[0] - 2 * rank
+    win = (0.5 * win_ref[:rank, :BLOCK].astype(F32)).astype(BF16)
+    out_ref[depth:, :] = jnp.concatenate([win, jnp.zeros_like(win)], axis=0)
+    for copy in copies:
+        copy.wait()
+
+
+def first_block(place, pieces, win):
+    whole = pl.BlockSpec(memory_space=pltpu.VMEM)
+    rows = len(pieces) * pieces[0].shape[0] + win.shape[0]
+    return pl.pallas_call(
+        functools.partial(first_kernel, len(pieces) // 2),
+        in_specs=[pl.BlockSpec(memory_space=pltpu.SMEM), whole]
+        + [pl.BlockSpec(memory_space=pl.ANY)] * len(pieces),
+        out_shape=pltpu.VMEM((rows, BLOCK), BF16),
+        out_specs=whole,
+        scratch_shapes=[pltpu.SemaphoreType.DMA((len(pieces),))],
+        cost_estimate=pl.CostEstimate(
+            flops=0, bytes_accessed=4 * rows * BLOCK, transcendentals=0
+        ),
+        compiler_params=pltpu.CompilerParams(vmem_limit_bytes=8 * 2**20),
+        name="first_block",
+    )(place, *in_vmem(win), *in_hbm(*pieces))
+
+
 def gradients_kernel(
     chips,
     place_ref,
     rows_hbm,
+    dw_hbm,
     narrow_s,
-    dw_s,
     dnt_s,
     win_s,
+    first_ref,
     *refs,
 ):
     pieces, refs = refs[: 2 * chips], refs[2 * chips :]
-    keep_ref, send_ref, x_rows, y_rows, x_s, y_s, w_s = refs[:7]
-    hid_s, dgate_s, dup_s, inb_s, dna_s, dnb_s, ina_s, sems = refs[7:]
+    keep_ref, send_ref, x_rows, y_rows, x_s, y_s, dw_s, w_s = refs[:8]
+    hid_s, dgate_s, dup_s, inb_s, dna_s, dnb_s, ina_s, sems = refs[8:]
     slots = x_rows.shape[0]
     cap, width = x_s.shape[1:]
     rank, units = dnt_s.shape
@@ -194,9 +231,8 @@
         return w_s[:, i * BLOCK : (i + 1) * BLOCK]
 
     x_in = [fetch(rows_hbm.at[:, pl.ds(0, cap), :], x_s)]
-    y_in = [fetch(rows_hbm.at[:, pl.ds(cap, cap), :], y_s)]
-    y_in += fetch_blocks(0, 1)
-    u_in = fetch_blocks(1, 3)
+    y_in = [fetch(rows_hbm.at[:, pl.ds(cap, cap), :], y_s), fetch(dw_hbm, dw_s)]
+    y_in += fetch_blocks(1, 3)
     wait(x_in)
     zero = jnp.zeros((rank, BLOCK), BF16)
     for step in range(steps):
@@ -211,6 +247,7 @@
     low = dot_nn(x_rows[:, :width], narrow_s[...])
     low_t = low.T.astype(BF16)
     x_rows[:, width:] = low.astype(BF16)
+    vals = [dot_nn(x_rows[...], first_ref[...])]
     rest = fetch_blocks(3, 6)
     wait(y_in)
     y_rows[:, :width] = y_s[...].reshape(slots, width)
@@ -218,8 +255,6 @@
     z_t = z.T.astype(BF16)
     z = z.astype(BF16)
     y_rows[:, width:] = jnp.concatenate([z, jnp.zeros_like(z)], axis=1)
-    vals = [dot_nn(x_rows[...], block(0))]
-    wait(u_in)
     vals += [dot_nn(x_rows[...], block(1)), dot_nn(y_rows[...], block(2))]
     wait(rest)
     for i in range(3, 6):
@@ -283,10 +318,11 @@
     acts = pltpu.VMEM((sources, cap, width), BF16)
     deep = pltpu.VMEM((slots, width + 2 * rank), BF16)
     hidden = pltpu.VMEM((slots, units), BF16)
+    first = first_block(place, pieces, win)
     return pl.pallas_call(
         functools.partial(gradients_kernel, parts // 2),
         in_specs=[pl.BlockSpec(memory_space=pltpu.SMEM)]
-        + [pl.BlockSpec(memory_space=pl.ANY)]
+        + [pl.BlockSpec(memory_space=pl.ANY)] * 2
         + [pl.BlockSpec(memory_space=pltpu.VMEM)] * 4
         + [pl.BlockSpec(memory_space=pl.ANY)] * len(pieces),
         out_shape=(out, out),
@@ -296,6 +332,7 @@
             deep,
             acts,
             acts,
+            pltpu.VMEM(dw.shape, BF16),
             pltpu.VMEM((width + 2 * rank, 3 * units), BF16),
             hidden,
             hidden,
@@ -313,7 +350,7 @@
         ),
         compiler_params=pltpu.CompilerParams(vmem_limit_bytes=VMEM),
         name="gradients",
-    )(place, *in_hbm(rows), *in_vmem(narrow, dw, dnt, win), *in_hbm(*pieces))
+    )(place, *in_hbm(rows, dw), *in_vmem(narrow, dnt, win, first), *in_hbm(*pieces))
 
 
 def finish_kernel(factor, parts_ref, ina_ref, inb_ref, dna_ref, dnb_ref):

time: 161 us -> 161 us (level)
  waiting for transfers between devices: 55.8 us -> 52.7 us
  Pallas kernels: 20.4 us -> 22.4 us
    all_to_all x1, waiting for transfers between devices: 9.78 us -> 7.4 us  [body(): rows = lax.all_to_all(rows, 'expert', 0, 0, tiled=True)]
    pallas_call x0 -> x1, Pallas kernels: none -> 2.32 us  [first_block(): pl.pallas_call(functools.partial(first_kernel, len(pieces) // 2), in_spec...]
  transfers between devices with their start and end apart: 17 -> 17, of which waited for: 8 -> 8; matrix products, arithmetic and copies ran while one was open for 0% -> 0% of each run, Pallas kernels for 0% -> 1%
where the time goes in v5:
time: 161 us; the launch traced here: 160 us
  starting transfers between devices  56.7 us (35%)
  waiting for transfers between devices  52.7 us (33%)
  blocking collectives  26.1 us (16%)
  Pallas kernels  22.4 us (14%)
    ppermute x7, waiting for transfers between devices, gather_weights(): lax.ppermute(a, 'dp', [(i, (i + 2 * way(i)) % groups) for i in range(grou...  41 us
    all_to_all x1, blocking collectives, body(): lax.all_to_all(pair, 'dp', 0, 0, tiled=True, axis_index_groups=lines)  26.1 us
    ppermute x7, starting transfers between devices, gather_weights(): lax.ppermute(a, 'dp', [(i, (i + 2 * way(i)) % groups) for i in range(grou...  24.2 us
    ppermute x8, starting transfers between devices, gather_weights(): swap = lambda a: lax.ppermute(a, 'dp', [(i, i ^ 1) for i in range(groups)])  17 us
    pallas_call x1, Pallas kernels, gradients(): pl.pallas_call(functools.partial(gradients_kernel, parts // 2), in_specs=...  15.6 us
    all_to_all x1, starting transfers between devices, body(): rows = lax.all_to_all(rows, 'expert', 0, 0, tiled=True)  13.6 us
    all_to_all x1, waiting for transfers between devices, body(): rows = lax.all_to_all(rows, 'expert', 0, 0, tiled=True)  7.4 us
    pallas_call x1, Pallas kernels, pack_rows(): pl.pallas_call(functools.partial(pack_kernel, cap), in_specs=[pl.BlockSpe...  3.64 us
  transfers between devices with their start and end apart: 17, of which 8 were waited for; matrix products, arithmetic and copies ran while one was open for 0% of the time, Pallas kernels for 1%

profile of v5, /device:TPU:6, one launch (start us, length us, event | category | flops | bytes accessed | tf_op | source)
XLA Modules:
  0.0 160.2 jit_solution(4563608997365885944)
XLA Ops:
  0.6 3.6 %pack_rows.1 = bf16[32,32,2048]{2,1,0:T(8,128)(2,1)} custom-call(s32[8,128]{1,0:T(8,128)} %bitcast.22, f32[8,128]{1,0:T(8,128)} %bitcast.23, bf16[128,2048]{1,0:T(8,128)(2,1)} %tok_hbm.1, bf16[128,2048]{1,0:T(8,128)(2,1)} %cot_hbm.1), custom_call_target="tpu_custom_call" | custom-call | flops 536870912 | bytes 5242880 | tf_op jit(solution)/shard_map/pack_rows/pallas_call | solution.py:95
  4.3 13.6 %all-to-all-start = ((bf16[32,32,2048]{2,1,0:T(8,128)(2,1)}), bf16[32,32,2048]{2,1,0:T(8,128)(2,1)}, u32[]{:S(2)}, u32[]{:S(2)}) async-start(bf16[32,32,2048]{2,1,0:T(8,128)(2,1)} %pack_rows.1), calls=%async_computation | async-start | bytes 8388608 | tf_op jit(solution)/shard_map/all_to_all | solution.py:411
  18.1 3.5 %collective-permute-start = (bf16[128,3072]{1,0:T(8,128)(2,1)S(1)}, bf16[128,3072]{1,0:T(8,128)(2,1)S(1)}, u32[]{:S(2)}, u32[]{:S(2)}) collective-permute-start(bf16[128,3072]{1,0:T(8,128)(2,1)S(1)} %slice_dynamic-update-slice_fusion.refs_0_), channel_id=1, source_target_pairs={{0,64},{32,96},{64,128},{96,160},{128,192},{160,224},{192,256},{22... | collective-permute-start | bytes 2359304 | tf_op jit(solution)/shard_map/ppermute | solution.py:134
  21.6 3.8 %collective-permute-start.1 = (bf16[128,3072]{1,0:T(8,128)(2,1)S(1)}, bf16[128,3072]{1,0:T(8,128)(2,1)S(1)}, u32[]{:S(2)}, u32[]{:S(2)}) collective-permute-start(bf16[128,3072]{1,0:T(8,128)(2,1)S(1)} %slice_dynamic-update-slice_fusion.refs_0_), channel_id=1, source_target_pairs={{0,448},{32,480},{64,0},{96,32},{128,64},{160,96},{192,128},{224,1... | collective-permute-start | bytes 2359304 | tf_op jit(solution)/shard_map/ppermute | solution.py:134
  25.4 15.0 %collective-permute-done.refs_1_ = bf16[128,3072]{1,0:T(8,128)(2,1)S(1)} collective-permute-done((bf16[128,3072]{1,0:T(8,128)(2,1)S(1)}, bf16[128,3072]{1,0:T(8,128)(2,1)S(1)}, u32[]{:S(2)}, u32[]{:S(2)}) %collective-permute-start) | collective-permute-done | bytes 786464 | tf_op jit(solution)/shard_map/ppermute | solution.py:134
  42.4 5.1 %collective-permute-start.3 = (bf16[128,3072]{1,0:T(8,128)(2,1)S(1)}, bf16[128,3072]{1,0:T(8,128)(2,1)}, u32[]{:S(2)}, u32[]{:S(2)}) collective-permute-start(bf16[128,3072]{1,0:T(8,128)(2,1)S(1)} %collective-permute-done.1.refs_2_), channel_id=1, source_target_pairs={{0,448},{32,480},{64,0},{96,32},{128,64},{160,96},{192,128},{224,1... | collective-permute-start | bytes 2359304 | tf_op jit(solution)/shard_map/ppermute | solution.py:134
  47.5 14.3 %collective-permute-done.2.refs_3_ = bf16[128,3072]{1,0:T(8,128)(2,1)} collective-permute-done((bf16[128,3072]{1,0:T(8,128)(2,1)S(1)}, bf16[128,3072]{1,0:T(8,128)(2,1)}, u32[]{:S(2)}, u32[]{:S(2)}) %collective-permute-start.2) | collective-permute-done | bytes 786464 | tf_op jit(solution)/shard_map/ppermute | solution.py:134
  63.8 5.1 %collective-permute-start.5 = (bf16[128,3072]{1,0:T(8,128)(2,1)}, bf16[128,3072]{1,0:T(8,128)(2,1)S(1)}, u32[]{:S(2)}, u32[]{:S(2)}) collective-permute-start(bf16[128,3072]{1,0:T(8,128)(2,1)} %collective-permute-done.3.refs_4_), channel_id=1, source_target_pairs={{0,448},{32,480},{64,0},{96,32},{128,64},{160,96},{192,128},{224,1... | collective-permute-start | bytes 2359304 | tf_op jit(solution)/shard_map/ppermute | solution.py:134
  68.9 1.9 %collective-permute-start.7 = (bf16[128,3072]{1,0:T(8,128)(2,1)S(1)}, bf16[128,3072]{1,0:T(8,128)(2,1)}, u32[]{:S(2)}, u32[]{:S(2)}) collective-permute-start(bf16[128,3072]{1,0:T(8,128)(2,1)S(1)} %slice_dynamic-update-slice_fusion.refs_0_), channel_id=1, source_target_pairs={{0,32},{32,0},{64,96},{96,64},{128,160},{160,128},{192,224},{224,1... | collective-permute-start | bytes 2359304 | tf_op jit(solution)/shard_map/ppermute | solution.py:133
  70.8 2.4 %collective-permute-start.8 = (bf16[128,3072]{1,0:T(8,128)(2,1)S(1)}, bf16[128,3072]{1,0:T(8,128)(2,1)S(1)}, u32[]{:S(2)}, u32[]{:S(2)}) collective-permute-start(bf16[128,3072]{1,0:T(8,128)(2,1)S(1)} %collective-permute-done.refs_1_), channel_id=1, source_target_pairs={{0,32},{32,0},{64,96},{96,64},{128,160},{160,128},{192,224},{224,1... | collective-permute-start | bytes 2359304 | tf_op jit(solution)/shard_map/ppermute | solution.py:133
  75.2 7.2 %collective-permute-done.4.refs_5_ = bf16[128,3072]{1,0:T(8,128)(2,1)S(1)} collective-permute-done((bf16[128,3072]{1,0:T(8,128)(2,1)}, bf16[128,3072]{1,0:T(8,128)(2,1)S(1)}, u32[]{:S(2)}, u32[]{:S(2)}) %collective-permute-start.4) | collective-permute-done | bytes 786464 | tf_op jit(solution)/shard_map/ppermute | solution.py:134
  83.8 2.8 %collective-permute-start.6 = (bf16[128,3072]{1,0:T(8,128)(2,1)S(1)}, bf16[128,3072]{1,0:T(8,128)(2,1)}, u32[]{:S(2)}, u32[]{:S(2)}) collective-permute-start(bf16[128,3072]{1,0:T(8,128)(2,1)S(1)} %broadcast_select_fusion), channel_id=1, source_target_pairs={{0,64},{32,480},{64,128},{96,32},{128,192},{160,96},{192,256},{224... | collective-permute-start | bytes 2359304 | tf_op jit(solution)/shard_map/ppermute | solution.py:134
  86.6 1.9 %collective-permute-start.10 = (bf16[128,3072]{1,0:T(8,128)(2,1)}, bf16[128,3072]{1,0:T(8,128)(2,1)}, u32[]{:S(2)}, u32[]{:S(2)}) collective-permute-start(bf16[128,3072]{1,0:T(8,128)(2,1)} %collective-permute-done.2.refs_3_), channel_id=1, source_target_pairs={{0,32},{32,0},{64,96},{96,64},{128,160},{160,128},{192,224},{224,1... | collective-permute-start | bytes 2359304 | tf_op jit(solution)/shard_map/ppermute | solution.py:133
  88.5 2.4 %collective-permute-start.11 = (bf16[128,3072]{1,0:T(8,128)(2,1)}, bf16[128,3072]{1,0:T(8,128)(2,1)}, u32[]{:S(2)}, u32[]{:S(2)}) collective-permute-start(bf16[128,3072]{1,0:T(8,128)(2,1)} %collective-permute-done.3.refs_4_), channel_id=1, source_target_pairs={{0,32},{32,0},{64,96},{96,64},{128,160},{160,128},{192,224},{224,1... | collective-permute-start | bytes 2359304 | tf_op jit(solution)/shard_map/ppermute | solution.py:133
  91.0 1.9 %collective-permute-start.12 = (bf16[128,3072]{1,0:T(8,128)(2,1)S(1)}, bf16[128,3072]{1,0:T(8,128)(2,1)}, u32[]{:S(2)}, u32[]{:S(2)}) collective-permute-start(bf16[128,3072]{1,0:T(8,128)(2,1)S(1)} %collective-permute-done.4.refs_5_), channel_id=1, source_target_pairs={{0,32},{32,0},{64,96},{96,64},{128,160},{160,128},{192,224},{224,1... | collective-permute-start | bytes 2359304 | tf_op jit(solution)/shard_map/ppermute | solution.py:133
  93.8 2.4 %collective-permute-start.13 = (bf16[128,3072]{1,0:T(8,128)(2,1)S(1)}, bf16[128,3072]{1,0:T(8,128)(2,1)}, u32[]{:S(2)}, u32[]{:S(2)}) collective-permute-start(bf16[128,3072]{1,0:T(8,128)(2,1)S(1)} %collective-permute-done.5.refs_6_), channel_id=1, source_target_pairs={{0,32},{32,0},{64,96},{96,64},{128,160},{160,128},{192,224},{224,1... | collective-permute-start | bytes 2359304 | tf_op jit(solution)/shard_map/ppermute | solution.py:133
  96.2 3.1 %collective-permute-done.6.refs_7_ = bf16[128,3072]{1,0:T(8,128)(2,1)} collective-permute-done((bf16[128,3072]{1,0:T(8,128)(2,1)S(1)}, bf16[128,3072]{1,0:T(8,128)(2,1)}, u32[]{:S(2)}, u32[]{:S(2)}) %collective-permute-start.6) | collective-permute-done | bytes 786464 | tf_op jit(solution)/shard_map/ppermute | solution.py:134
  99.4 2.1 %collective-permute-start.14 = (bf16[128,3072]{1,0:T(8,128)(2,1)}, bf16[128,3072]{1,0:T(8,128)(2,1)}, u32[]{:S(2)}, u32[]{:S(2)}) collective-permute-start(bf16[128,3072]{1,0:T(8,128)(2,1)} %collective-permute-done.6.refs_7_), channel_id=1, source_target_pairs={{0,32},{32,0},{64,96},{96,64},{128,160},{160,128},{192,224},{224,1... | collective-permute-start | bytes 2359304 | tf_op jit(solution)/shard_map/ppermute | solution.py:133
  101.6 2.3 %collective-permute-done.14.refs_15_ = bf16[128,3072]{1,0:T(8,128)(2,1)} collective-permute-done((bf16[128,3072]{1,0:T(8,128)(2,1)}, bf16[128,3072]{1,0:T(8,128)(2,1)}, u32[]{:S(2)}, u32[]{:S(2)}) %collective-permute-start.14) | collective-permute-done | bytes 786464 | tf_op jit(solution)/shard_map/ppermute | solution.py:133
  103.9 2.3 %first_block.1.first_ref = bf16[2176,512]{1,0:T(8,128)(2,1)S(1)} custom-call(s32[2]{0:T(128)S(1)} %pad_add_fusion.place_ref, bf16[128,1024]{1,0:T(8,128)(2,1)S(1)} %bitcast.12, bf16[128,3072]{1,0:T(8,128)(2,1)} %copy-done.5, bf16[128,3072]{1,0:T(8,128)(2,1)} %copy-done.6, bf16[128,3072]{1,0:T(8,128)(2,1)} %copy-done.7, ...), custom_call_target="tpu_custom_call" | custom-call | bytes 4456448 | tf_op jit(solution)/shard_map/first_block/pallas_call | solution.py:178
  106.3 7.4 %all-to-all-done.rows_hbm = bf16[32,32,2048]{2,1,0:T(8,128)(2,1)} async-done(((bf16[32,32,2048]{2,1,0:T(8,128)(2,1)}), bf16[32,32,2048]{2,1,0:T(8,128)(2,1)}, u32[]{:S(2)}, u32[]{:S(2)}) %all-to-all-start) | async-done | bytes 4194336 | tf_op jit(solution)/shard_map/all_to_all | solution.py:411
  113.7 15.6 %gradients.1 = (bf16[8,288,128]{2,1,0:T(8,128)(2,1)S(1)}, bf16[8,288,128]{2,1,0:T(8,128)(2,1)S(1)}) custom-call(s32[2]{0:T(128)S(1)} %pad_add_fusion.place_ref, bf16[32,32,2048]{2,1,0:T(8,128)(2,1)} %all-to-all-done.rows_hbm, bf16[64,2048]{1,0:T(8,128)(2,1)} %bitcast.24, bf16[2048,128]{1,0:T(8,128)(2,1)S(1)} %bitcast.14, bf16[64,1024]{1,0:T(8,128)(2,1)S(1)} %bitcast.15, ...), custom_call_target="tpu_custom_call" | custom-call | flops 7247757312 | bytes 16777216 | tf_op jit(solution)/shard_map/gradients/pallas_call | solution.py:322
  131.2 2.0 %collective-permute-done.15 = bf16[8,288,128]{2,1,0:T(8,128)(2,1)S(1)} collective-permute-done((bf16[8,288,128]{2,1,0:T(8,128)(2,1)S(1)}, bf16[8,288,128]{2,1,0:T(8,128)(2,1)S(1)}, u32[]{:S(2)}, u32[]{:S(2)}) %collective-permute-start.15) | collective-permute-done | bytes 589856 | tf_op jit(solution)/shard_map/ppermute | solution.py:424
  133.4 26.1 %all_to_all.10.parts_ref = bf16[8,288,128]{2,1,0:T(8,128)(2,1)S(1)} all-to-all(bf16[8,288,128]{2,1,0:T(8,128)(2,1)S(1)} %add_convert_fusion), channel_id=1, replica_groups={{0,64,128,192,256,320,384,448},{32,96,160,224,288,352,416,480},{1,65,12..., dimensions={0} | all-to-all | bytes 1179648 | tf_op jit(solution)/shard_map/all_to_all | solution.py:427
  (48 shorter events, 11.1 us)
Async XLA Ops:
  4.3 13.7 %copy-start.11 = (bf16[1,128,1024]{2,1,0:T(8,128)(2,1)S(1)}, bf16[1,128,1024]{2,1,0:T(8,128)(2,1)}, u32[]{:S(2)}) copy-start(bf16[1,128,1024]{2,1,0:T(8,128)(2,1)} %param.15) | copy-start | bytes 786436
  4.3 109.4 %all-to-all-start = ((bf16[32,32,2048]{2,1,0:T(8,128)(2,1)}), bf16[32,32,2048]{2,1,0:T(8,128)(2,1)}, u32[]{:S(2)}, u32[]{:S(2)}) async-start(bf16[32,32,2048]{2,1,0:T(8,128)(2,1)} %pack_rows.1), calls=%async_computation | async-start | bytes 8388608 | tf_op jit(solution)/shard_map/all_to_all | solution.py:411
  17.9 86.0 %copy-start = (bf16[1,128,1024]{2,1,0:T(8,128)(2,1)S(1)}, bf16[1,128,1024]{2,1,0:T(8,128)(2,1)}, u32[]{:S(2)}) copy-start(bf16[1,128,1024]{2,1,0:T(8,128)(2,1)} %param.17) | copy-start | bytes 786436
  18.1 85.8 %copy-start.5 = (bf16[128,3072]{1,0:T(8,128)(2,1)}, bf16[128,3072]{1,0:T(8,128)(2,1)S(1)}, u32[]{:S(2)}) copy-start(bf16[128,3072]{1,0:T(8,128)(2,1)S(1)} %slice_dynamic-update-slice_fusion.refs_0_) | copy-start | bytes 2359300
  18.1 22.4 %collective-permute-start = (bf16[128,3072]{1,0:T(8,128)(2,1)S(1)}, bf16[128,3072]{1,0:T(8,128)(2,1)S(1)}, u32[]{:S(2)}, u32[]{:S(2)}) collective-permute-start(bf16[128,3072]{1,0:T(8,128)(2,1)S(1)} %slice_dynamic-update-slice_fusion.refs_0_), channel_id=1, source_target_pairs={{0,64},{32,96},{64,128},{96,160},{128,192},{160,224},{192,256},{22... | collective-permute-start | bytes 2359304 | tf_op jit(solution)/shard_map/ppermute | solution.py:134
  21.6 20.8 %collective-permute-start.1 = (bf16[128,3072]{1,0:T(8,128)(2,1)S(1)}, bf16[128,3072]{1,0:T(8,128)(2,1)S(1)}, u32[]{:S(2)}, u32[]{:S(2)}) collective-permute-start(bf16[128,3072]{1,0:T(8,128)(2,1)S(1)} %slice_dynamic-update-slice_fusion.refs_0_), channel_id=1, source_target_pairs={{0,448},{32,480},{64,0},{96,32},{128,64},{160,96},{192,128},{224,1... | collective-permute-start | bytes 2359304 | tf_op jit(solution)/shard_map/ppermute | solution.py:134
  40.4 63.5 %copy-start.6 = (bf16[128,3072]{1,0:T(8,128)(2,1)}, bf16[128,3072]{1,0:T(8,128)(2,1)S(1)}, u32[]{:S(2)}) copy-start(bf16[128,3072]{1,0:T(8,128)(2,1)S(1)} %collective-permute-done.refs_1_) | copy-start | bytes 2359300
  40.4 21.4 %collective-permute-start.2 = (bf16[128,3072]{1,0:T(8,128)(2,1)S(1)}, bf16[128,3072]{1,0:T(8,128)(2,1)}, u32[]{:S(2)}, u32[]{:S(2)}) collective-permute-start(bf16[128,3072]{1,0:T(8,128)(2,1)S(1)} %collective-permute-done.refs_1_), channel_id=1, source_target_pairs={{0,64},{32,96},{64,128},{96,160},{128,192},{160,224},{192,256},{22... | collective-permute-start | bytes 2359304 | tf_op jit(solution)/shard_map/ppermute | solution.py:134
  42.4 21.4 %copy-start.7 = (bf16[128,3072]{1,0:T(8,128)(2,1)}, bf16[128,3072]{1,0:T(8,128)(2,1)S(1)}, u32[]{:S(2)}) copy-start(bf16[128,3072]{1,0:T(8,128)(2,1)S(1)} %collective-permute-done.1.refs_2_) | copy-start | bytes 2359300
  42.4 21.4 %collective-permute-start.3 = (bf16[128,3072]{1,0:T(8,128)(2,1)S(1)}, bf16[128,3072]{1,0:T(8,128)(2,1)}, u32[]{:S(2)}, u32[]{:S(2)}) collective-permute-start(bf16[128,3072]{1,0:T(8,128)(2,1)S(1)} %collective-permute-done.1.refs_2_), channel_id=1, source_target_pairs={{0,448},{32,480},{64,0},{96,32},{128,64},{160,96},{192,128},{224,1... | collective-permute-start | bytes 2359304 | tf_op jit(solution)/shard_map/ppermute | solution.py:134
  61.8 20.6 %collective-permute-start.4 = (bf16[128,3072]{1,0:T(8,128)(2,1)}, bf16[128,3072]{1,0:T(8,128)(2,1)S(1)}, u32[]{:S(2)}, u32[]{:S(2)}) collective-permute-start(bf16[128,3072]{1,0:T(8,128)(2,1)} %collective-permute-done.2.refs_3_), channel_id=1, source_target_pairs={{0,64},{32,96},{64,128},{96,160},{128,192},{160,224},{192,256},{22... | collective-permute-start | bytes 2359304 | tf_op jit(solution)/shard_map/ppermute | solution.py:134
  63.8 19.9 %collective-permute-start.5 = (bf16[128,3072]{1,0:T(8,128)(2,1)}, bf16[128,3072]{1,0:T(8,128)(2,1)S(1)}, u32[]{:S(2)}, u32[]{:S(2)}) collective-permute-start(bf16[128,3072]{1,0:T(8,128)(2,1)} %collective-permute-done.3.refs_4_), channel_id=1, source_target_pairs={{0,448},{32,480},{64,0},{96,32},{128,64},{160,96},{192,128},{224,1... | collective-permute-start | bytes 2359304 | tf_op jit(solution)/shard_map/ppermute | solution.py:134
  68.9 19.6 %collective-permute-start.7 = (bf16[128,3072]{1,0:T(8,128)(2,1)S(1)}, bf16[128,3072]{1,0:T(8,128)(2,1)}, u32[]{:S(2)}, u32[]{:S(2)}) collective-permute-start(bf16[128,3072]{1,0:T(8,128)(2,1)S(1)} %slice_dynamic-update-slice_fusion.refs_0_), channel_id=1, source_target_pairs={{0,32},{32,0},{64,96},{96,64},{128,160},{160,128},{192,224},{224,1... | collective-permute-start | bytes 2359304 | tf_op jit(solution)/shard_map/ppermute | solution.py:133
  70.8 20.1 %collective-permute-start.8 = (bf16[128,3072]{1,0:T(8,128)(2,1)S(1)}, bf16[128,3072]{1,0:T(8,128)(2,1)S(1)}, u32[]{:S(2)}, u32[]{:S(2)}) collective-permute-start(bf16[128,3072]{1,0:T(8,128)(2,1)S(1)} %collective-permute-done.refs_1_), channel_id=1, source_target_pairs={{0,32},{32,0},{64,96},{96,64},{128,160},{160,128},{192,224},{224,1... | collective-permute-start | bytes 2359304 | tf_op jit(solution)/shard_map/ppermute | solution.py:133
  73.3 19.6 %collective-permute-start.9 = (bf16[128,3072]{1,0:T(8,128)(2,1)}, bf16[128,3072]{1,0:T(8,128)(2,1)S(1)}, u32[]{:S(2)}, u32[]{:S(2)}) collective-permute-start(bf16[128,3072]{1,0:T(8,128)(2,1)} %copy-done.7), channel_id=1, source_target_pairs={{0,32},{32,0},{64,96},{96,64},{128,160},{160,128},{192,224},{224,1... | collective-permute-start | bytes 2359304 | tf_op jit(solution)/shard_map/ppermute | solution.py:133
  82.4 21.5 %copy-start.3 = (bf16[128,3072]{1,0:T(8,128)(2,1)}, bf16[128,3072]{1,0:T(8,128)(2,1)S(1)}, u32[]{:S(2)}) copy-start(bf16[128,3072]{1,0:T(8,128)(2,1)S(1)} %collective-permute-done.4.refs_5_) | copy-start | bytes 2359300
  83.7 20.2 %copy-start.4 = (bf16[128,3072]{1,0:T(8,128)(2,1)}, bf16[128,3072]{1,0:T(8,128)(2,1)S(1)}, u32[]{:S(2)}) copy-start(bf16[128,3072]{1,0:T(8,128)(2,1)S(1)} %collective-permute-done.5.refs_6_) | copy-start | bytes 2359300
  83.8 15.6 %collective-permute-start.6 = (bf16[128,3072]{1,0:T(8,128)(2,1)S(1)}, bf16[128,3072]{1,0:T(8,128)(2,1)}, u32[]{:S(2)}, u32[]{:S(2)}) collective-permute-start(bf16[128,3072]{1,0:T(8,128)(2,1)S(1)} %broadcast_select_fusion), channel_id=1, source_target_pairs={{0,64},{32,480},{64,128},{96,32},{128,192},{160,96},{192,256},{224... | collective-permute-start | bytes 2359304 | tf_op jit(solution)/shard_map/ppermute | solution.py:134
  86.6 15.0 %collective-permute-start.10 = (bf16[128,3072]{1,0:T(8,128)(2,1)}, bf16[128,3072]{1,0:T(8,128)(2,1)}, u32[]{:S(2)}, u32[]{:S(2)}) collective-permute-start(bf16[128,3072]{1,0:T(8,128)(2,1)} %collective-permute-done.2.refs_3_), channel_id=1, source_target_pairs={{0,32},{32,0},{64,96},{96,64},{128,160},{160,128},{192,224},{224,1... | collective-permute-start | bytes 2359304 | tf_op jit(solution)/shard_map/ppermute | solution.py:133
  88.5 13.0 %collective-permute-start.11 = (bf16[128,3072]{1,0:T(8,128)(2,1)}, bf16[128,3072]{1,0:T(8,128)(2,1)}, u32[]{:S(2)}, u32[]{:S(2)}) collective-permute-start(bf16[128,3072]{1,0:T(8,128)(2,1)} %collective-permute-done.3.refs_4_), channel_id=1, source_target_pairs={{0,32},{32,0},{64,96},{96,64},{128,160},{160,128},{192,224},{224,1... | collective-permute-start | bytes 2359304 | tf_op jit(solution)/shard_map/ppermute | solution.py:133
  91.0 10.6 %collective-permute-start.12 = (bf16[128,3072]{1,0:T(8,128)(2,1)S(1)}, bf16[128,3072]{1,0:T(8,128)(2,1)}, u32[]{:S(2)}, u32[]{:S(2)}) collective-permute-start(bf16[128,3072]{1,0:T(8,128)(2,1)S(1)} %collective-permute-done.4.refs_5_), channel_id=1, source_target_pairs={{0,32},{32,0},{64,96},{96,64},{128,160},{160,128},{192,224},{224,1... | collective-permute-start | bytes 2359304 | tf_op jit(solution)/shard_map/ppermute | solution.py:133
  93.8 7.8 %collective-permute-start.13 = (bf16[128,3072]{1,0:T(8,128)(2,1)S(1)}, bf16[128,3072]{1,0:T(8,128)(2,1)}, u32[]{:S(2)}, u32[]{:S(2)}) collective-permute-start(bf16[128,3072]{1,0:T(8,128)(2,1)S(1)} %collective-permute-done.5.refs_6_), channel_id=1, source_target_pairs={{0,32},{32,0},{64,96},{96,64},{128,160},{160,128},{192,224},{224,1... | collective-permute-start | bytes 2359304 | tf_op jit(solution)/shard_map/ppermute | solution.py:133
  99.4 4.5 %collective-permute-start.14 = (bf16[128,3072]{1,0:T(8,128)(2,1)}, bf16[128,3072]{1,0:T(8,128)(2,1)}, u32[]{:S(2)}, u32[]{:S(2)}) collective-permute-start(bf16[128,3072]{1,0:T(8,128)(2,1)} %collective-permute-done.6.refs_7_), channel_id=1, source_target_pairs={{0,32},{32,0},{64,96},{96,64},{128,160},{160,128},{192,224},{224,1... | collective-permute-start | bytes 2359304 | tf_op jit(solution)/shard_map/ppermute | solution.py:133
  129.3 3.9 %collective-permute-start.15 = (bf16[8,288,128]{2,1,0:T(8,128)(2,1)S(1)}, bf16[8,288,128]{2,1,0:T(8,128)(2,1)S(1)}, u32[]{:S(2)}, u32[]{:S(2)}) collective-permute-start(bf16[8,288,128]{2,1,0:T(8,128)(2,1)S(1)} %get-tuple-element.7), channel_id=1, source_target_pairs={{0,32},{32,0},{64,96},{96,64},{128,160},{160,128},{192,224},{224,1... | collective-permute-start | bytes 1769480 | tf_op jit(solution)/shard_map/ppermute | solution.py:424
  (5 other events, 36.0 us)

commit v6 on v5

--- a/solution.py
+++ b/solution.py
@@ -244,16 +244,16 @@
             i = 3 * step + part
             w_s[width:, i * BLOCK : (i + 1) * BLOCK] = jnp.concatenate(extra[part], axis=0)
     x_rows[:, :width] = x_s[...].reshape(slots, width)
-    low = dot_nn(x_rows[:, :width], narrow_s[...])
-    low_t = low.T.astype(BF16)
-    x_rows[:, width:] = low.astype(BF16)
+    low_t = dot_nt(narrow_s[...], x_rows[:, :width])
+    x_rows[:, width:] = low_t.T.astype(BF16)
+    low_t = low_t.astype(BF16)
     vals = [dot_nn(x_rows[...], first_ref[...])]
     rest = fetch_blocks(3, 6)
     wait(y_in)
     y_rows[:, :width] = y_s[...].reshape(slots, width)
-    z = dot_nt(y_rows[:, :width], dw_s[...])
-    z_t = z.T.astype(BF16)
-    z = z.astype(BF16)
+    z_t = dot_nt(dw_s[...], y_rows[:, :width])
+    z = z_t.T.astype(BF16)
+    z_t = z_t.astype(BF16)
     y_rows[:, width:] = jnp.concatenate([z, jnp.zeros_like(z)], axis=1)
     vals += [dot_nn(x_rows[...], block(1)), dot_nn(y_rows[...], block(2))]
     wait(rest)
@@ -350,7 +350,7 @@
         ),
         compiler_params=pltpu.CompilerParams(vmem_limit_bytes=VMEM),
         name="gradients",
-    )(place, *in_hbm(rows, dw), *in_vmem(narrow, dnt, win, first), *in_hbm(*pieces))
+    )(place, *in_hbm(rows, dw), *in_vmem(narrow.T, dnt, win, first), *in_hbm(*pieces))
 
 
 def finish_kernel(factor, parts_ref, ina_ref, inb_ref, dna_ref, dnb_ref):

time: 161 us -> 160 us (level)
  transfers between devices with their start and end apart: 17 -> 17, of which waited for: 8 -> 8; matrix products, arithmetic and copies ran while one was open for 0% -> 1% of each run, Pallas kernels for 1% -> 1%
where the time goes in v6:
time: 160 us; the launch traced here: 159 us
  starting transfers between devices  56.7 us (35%)
  waiting for transfers between devices  51.5 us (32%)
  blocking collectives  26.1 us (16%)
  Pallas kernels  21.6 us (14%)
  local copies, waits for them, and re-layouts  2.23 us (1%)
    ppermute x7, waiting for transfers between devices, gather_weights(): lax.ppermute(a, 'dp', [(i, (i + 2 * way(i)) % groups) for i in range(grou...  41.1 us
    all_to_all x1, blocking collectives, body(): lax.all_to_all(pair, 'dp', 0, 0, tiled=True, axis_index_groups=lines)  26.1 us
    ppermute x7, starting transfers between devices, gather_weights(): lax.ppermute(a, 'dp', [(i, (i + 2 * way(i)) % groups) for i in range(grou...  24.2 us
    ppermute x8, starting transfers between devices, gather_weights(): swap = lambda a: lax.ppermute(a, 'dp', [(i, i ^ 1) for i in range(groups)])  17 us
    pallas_call x1, Pallas kernels, gradients(): pl.pallas_call(functools.partial(gradients_kernel, parts // 2), in_specs=...  14.8 us
    all_to_all x1, starting transfers between devices, body(): rows = lax.all_to_all(rows, 'expert', 0, 0, tiled=True)  13.6 us
    all_to_all x1, waiting for transfers between devices, body(): rows = lax.all_to_all(rows, 'expert', 0, 0, tiled=True)  7.33 us
    pallas_call x1, Pallas kernels, pack_rows(): pl.pallas_call(functools.partial(pack_kernel, cap), in_specs=[pl.BlockSpe...  3.66 us
  transfers between devices with their start and end apart: 17, of which 8 were waited for; matrix products, arithmetic and copies ran while one was open for 1% of the time, Pallas kernels for 1%

profile of v6, /device:TPU:6, one launch (start us, length us, event | category | flops | bytes accessed | tf_op | source)
XLA Modules:
  0.0 159.5 jit_solution(14358994807477401794)
XLA Ops:
  0.6 3.7 %pack_rows.1 = bf16[32,32,2048]{2,1,0:T(8,128)(2,1)} custom-call(s32[8,128]{1,0:T(8,128)} %bitcast.24, f32[8,128]{1,0:T(8,128)} %bitcast.25, bf16[128,2048]{1,0:T(8,128)(2,1)} %tok_hbm.1, bf16[128,2048]{1,0:T(8,128)(2,1)} %cot_hbm.1), custom_call_target="tpu_custom_call" | custom-call | flops 536870912 | bytes 5242880 | tf_op jit(solution)/shard_map/pack_rows/pallas_call | solution.py:95
  4.3 13.6 %all-to-all-start = ((bf16[32,32,2048]{2,1,0:T(8,128)(2,1)}), bf16[32,32,2048]{2,1,0:T(8,128)(2,1)}, u32[]{:S(2)}, u32[]{:S(2)}) async-start(bf16[32,32,2048]{2,1,0:T(8,128)(2,1)} %pack_rows.1), calls=%async_computation | async-start | bytes 8388608 | tf_op jit(solution)/shard_map/all_to_all | solution.py:411
  18.1 3.5 %collective-permute-start = (bf16[128,3072]{1,0:T(8,128)(2,1)S(1)}, bf16[128,3072]{1,0:T(8,128)(2,1)}, u32[]{:S(2)}, u32[]{:S(2)}) collective-permute-start(bf16[128,3072]{1,0:T(8,128)(2,1)S(1)} %slice_dynamic-update-slice_fusion.refs_0_), channel_id=1, source_target_pairs={{0,64},{32,96},{64,128},{96,160},{128,192},{160,224},{192,256},{22... | collective-permute-start | bytes 2359304 | tf_op jit(solution)/shard_map/ppermute | solution.py:134
  21.6 3.8 %collective-permute-start.1 = (bf16[128,3072]{1,0:T(8,128)(2,1)S(1)}, bf16[128,3072]{1,0:T(8,128)(2,1)}, u32[]{:S(2)}, u32[]{:S(2)}) collective-permute-start(bf16[128,3072]{1,0:T(8,128)(2,1)S(1)} %slice_dynamic-update-slice_fusion.refs_0_), channel_id=1, source_target_pairs={{0,448},{32,480},{64,0},{96,32},{128,64},{160,96},{192,128},{224,1... | collective-permute-start | bytes 2359304 | tf_op jit(solution)/shard_map/ppermute | solution.py:134
  25.4 15.1 %collective-permute-done.refs_1_ = bf16[128,3072]{1,0:T(8,128)(2,1)} collective-permute-done((bf16[128,3072]{1,0:T(8,128)(2,1)S(1)}, bf16[128,3072]{1,0:T(8,128)(2,1)}, u32[]{:S(2)}, u32[]{:S(2)}) %collective-permute-start) | collective-permute-done | bytes 786464 | tf_op jit(solution)/shard_map/ppermute | solution.py:134
  42.5 5.1 %collective-permute-start.3 = (bf16[128,3072]{1,0:T(8,128)(2,1)}, bf16[128,3072]{1,0:T(8,128)(2,1)}, u32[]{:S(2)}, u32[]{:S(2)}) collective-permute-start(bf16[128,3072]{1,0:T(8,128)(2,1)} %collective-permute-done.1.refs_2_), channel_id=1, source_target_pairs={{0,448},{32,480},{64,0},{96,32},{128,64},{160,96},{192,128},{224,1... | collective-permute-start | bytes 2359304 | tf_op jit(solution)/shard_map/ppermute | solution.py:134
  47.6 14.4 %collective-permute-done.2.refs_3_ = bf16[128,3072]{1,0:T(8,128)(2,1)} collective-permute-done((bf16[128,3072]{1,0:T(8,128)(2,1)}, bf16[128,3072]{1,0:T(8,128)(2,1)}, u32[]{:S(2)}, u32[]{:S(2)}) %collective-permute-start.2) | collective-permute-done | bytes 786464 | tf_op jit(solution)/shard_map/ppermute | solution.py:134
  64.0 5.1 %collective-permute-start.5 = (bf16[128,3072]{1,0:T(8,128)(2,1)}, bf16[128,3072]{1,0:T(8,128)(2,1)S(1)}, u32[]{:S(2)}, u32[]{:S(2)}) collective-permute-start(bf16[128,3072]{1,0:T(8,128)(2,1)} %collective-permute-done.3.refs_4_), channel_id=1, source_target_pairs={{0,448},{32,480},{64,0},{96,32},{128,64},{160,96},{192,128},{224,1... | collective-permute-start | bytes 2359304 | tf_op jit(solution)/shard_map/ppermute | solution.py:134
  69.1 1.9 %collective-permute-start.7 = (bf16[128,3072]{1,0:T(8,128)(2,1)S(1)}, bf16[128,3072]{1,0:T(8,128)(2,1)}, u32[]{:S(2)}, u32[]{:S(2)}) collective-permute-start(bf16[128,3072]{1,0:T(8,128)(2,1)S(1)} %slice_dynamic-update-slice_fusion.refs_0_), channel_id=1, source_target_pairs={{0,32},{32,0},{64,96},{96,64},{128,160},{160,128},{192,224},{224,1... | collective-permute-start | bytes 2359304 | tf_op jit(solution)/shard_map/ppermute | solution.py:133
  71.1 2.4 %collective-permute-start.8 = (bf16[128,3072]{1,0:T(8,128)(2,1)}, bf16[128,3072]{1,0:T(8,128)(2,1)S(1)}, u32[]{:S(2)}, u32[]{:S(2)}) collective-permute-start(bf16[128,3072]{1,0:T(8,128)(2,1)} %collective-permute-done.refs_1_), channel_id=1, source_target_pairs={{0,32},{32,0},{64,96},{96,64},{128,160},{160,128},{192,224},{224,1... | collective-permute-start | bytes 2359304 | tf_op jit(solution)/shard_map/ppermute | solution.py:133
  75.4 7.1 %collective-permute-done.4.refs_5_ = bf16[128,3072]{1,0:T(8,128)(2,1)S(1)} collective-permute-done((bf16[128,3072]{1,0:T(8,128)(2,1)}, bf16[128,3072]{1,0:T(8,128)(2,1)S(1)}, u32[]{:S(2)}, u32[]{:S(2)}) %collective-permute-start.4) | collective-permute-done | bytes 786464 | tf_op jit(solution)/shard_map/ppermute | solution.py:134
  83.9 2.8 %collective-permute-start.6 = (bf16[128,3072]{1,0:T(8,128)(2,1)S(1)}, bf16[128,3072]{1,0:T(8,128)(2,1)}, u32[]{:S(2)}, u32[]{:S(2)}) collective-permute-start(bf16[128,3072]{1,0:T(8,128)(2,1)S(1)} %broadcast_select_fusion), channel_id=1, source_target_pairs={{0,64},{32,480},{64,128},{96,32},{128,192},{160,96},{192,256},{224... | collective-permute-start | bytes 2359304 | tf_op jit(solution)/shard_map/ppermute | solution.py:134
  86.7 1.9 %collective-permute-start.10 = (bf16[128,3072]{1,0:T(8,128)(2,1)}, bf16[128,3072]{1,0:T(8,128)(2,1)}, u32[]{:S(2)}, u32[]{:S(2)}) collective-permute-start(bf16[128,3072]{1,0:T(8,128)(2,1)} %collective-permute-done.2.refs_3_), channel_id=1, source_target_pairs={{0,32},{32,0},{64,96},{96,64},{128,160},{160,128},{192,224},{224,1... | collective-permute-start | bytes 2359304 | tf_op jit(solution)/shard_map/ppermute | solution.py:133
  88.6 2.4 %collective-permute-start.11 = (bf16[128,3072]{1,0:T(8,128)(2,1)}, bf16[128,3072]{1,0:T(8,128)(2,1)}, u32[]{:S(2)}, u32[]{:S(2)}) collective-permute-start(bf16[128,3072]{1,0:T(8,128)(2,1)} %collective-permute-done.3.refs_4_), channel_id=1, source_target_pairs={{0,32},{32,0},{64,96},{96,64},{128,160},{160,128},{192,224},{224,1... | collective-permute-start | bytes 2359304 | tf_op jit(solution)/shard_map/ppermute | solution.py:133
  91.1 1.9 %collective-permute-start.12 = (bf16[128,3072]{1,0:T(8,128)(2,1)S(1)}, bf16[128,3072]{1,0:T(8,128)(2,1)}, u32[]{:S(2)}, u32[]{:S(2)}) collective-permute-start(bf16[128,3072]{1,0:T(8,128)(2,1)S(1)} %collective-permute-done.4.refs_5_), channel_id=1, source_target_pairs={{0,32},{32,0},{64,96},{96,64},{128,160},{160,128},{192,224},{224,1... | collective-permute-start | bytes 2359304 | tf_op jit(solution)/shard_map/ppermute | solution.py:133
  93.9 2.4 %collective-permute-start.13 = (bf16[128,3072]{1,0:T(8,128)(2,1)S(1)}, bf16[128,3072]{1,0:T(8,128)(2,1)}, u32[]{:S(2)}, u32[]{:S(2)}) collective-permute-start(bf16[128,3072]{1,0:T(8,128)(2,1)S(1)} %collective-permute-done.5.refs_6_), channel_id=1, source_target_pairs={{0,32},{32,0},{64,96},{96,64},{128,160},{160,128},{192,224},{224,1... | collective-permute-start | bytes 2359304 | tf_op jit(solution)/shard_map/ppermute | solution.py:133
  96.3 3.2 %collective-permute-done.6.refs_7_ = bf16[128,3072]{1,0:T(8,128)(2,1)} collective-permute-done((bf16[128,3072]{1,0:T(8,128)(2,1)S(1)}, bf16[128,3072]{1,0:T(8,128)(2,1)}, u32[]{:S(2)}, u32[]{:S(2)}) %collective-permute-start.6) | collective-permute-done | bytes 786464 | tf_op jit(solution)/shard_map/ppermute | solution.py:134
  99.5 2.1 %collective-permute-start.14 = (bf16[128,3072]{1,0:T(8,128)(2,1)}, bf16[128,3072]{1,0:T(8,128)(2,1)}, u32[]{:S(2)}, u32[]{:S(2)}) collective-permute-start(bf16[128,3072]{1,0:T(8,128)(2,1)} %collective-permute-done.6.refs_7_), channel_id=1, source_target_pairs={{0,32},{32,0},{64,96},{96,64},{128,160},{160,128},{192,224},{224,1... | collective-permute-start | bytes 2359304 | tf_op jit(solution)/shard_map/ppermute | solution.py:133
  104.0 2.3 %first_block.1.first_ref = bf16[2176,512]{1,0:T(8,128)(2,1)S(1)} custom-call(s32[2]{0:T(128)S(1)} %pad_add_fusion.place_ref, bf16[128,1024]{1,0:T(8,128)(2,1)S(1)} %bitcast.15, bf16[128,3072]{1,0:T(8,128)(2,1)} %copy-done.4, bf16[128,3072]{1,0:T(8,128)(2,1)} %collective-permute-done.refs_1_, bf16[128,3072]{1,0:T(8,128)(2,1)} %collective-permute-done.1.refs_2_, ...), custom_call_target="tpu_custom_call" | custom-call | bytes 4456448 | tf_op jit(solution)/shard_map/first_block/pallas_call | solution.py:178
  106.4 7.3 %all-to-all-done.rows_hbm = bf16[32,32,2048]{2,1,0:T(8,128)(2,1)} async-done(((bf16[32,32,2048]{2,1,0:T(8,128)(2,1)}), bf16[32,32,2048]{2,1,0:T(8,128)(2,1)}, u32[]{:S(2)}, u32[]{:S(2)}) %all-to-all-start) | async-done | bytes 4194336 | tf_op jit(solution)/shard_map/all_to_all | solution.py:411
  113.7 14.8 %gradients.1 = (bf16[8,288,128]{2,1,0:T(8,128)(2,1)S(1)}, bf16[8,288,128]{2,1,0:T(8,128)(2,1)S(1)}) custom-call(s32[2]{0:T(128)S(1)} %pad_add_fusion.place_ref, bf16[32,32,2048]{2,1,0:T(8,128)(2,1)} %all-to-all-done.rows_hbm, bf16[64,2048]{1,0:T(8,128)(2,1)} %bitcast.26, bf16[128,2048]{1,0:T(8,128)(2,1)S(1)} %bitcast.14, bf16[64,1024]{1,0:T(8,128)(2,1)S(1)} %bitcast.17, ...), custom_call_target="tpu_custom_call" | custom-call | flops 7247757312 | bytes 16777216 | tf_op jit(solution)/shard_map/gradients/pallas_call | solution.py:322
  128.5 1.9 %collective-permute-start.15 = (bf16[8,288,128]{2,1,0:T(8,128)(2,1)S(1)}, bf16[8,288,128]{2,1,0:T(8,128)(2,1)S(1)}, u32[]{:S(2)}, u32[]{:S(2)}) collective-permute-start(bf16[8,288,128]{2,1,0:T(8,128)(2,1)S(1)} %get-tuple-element.7), channel_id=1, source_target_pairs={{0,32},{32,0},{64,96},{96,64},{128,160},{160,128},{192,224},{224,1... | collective-permute-start | bytes 1769480 | tf_op jit(solution)/shard_map/ppermute | solution.py:424
  130.5 2.0 %collective-permute-done.15 = bf16[8,288,128]{2,1,0:T(8,128)(2,1)S(1)} collective-permute-done((bf16[8,288,128]{2,1,0:T(8,128)(2,1)S(1)}, bf16[8,288,128]{2,1,0:T(8,128)(2,1)S(1)}, u32[]{:S(2)}, u32[]{:S(2)}) %collective-permute-start.15) | collective-permute-done | bytes 589856 | tf_op jit(solution)/shard_map/ppermute | solution.py:424
  132.6 26.1 %all_to_all.10.parts_ref = bf16[8,288,128]{2,1,0:T(8,128)(2,1)S(1)} all-to-all(bf16[8,288,128]{2,1,0:T(8,128)(2,1)S(1)} %add_convert_fusion), channel_id=1, replica_groups={{0,64,128,192,256,320,384,448},{32,96,160,224,288,352,416,480},{1,65,12..., dimensions={0} | all-to-all | bytes 1179648 | tf_op jit(solution)/shard_map/all_to_all | solution.py:427
  (43 shorter events, 11.4 us)
Async XLA Ops:
  4.3 13.6 %copy-start.7 = (bf16[1,128,2048]{2,1,0:T(8,128)(2,1)S(1)}, bf16[1,128,2048]{2,1,0:T(8,128)(2,1)}, u32[]{:S(2)}) copy-start(bf16[1,128,2048]{2,1,0:T(8,128)(2,1)} %param.14) | copy-start | bytes 1572868
  4.3 13.7 %copy-start.8 = (bf16[1,128,1024]{2,1,0:T(8,128)(2,1)S(1)}, bf16[1,128,1024]{2,1,0:T(8,128)(2,1)}, u32[]{:S(2)}) copy-start(bf16[1,128,1024]{2,1,0:T(8,128)(2,1)} %param.15) | copy-start | bytes 786436
  4.3 109.4 %all-to-all-start = ((bf16[32,32,2048]{2,1,0:T(8,128)(2,1)}), bf16[32,32,2048]{2,1,0:T(8,128)(2,1)}, u32[]{:S(2)}, u32[]{:S(2)}) async-start(bf16[32,32,2048]{2,1,0:T(8,128)(2,1)} %pack_rows.1), calls=%async_computation | async-start | bytes 8388608 | tf_op jit(solution)/shard_map/all_to_all | solution.py:411
  18.0 86.0 %copy-start = (bf16[1,128,1024]{2,1,0:T(8,128)(2,1)S(1)}, bf16[1,128,1024]{2,1,0:T(8,128)(2,1)}, u32[]{:S(2)}) copy-start(bf16[1,128,1024]{2,1,0:T(8,128)(2,1)} %param.17) | copy-start | bytes 786436
  18.1 85.9 %copy-start.4 = (bf16[128,3072]{1,0:T(8,128)(2,1)}, bf16[128,3072]{1,0:T(8,128)(2,1)S(1)}, u32[]{:S(2)}) copy-start(bf16[128,3072]{1,0:T(8,128)(2,1)S(1)} %slice_dynamic-update-slice_fusion.refs_0_) | copy-start | bytes 2359300
  18.1 22.5 %collective-permute-start = (bf16[128,3072]{1,0:T(8,128)(2,1)S(1)}, bf16[128,3072]{1,0:T(8,128)(2,1)}, u32[]{:S(2)}, u32[]{:S(2)}) collective-permute-start(bf16[128,3072]{1,0:T(8,128)(2,1)S(1)} %slice_dynamic-update-slice_fusion.refs_0_), channel_id=1, source_target_pairs={{0,64},{32,96},{64,128},{96,160},{128,192},{160,224},{192,256},{22... | collective-permute-start | bytes 2359304 | tf_op jit(solution)/shard_map/ppermute | solution.py:134
  21.6 20.9 %collective-permute-start.1 = (bf16[128,3072]{1,0:T(8,128)(2,1)S(1)}, bf16[128,3072]{1,0:T(8,128)(2,1)}, u32[]{:S(2)}, u32[]{:S(2)}) collective-permute-start(bf16[128,3072]{1,0:T(8,128)(2,1)S(1)} %slice_dynamic-update-slice_fusion.refs_0_), channel_id=1, source_target_pairs={{0,448},{32,480},{64,0},{96,32},{128,64},{160,96},{192,128},{224,1... | collective-permute-start | bytes 2359304 | tf_op jit(solution)/shard_map/ppermute | solution.py:134
  40.6 21.5 %collective-permute-start.2 = (bf16[128,3072]{1,0:T(8,128)(2,1)}, bf16[128,3072]{1,0:T(8,128)(2,1)}, u32[]{:S(2)}, u32[]{:S(2)}) collective-permute-start(bf16[128,3072]{1,0:T(8,128)(2,1)} %collective-permute-done.refs_1_), channel_id=1, source_target_pairs={{0,64},{32,96},{64,128},{96,160},{128,192},{160,224},{192,256},{22... | collective-permute-start | bytes 2359304 | tf_op jit(solution)/shard_map/ppermute | solution.py:134
  42.5 21.5 %collective-permute-start.3 = (bf16[128,3072]{1,0:T(8,128)(2,1)}, bf16[128,3072]{1,0:T(8,128)(2,1)}, u32[]{:S(2)}, u32[]{:S(2)}) collective-permute-start(bf16[128,3072]{1,0:T(8,128)(2,1)} %collective-permute-done.1.refs_2_), channel_id=1, source_target_pairs={{0,448},{32,480},{64,0},{96,32},{128,64},{160,96},{192,128},{224,1... | collective-permute-start | bytes 2359304 | tf_op jit(solution)/shard_map/ppermute | solution.py:134
  62.1 20.5 %collective-permute-start.4 = (bf16[128,3072]{1,0:T(8,128)(2,1)}, bf16[128,3072]{1,0:T(8,128)(2,1)S(1)}, u32[]{:S(2)}, u32[]{:S(2)}) collective-permute-start(bf16[128,3072]{1,0:T(8,128)(2,1)} %collective-permute-done.2.refs_3_), channel_id=1, source_target_pairs={{0,64},{32,96},{64,128},{96,160},{128,192},{160,224},{192,256},{22... | collective-permute-start | bytes 2359304 | tf_op jit(solution)/shard_map/ppermute | solution.py:134
  64.0 19.8 %collective-permute-start.5 = (bf16[128,3072]{1,0:T(8,128)(2,1)}, bf16[128,3072]{1,0:T(8,128)(2,1)S(1)}, u32[]{:S(2)}, u32[]{:S(2)}) collective-permute-start(bf16[128,3072]{1,0:T(8,128)(2,1)} %collective-permute-done.3.refs_4_), channel_id=1, source_target_pairs={{0,448},{32,480},{64,0},{96,32},{128,64},{160,96},{192,128},{224,1... | collective-permute-start | bytes 2359304 | tf_op jit(solution)/shard_map/ppermute | solution.py:134
  69.1 19.5 %collective-permute-start.7 = (bf16[128,3072]{1,0:T(8,128)(2,1)S(1)}, bf16[128,3072]{1,0:T(8,128)(2,1)}, u32[]{:S(2)}, u32[]{:S(2)}) collective-permute-start(bf16[128,3072]{1,0:T(8,128)(2,1)S(1)} %slice_dynamic-update-slice_fusion.refs_0_), channel_id=1, source_target_pairs={{0,32},{32,0},{64,96},{96,64},{128,160},{160,128},{192,224},{224,1... | collective-permute-start | bytes 2359304 | tf_op jit(solution)/shard_map/ppermute | solution.py:133
  71.1 20.0 %collective-permute-start.8 = (bf16[128,3072]{1,0:T(8,128)(2,1)}, bf16[128,3072]{1,0:T(8,128)(2,1)S(1)}, u32[]{:S(2)}, u32[]{:S(2)}) collective-permute-start(bf16[128,3072]{1,0:T(8,128)(2,1)} %collective-permute-done.refs_1_), channel_id=1, source_target_pairs={{0,32},{32,0},{64,96},{96,64},{128,160},{160,128},{192,224},{224,1... | collective-permute-start | bytes 2359304 | tf_op jit(solution)/shard_map/ppermute | solution.py:133
  73.5 19.5 %collective-permute-start.9 = (bf16[128,3072]{1,0:T(8,128)(2,1)}, bf16[128,3072]{1,0:T(8,128)(2,1)S(1)}, u32[]{:S(2)}, u32[]{:S(2)}) collective-permute-start(bf16[128,3072]{1,0:T(8,128)(2,1)} %collective-permute-done.1.refs_2_), channel_id=1, source_target_pairs={{0,32},{32,0},{64,96},{96,64},{128,160},{160,128},{192,224},{224,1... | collective-permute-start | bytes 2359304 | tf_op jit(solution)/shard_map/ppermute | solution.py:133
  82.5 21.5 %copy-start.2 = (bf16[128,3072]{1,0:T(8,128)(2,1)}, bf16[128,3072]{1,0:T(8,128)(2,1)S(1)}, u32[]{:S(2)}) copy-start(bf16[128,3072]{1,0:T(8,128)(2,1)S(1)} %collective-permute-done.4.refs_5_) | copy-start | bytes 2359300
  83.8 20.2 %copy-start.3 = (bf16[128,3072]{1,0:T(8,128)(2,1)}, bf16[128,3072]{1,0:T(8,128)(2,1)S(1)}, u32[]{:S(2)}) copy-start(bf16[128,3072]{1,0:T(8,128)(2,1)S(1)} %collective-permute-done.5.refs_6_) | copy-start | bytes 2359300
  83.9 15.6 %collective-permute-start.6 = (bf16[128,3072]{1,0:T(8,128)(2,1)S(1)}, bf16[128,3072]{1,0:T(8,128)(2,1)}, u32[]{:S(2)}, u32[]{:S(2)}) collective-permute-start(bf16[128,3072]{1,0:T(8,128)(2,1)S(1)} %broadcast_select_fusion), channel_id=1, source_target_pairs={{0,64},{32,480},{64,128},{96,32},{128,192},{160,96},{192,256},{224... | collective-permute-start | bytes 2359304 | tf_op jit(solution)/shard_map/ppermute | solution.py:134
  86.7 16.2 %collective-permute-start.10 = (bf16[128,3072]{1,0:T(8,128)(2,1)}, bf16[128,3072]{1,0:T(8,128)(2,1)}, u32[]{:S(2)}, u32[]{:S(2)}) collective-permute-start(bf16[128,3072]{1,0:T(8,128)(2,1)} %collective-permute-done.2.refs_3_), channel_id=1, source_target_pairs={{0,32},{32,0},{64,96},{96,64},{128,160},{160,128},{192,224},{224,1... | collective-permute-start | bytes 2359304 | tf_op jit(solution)/shard_map/ppermute | solution.py:133
  88.6 14.3 %collective-permute-start.11 = (bf16[128,3072]{1,0:T(8,128)(2,1)}, bf16[128,3072]{1,0:T(8,128)(2,1)}, u32[]{:S(2)}, u32[]{:S(2)}) collective-permute-start(bf16[128,3072]{1,0:T(8,128)(2,1)} %collective-permute-done.3.refs_4_), channel_id=1, source_target_pairs={{0,32},{32,0},{64,96},{96,64},{128,160},{160,128},{192,224},{224,1... | collective-permute-start | bytes 2359304 | tf_op jit(solution)/shard_map/ppermute | solution.py:133
  91.1 11.9 %collective-permute-start.12 = (bf16[128,3072]{1,0:T(8,128)(2,1)S(1)}, bf16[128,3072]{1,0:T(8,128)(2,1)}, u32[]{:S(2)}, u32[]{:S(2)}) collective-permute-start(bf16[128,3072]{1,0:T(8,128)(2,1)S(1)} %collective-permute-done.4.refs_5_), channel_id=1, source_target_pairs={{0,32},{32,0},{64,96},{96,64},{128,160},{160,128},{192,224},{224,1... | collective-permute-start | bytes 2359304 | tf_op jit(solution)/shard_map/ppermute | solution.py:133
  93.9 9.0 %collective-permute-start.13 = (bf16[128,3072]{1,0:T(8,128)(2,1)S(1)}, bf16[128,3072]{1,0:T(8,128)(2,1)}, u32[]{:S(2)}, u32[]{:S(2)}) collective-permute-start(bf16[128,3072]{1,0:T(8,128)(2,1)S(1)} %collective-permute-done.5.refs_6_), channel_id=1, source_target_pairs={{0,32},{32,0},{64,96},{96,64},{128,160},{160,128},{192,224},{224,1... | collective-permute-start | bytes 2359304 | tf_op jit(solution)/shard_map/ppermute | solution.py:133
  99.5 4.5 %collective-permute-start.14 = (bf16[128,3072]{1,0:T(8,128)(2,1)}, bf16[128,3072]{1,0:T(8,128)(2,1)}, u32[]{:S(2)}, u32[]{:S(2)}) collective-permute-start(bf16[128,3072]{1,0:T(8,128)(2,1)} %collective-permute-done.6.refs_7_), channel_id=1, source_target_pairs={{0,32},{32,0},{64,96},{96,64},{128,160},{160,128},{192,224},{224,1... | collective-permute-start | bytes 2359304 | tf_op jit(solution)/shard_map/ppermute | solution.py:133
  104.0 9.7 %copy-start.1 = (bf16[1,1024,64]{1,2,0:T(8,128)(2,1)S(1)}, bf16[1,1024,64]{1,2,0:T(8,128)(2,1)}, u32[]{:S(2)}) copy-start(bf16[1,1024,64]{1,2,0:T(8,128)(2,1)} %param.18) | copy-start | bytes 393220
  128.5 3.9 %collective-permute-start.15 = (bf16[8,288,128]{2,1,0:T(8,128)(2,1)S(1)}, bf16[8,288,128]{2,1,0:T(8,128)(2,1)S(1)}, u32[]{:S(2)}, u32[]{:S(2)}) collective-permute-start(bf16[8,288,128]{2,1,0:T(8,128)(2,1)S(1)} %get-tuple-element.7), channel_id=1, source_target_pairs={{0,32},{32,0},{64,96},{96,64},{128,160},{160,128},{192,224},{224,1... | collective-permute-start | bytes 1769480 | tf_op jit(solution)/shard_map/ppermute | solution.py:424
  (2 other events, 2.8 us)

commit v7 on v6

--- a/solution.py
+++ b/solution.py
@@ -250,12 +250,13 @@
     vals = [dot_nn(x_rows[...], first_ref[...])]
     rest = fetch_blocks(3, 6)
     wait(y_in)
+    vals.append(dot_nn(x_rows[...], block(1)))
     y_rows[:, :width] = y_s[...].reshape(slots, width)
     z_t = dot_nt(dw_s[...], y_rows[:, :width])
     z = z_t.T.astype(BF16)
     z_t = z_t.astype(BF16)
     y_rows[:, width:] = jnp.concatenate([z, jnp.zeros_like(z)], axis=1)
-    vals += [dot_nn(x_rows[...], block(1)), dot_nn(y_rows[...], block(2))]
+    vals.append(dot_nn(y_rows[...], block(2)))
     wait(rest)
     for i in range(3, 6):
         vals.append(dot_nn(y_rows[...] if i % 3 == 2 else x_rows[...], block(i)))

time: 160 us -> 160 us (level)
  no operation moved by 1% of the time
where the time goes in v7:
time: 160 us; the launch traced here: 159 us
  starting transfers between devices  56.5 us (35%)
  waiting for transfers between devices  51.7 us (32%)
  blocking collectives  26.1 us (16%)
  Pallas kernels  21.5 us (13%)
  local copies, waits for them, and re-layouts  2.23 us (1%)
    ppermute x7, waiting for transfers between devices, gather_weights(): lax.ppermute(a, 'dp', [(i, (i + 2 * way(i)) % groups) for i in range(grou...  41.2 us
    all_to_all x1, blocking collectives, body(): lax.all_to_all(pair, 'dp', 0, 0, tiled=True, axis_index_groups=lines)  26.1 us
    ppermute x7, starting transfers between devices, gather_weights(): lax.ppermute(a, 'dp', [(i, (i + 2 * way(i)) % groups) for i in range(grou...  24.2 us
    ppermute x8, starting transfers between devices, gather_weights(): swap = lambda a: lax.ppermute(a, 'dp', [(i, i ^ 1) for i in range(groups)])  16.8 us
    pallas_call x1, Pallas kernels, gradients(): pl.pallas_call(functools.partial(gradients_kernel, parts // 2), in_specs=...  14.8 us
    all_to_all x1, starting transfers between devices, body(): rows = lax.all_to_all(rows, 'expert', 0, 0, tiled=True)  13.6 us
    all_to_all x1, waiting for transfers between devices, body(): rows = lax.all_to_all(rows, 'expert', 0, 0, tiled=True)  7.33 us
    pallas_call x1, Pallas kernels, pack_rows(): pl.pallas_call(functools.partial(pack_kernel, cap), in_specs=[pl.BlockSpe...  3.66 us
  transfers between devices with their start and end apart: 17, of which 8 were waited for; matrix products, arithmetic and copies ran while one was open for 1% of the time, Pallas kernels for 1%

profile of v7, /device:TPU:6, one launch (start us, length us, event | category | flops | bytes accessed | tf_op | source)
XLA Modules:
  0.0 159.4 jit_solution(10688821737700369753)
XLA Ops:
  0.6 3.7 %pack_rows.1 = bf16[32,32,2048]{2,1,0:T(8,128)(2,1)} custom-call(s32[8,128]{1,0:T(8,128)} %bitcast.24, f32[8,128]{1,0:T(8,128)} %bitcast.25, bf16[128,2048]{1,0:T(8,128)(2,1)} %tok_hbm.1, bf16[128,2048]{1,0:T(8,128)(2,1)} %cot_hbm.1), custom_call_target="tpu_custom_call" | custom-call | flops 536870912 | bytes 5242880 | tf_op jit(solution)/shard_map/pack_rows/pallas_call | solution.py:95
  4.3 13.6 %all-to-all-start = ((bf16[32,32,2048]{2,1,0:T(8,128)(2,1)}), bf16[32,32,2048]{2,1,0:T(8,128)(2,1)}, u32[]{:S(2)}, u32[]{:S(2)}) async-start(bf16[32,32,2048]{2,1,0:T(8,128)(2,1)} %pack_rows.1), calls=%async_computation | async-start | bytes 8388608 | tf_op jit(solution)/shard_map/all_to_all | solution.py:412
  18.1 3.5 %collective-permute-start = (bf16[128,3072]{1,0:T(8,128)(2,1)S(1)}, bf16[128,3072]{1,0:T(8,128)(2,1)}, u32[]{:S(2)}, u32[]{:S(2)}) collective-permute-start(bf16[128,3072]{1,0:T(8,128)(2,1)S(1)} %slice_dynamic-update-slice_fusion.refs_0_), channel_id=1, source_target_pairs={{0,64},{32,96},{64,128},{96,160},{128,192},{160,224},{192,256},{22... | collective-permute-start | bytes 2359304 | tf_op jit(solution)/shard_map/ppermute | solution.py:134
  21.6 3.8 %collective-permute-start.1 = (bf16[128,3072]{1,0:T(8,128)(2,1)S(1)}, bf16[128,3072]{1,0:T(8,128)(2,1)}, u32[]{:S(2)}, u32[]{:S(2)}) collective-permute-start(bf16[128,3072]{1,0:T(8,128)(2,1)S(1)} %slice_dynamic-update-slice_fusion.refs_0_), channel_id=1, source_target_pairs={{0,448},{32,480},{64,0},{96,32},{128,64},{160,96},{192,128},{224,1... | collective-permute-start | bytes 2359304 | tf_op jit(solution)/shard_map/ppermute | solution.py:134
  25.4 15.1 %collective-permute-done.refs_1_ = bf16[128,3072]{1,0:T(8,128)(2,1)} collective-permute-done((bf16[128,3072]{1,0:T(8,128)(2,1)S(1)}, bf16[128,3072]{1,0:T(8,128)(2,1)}, u32[]{:S(2)}, u32[]{:S(2)}) %collective-permute-start) | collective-permute-done | bytes 786464 | tf_op jit(solution)/shard_map/ppermute | solution.py:134
  42.5 5.1 %collective-permute-start.3 = (bf16[128,3072]{1,0:T(8,128)(2,1)}, bf16[128,3072]{1,0:T(8,128)(2,1)}, u32[]{:S(2)}, u32[]{:S(2)}) collective-permute-start(bf16[128,3072]{1,0:T(8,128)(2,1)} %collective-permute-done.1.refs_2_), channel_id=1, source_target_pairs={{0,448},{32,480},{64,0},{96,32},{128,64},{160,96},{192,128},{224,1... | collective-permute-start | bytes 2359304 | tf_op jit(solution)/shard_map/ppermute | solution.py:134
  47.6 14.4 %collective-permute-done.2.refs_3_ = bf16[128,3072]{1,0:T(8,128)(2,1)} collective-permute-done((bf16[128,3072]{1,0:T(8,128)(2,1)}, bf16[128,3072]{1,0:T(8,128)(2,1)}, u32[]{:S(2)}, u32[]{:S(2)}) %collective-permute-start.2) | collective-permute-done | bytes 786464 | tf_op jit(solution)/shard_map/ppermute | solution.py:134
  64.0 5.1 %collective-permute-start.5 = (bf16[128,3072]{1,0:T(8,128)(2,1)}, bf16[128,3072]{1,0:T(8,128)(2,1)S(1)}, u32[]{:S(2)}, u32[]{:S(2)}) collective-permute-start(bf16[128,3072]{1,0:T(8,128)(2,1)} %collective-permute-done.3.refs_4_), channel_id=1, source_target_pairs={{0,448},{32,480},{64,0},{96,32},{128,64},{160,96},{192,128},{224,1... | collective-permute-start | bytes 2359304 | tf_op jit(solution)/shard_map/ppermute | solution.py:134
  69.1 1.9 %collective-permute-start.7 = (bf16[128,3072]{1,0:T(8,128)(2,1)S(1)}, bf16[128,3072]{1,0:T(8,128)(2,1)}, u32[]{:S(2)}, u32[]{:S(2)}) collective-permute-start(bf16[128,3072]{1,0:T(8,128)(2,1)S(1)} %slice_dynamic-update-slice_fusion.refs_0_), channel_id=1, source_target_pairs={{0,32},{32,0},{64,96},{96,64},{128,160},{160,128},{192,224},{224,1... | collective-permute-start | bytes 2359304 | tf_op jit(solution)/shard_map/ppermute | solution.py:133
  71.1 2.4 %collective-permute-start.8 = (bf16[128,3072]{1,0:T(8,128)(2,1)}, bf16[128,3072]{1,0:T(8,128)(2,1)S(1)}, u32[]{:S(2)}, u32[]{:S(2)}) collective-permute-start(bf16[128,3072]{1,0:T(8,128)(2,1)} %collective-permute-done.refs_1_), channel_id=1, source_target_pairs={{0,32},{32,0},{64,96},{96,64},{128,160},{160,128},{192,224},{224,1... | collective-permute-start | bytes 2359304 | tf_op jit(solution)/shard_map/ppermute | solution.py:133
  73.5 1.9 %collective-permute-start.9 = (bf16[128,3072]{1,0:T(8,128)(2,1)}, bf16[128,3072]{1,0:T(8,128)(2,1)S(1)}, u32[]{:S(2)}, u32[]{:S(2)}) collective-permute-start(bf16[128,3072]{1,0:T(8,128)(2,1)} %collective-permute-done.1.refs_2_), channel_id=1, source_target_pairs={{0,32},{32,0},{64,96},{96,64},{128,160},{160,128},{192,224},{224,1... | collective-permute-start | bytes 2359304 | tf_op jit(solution)/shard_map/ppermute | solution.py:133
  75.4 7.1 %collective-permute-done.4.refs_5_ = bf16[128,3072]{1,0:T(8,128)(2,1)S(1)} collective-permute-done((bf16[128,3072]{1,0:T(8,128)(2,1)}, bf16[128,3072]{1,0:T(8,128)(2,1)S(1)}, u32[]{:S(2)}, u32[]{:S(2)}) %collective-permute-start.4) | collective-permute-done | bytes 786464 | tf_op jit(solution)/shard_map/ppermute | solution.py:134
  83.9 2.8 %collective-permute-start.6 = (bf16[128,3072]{1,0:T(8,128)(2,1)S(1)}, bf16[128,3072]{1,0:T(8,128)(2,1)}, u32[]{:S(2)}, u32[]{:S(2)}) collective-permute-start(bf16[128,3072]{1,0:T(8,128)(2,1)S(1)} %broadcast_select_fusion), channel_id=1, source_target_pairs={{0,64},{32,480},{64,128},{96,32},{128,192},{160,96},{192,256},{224... | collective-permute-start | bytes 2359304 | tf_op jit(solution)/shard_map/ppermute | solution.py:134
  86.7 1.9 %collective-permute-start.10 = (bf16[128,3072]{1,0:T(8,128)(2,1)}, bf16[128,3072]{1,0:T(8,128)(2,1)}, u32[]{:S(2)}, u32[]{:S(2)}) collective-permute-start(bf16[128,3072]{1,0:T(8,128)(2,1)} %collective-permute-done.2.refs_3_), channel_id=1, source_target_pairs={{0,32},{32,0},{64,96},{96,64},{128,160},{160,128},{192,224},{224,1... | collective-permute-start | bytes 2359304 | tf_op jit(solution)/shard_map/ppermute | solution.py:133
  88.6 2.4 %collective-permute-start.11 = (bf16[128,3072]{1,0:T(8,128)(2,1)}, bf16[128,3072]{1,0:T(8,128)(2,1)}, u32[]{:S(2)}, u32[]{:S(2)}) collective-permute-start(bf16[128,3072]{1,0:T(8,128)(2,1)} %collective-permute-done.3.refs_4_), channel_id=1, source_target_pairs={{0,32},{32,0},{64,96},{96,64},{128,160},{160,128},{192,224},{224,1... | collective-permute-start | bytes 2359304 | tf_op jit(solution)/shard_map/ppermute | solution.py:133
  91.1 1.9 %collective-permute-start.12 = (bf16[128,3072]{1,0:T(8,128)(2,1)S(1)}, bf16[128,3072]{1,0:T(8,128)(2,1)}, u32[]{:S(2)}, u32[]{:S(2)}) collective-permute-start(bf16[128,3072]{1,0:T(8,128)(2,1)S(1)} %collective-permute-done.4.refs_5_), channel_id=1, source_target_pairs={{0,32},{32,0},{64,96},{96,64},{128,160},{160,128},{192,224},{224,1... | collective-permute-start | bytes 2359304 | tf_op jit(solution)/shard_map/ppermute | solution.py:133
  93.9 2.4 %collective-permute-start.13 = (bf16[128,3072]{1,0:T(8,128)(2,1)S(1)}, bf16[128,3072]{1,0:T(8,128)(2,1)}, u32[]{:S(2)}, u32[]{:S(2)}) collective-permute-start(bf16[128,3072]{1,0:T(8,128)(2,1)S(1)} %collective-permute-done.5.refs_6_), channel_id=1, source_target_pairs={{0,32},{32,0},{64,96},{96,64},{128,160},{160,128},{192,224},{224,1... | collective-permute-start | bytes 2359304 | tf_op jit(solution)/shard_map/ppermute | solution.py:133
  96.3 3.2 %collective-permute-done.6.refs_7_ = bf16[128,3072]{1,0:T(8,128)(2,1)} collective-permute-done((bf16[128,3072]{1,0:T(8,128)(2,1)S(1)}, bf16[128,3072]{1,0:T(8,128)(2,1)}, u32[]{:S(2)}, u32[]{:S(2)}) %collective-permute-start.6) | collective-permute-done | bytes 786464 | tf_op jit(solution)/shard_map/ppermute | solution.py:134
  104.0 2.3 %first_block.1.first_ref = bf16[2176,512]{1,0:T(8,128)(2,1)S(1)} custom-call(s32[2]{0:T(128)S(1)} %pad_add_fusion.place_ref, bf16[128,1024]{1,0:T(8,128)(2,1)S(1)} %bitcast.15, bf16[128,3072]{1,0:T(8,128)(2,1)} %copy-done.4, bf16[128,3072]{1,0:T(8,128)(2,1)} %collective-permute-done.refs_1_, bf16[128,3072]{1,0:T(8,128)(2,1)} %collective-permute-done.1.refs_2_, ...), custom_call_target="tpu_custom_call" | custom-call | bytes 4456448 | tf_op jit(solution)/shard_map/first_block/pallas_call | solution.py:178
  106.4 7.3 %all-to-all-done.rows_hbm = bf16[32,32,2048]{2,1,0:T(8,128)(2,1)} async-done(((bf16[32,32,2048]{2,1,0:T(8,128)(2,1)}), bf16[32,32,2048]{2,1,0:T(8,128)(2,1)}, u32[]{:S(2)}, u32[]{:S(2)}) %all-to-all-start) | async-done | bytes 4194336 | tf_op jit(solution)/shard_map/all_to_all | solution.py:412
  113.7 14.8 %gradients.1 = (bf16[8,288,128]{2,1,0:T(8,128)(2,1)S(1)}, bf16[8,288,128]{2,1,0:T(8,128)(2,1)S(1)}) custom-call(s32[2]{0:T(128)S(1)} %pad_add_fusion.place_ref, bf16[32,32,2048]{2,1,0:T(8,128)(2,1)} %all-to-all-done.rows_hbm, bf16[64,2048]{1,0:T(8,128)(2,1)} %bitcast.26, bf16[128,2048]{1,0:T(8,128)(2,1)S(1)} %bitcast.14, bf16[64,1024]{1,0:T(8,128)(2,1)S(1)} %bitcast.17, ...), custom_call_target="tpu_custom_call" | custom-call | flops 7247757312 | bytes 16777216 | tf_op jit(solution)/shard_map/gradients/pallas_call | solution.py:323
  128.5 1.9 %collective-permute-start.15 = (bf16[8,288,128]{2,1,0:T(8,128)(2,1)S(1)}, bf16[8,288,128]{2,1,0:T(8,128)(2,1)S(1)}, u32[]{:S(2)}, u32[]{:S(2)}) collective-permute-start(bf16[8,288,128]{2,1,0:T(8,128)(2,1)S(1)} %get-tuple-element.7), channel_id=1, source_target_pairs={{0,32},{32,0},{64,96},{96,64},{128,160},{160,128},{192,224},{224,1... | collective-permute-start | bytes 1769480 | tf_op jit(solution)/shard_map/ppermute | solution.py:425
  130.4 2.0 %collective-permute-done.15 = bf16[8,288,128]{2,1,0:T(8,128)(2,1)S(1)} collective-permute-done((bf16[8,288,128]{2,1,0:T(8,128)(2,1)S(1)}, bf16[8,288,128]{2,1,0:T(8,128)(2,1)S(1)}, u32[]{:S(2)}, u32[]{:S(2)}) %collective-permute-start.15) | collective-permute-done | bytes 589856 | tf_op jit(solution)/shard_map/ppermute | solution.py:425
  132.5 26.1 %all_to_all.10.parts_ref = bf16[8,288,128]{2,1,0:T(8,128)(2,1)S(1)} all-to-all(bf16[8,288,128]{2,1,0:T(8,128)(2,1)S(1)} %add_convert_fusion), channel_id=1, replica_groups={{0,64,128,192,256,320,384,448},{32,96,160,224,288,352,416,480},{1,65,12..., dimensions={0} | all-to-all | bytes 1179648 | tf_op jit(solution)/shard_map/all_to_all | solution.py:428
  (43 shorter events, 11.6 us)
Async XLA Ops:
  4.3 13.6 %copy-start.7 = (bf16[1,128,2048]{2,1,0:T(8,128)(2,1)S(1)}, bf16[1,128,2048]{2,1,0:T(8,128)(2,1)}, u32[]{:S(2)}) copy-start(bf16[1,128,2048]{2,1,0:T(8,128)(2,1)} %param.14) | copy-start | bytes 1572868
  4.3 13.7 %copy-start.8 = (bf16[1,128,1024]{2,1,0:T(8,128)(2,1)S(1)}, bf16[1,128,1024]{2,1,0:T(8,128)(2,1)}, u32[]{:S(2)}) copy-start(bf16[1,128,1024]{2,1,0:T(8,128)(2,1)} %param.15) | copy-start | bytes 786436
  4.3 109.4 %all-to-all-start = ((bf16[32,32,2048]{2,1,0:T(8,128)(2,1)}), bf16[32,32,2048]{2,1,0:T(8,128)(2,1)}, u32[]{:S(2)}, u32[]{:S(2)}) async-start(bf16[32,32,2048]{2,1,0:T(8,128)(2,1)} %pack_rows.1), calls=%async_computation | async-start | bytes 8388608 | tf_op jit(solution)/shard_map/all_to_all | solution.py:412
  18.0 86.0 %copy-start = (bf16[1,128,1024]{2,1,0:T(8,128)(2,1)S(1)}, bf16[1,128,1024]{2,1,0:T(8,128)(2,1)}, u32[]{:S(2)}) copy-start(bf16[1,128,1024]{2,1,0:T(8,128)(2,1)} %param.17) | copy-start | bytes 786436
  18.1 85.9 %copy-start.4 = (bf16[128,3072]{1,0:T(8,128)(2,1)}, bf16[128,3072]{1,0:T(8,128)(2,1)S(1)}, u32[]{:S(2)}) copy-start(bf16[128,3072]{1,0:T(8,128)(2,1)S(1)} %slice_dynamic-update-slice_fusion.refs_0_) | copy-start | bytes 2359300
  18.1 22.5 %collective-permute-start = (bf16[128,3072]{1,0:T(8,128)(2,1)S(1)}, bf16[128,3072]{1,0:T(8,128)(2,1)}, u32[]{:S(2)}, u32[]{:S(2)}) collective-permute-start(bf16[128,3072]{1,0:T(8,128)(2,1)S(1)} %slice_dynamic-update-slice_fusion.refs_0_), channel_id=1, source_target_pairs={{0,64},{32,96},{64,128},{96,160},{128,192},{160,224},{192,256},{22... | collective-permute-start | bytes 2359304 | tf_op jit(solution)/shard_map/ppermute | solution.py:134
  21.6 20.9 %collective-permute-start.1 = (bf16[128,3072]{1,0:T(8,128)(2,1)S(1)}, bf16[128,3072]{1,0:T(8,128)(2,1)}, u32[]{:S(2)}, u32[]{:S(2)}) collective-permute-start(bf16[128,3072]{1,0:T(8,128)(2,1)S(1)} %slice_dynamic-update-slice_fusion.refs_0_), channel_id=1, source_target_pairs={{0,448},{32,480},{64,0},{96,32},{128,64},{160,96},{192,128},{224,1... | collective-permute-start | bytes 2359304 | tf_op jit(solution)/shard_map/ppermute | solution.py:134
  40.6 21.5 %collective-permute-start.2 = (bf16[128,3072]{1,0:T(8,128)(2,1)}, bf16[128,3072]{1,0:T(8,128)(2,1)}, u32[]{:S(2)}, u32[]{:S(2)}) collective-permute-start(bf16[128,3072]{1,0:T(8,128)(2,1)} %collective-permute-done.refs_1_), channel_id=1, source_target_pairs={{0,64},{32,96},{64,128},{96,160},{128,192},{160,224},{192,256},{22... | collective-permute-start | bytes 2359304 | tf_op jit(solution)/shard_map/ppermute | solution.py:134
  42.5 21.5 %collective-permute-start.3 = (bf16[128,3072]{1,0:T(8,128)(2,1)}, bf16[128,3072]{1,0:T(8,128)(2,1)}, u32[]{:S(2)}, u32[]{:S(2)}) collective-permute-start(bf16[128,3072]{1,0:T(8,128)(2,1)} %collective-permute-done.1.refs_2_), channel_id=1, source_target_pairs={{0,448},{32,480},{64,0},{96,32},{128,64},{160,96},{192,128},{224,1... | collective-permute-start | bytes 2359304 | tf_op jit(solution)/shard_map/ppermute | solution.py:134
  62.1 20.5 %collective-permute-start.4 = (bf16[128,3072]{1,0:T(8,128)(2,1)}, bf16[128,3072]{1,0:T(8,128)(2,1)S(1)}, u32[]{:S(2)}, u32[]{:S(2)}) collective-permute-start(bf16[128,3072]{1,0:T(8,128)(2,1)} %collective-permute-done.2.refs_3_), channel_id=1, source_target_pairs={{0,64},{32,96},{64,128},{96,160},{128,192},{160,224},{192,256},{22... | collective-permute-start | bytes 2359304 | tf_op jit(solution)/shard_map/ppermute | solution.py:134
  64.0 19.8 %collective-permute-start.5 = (bf16[128,3072]{1,0:T(8,128)(2,1)}, bf16[128,3072]{1,0:T(8,128)(2,1)S(1)}, u32[]{:S(2)}, u32[]{:S(2)}) collective-permute-start(bf16[128,3072]{1,0:T(8,128)(2,1)} %collective-permute-done.3.refs_4_), channel_id=1, source_target_pairs={{0,448},{32,480},{64,0},{96,32},{128,64},{160,96},{192,128},{224,1... | collective-permute-start | bytes 2359304 | tf_op jit(solution)/shard_map/ppermute | solution.py:134
  69.1 19.5 %collective-permute-start.7 = (bf16[128,3072]{1,0:T(8,128)(2,1)S(1)}, bf16[128,3072]{1,0:T(8,128)(2,1)}, u32[]{:S(2)}, u32[]{:S(2)}) collective-permute-start(bf16[128,3072]{1,0:T(8,128)(2,1)S(1)} %slice_dynamic-update-slice_fusion.refs_0_), channel_id=1, source_target_pairs={{0,32},{32,0},{64,96},{96,64},{128,160},{160,128},{192,224},{224,1... | collective-permute-start | bytes 2359304 | tf_op jit(solution)/shard_map/ppermute | solution.py:133
  71.1 20.0 %collective-permute-start.8 = (bf16[128,3072]{1,0:T(8,128)(2,1)}, bf16[128,3072]{1,0:T(8,128)(2,1)S(1)}, u32[]{:S(2)}, u32[]{:S(2)}) collective-permute-start(bf16[128,3072]{1,0:T(8,128)(2,1)} %collective-permute-done.refs_1_), channel_id=1, source_target_pairs={{0,32},{32,0},{64,96},{96,64},{128,160},{160,128},{192,224},{224,1... | collective-permute-start | bytes 2359304 | tf_op jit(solution)/shard_map/ppermute | solution.py:133
  73.5 19.5 %collective-permute-start.9 = (bf16[128,3072]{1,0:T(8,128)(2,1)}, bf16[128,3072]{1,0:T(8,128)(2,1)S(1)}, u32[]{:S(2)}, u32[]{:S(2)}) collective-permute-start(bf16[128,3072]{1,0:T(8,128)(2,1)} %collective-permute-done.1.refs_2_), channel_id=1, source_target_pairs={{0,32},{32,0},{64,96},{96,64},{128,160},{160,128},{192,224},{224,1... | collective-permute-start | bytes 2359304 | tf_op jit(solution)/shard_map/ppermute | solution.py:133
  82.5 21.5 %copy-start.2 = (bf16[128,3072]{1,0:T(8,128)(2,1)}, bf16[128,3072]{1,0:T(8,128)(2,1)S(1)}, u32[]{:S(2)}) copy-start(bf16[128,3072]{1,0:T(8,128)(2,1)S(1)} %collective-permute-done.4.refs_5_) | copy-start | bytes 2359300
  83.8 20.2 %copy-start.3 = (bf16[128,3072]{1,0:T(8,128)(2,1)}, bf16[128,3072]{1,0:T(8,128)(2,1)S(1)}, u32[]{:S(2)}) copy-start(bf16[128,3072]{1,0:T(8,128)(2,1)S(1)} %collective-permute-done.5.refs_6_) | copy-start | bytes 2359300
  83.9 15.6 %collective-permute-start.6 = (bf16[128,3072]{1,0:T(8,128)(2,1)S(1)}, bf16[128,3072]{1,0:T(8,128)(2,1)}, u32[]{:S(2)}, u32[]{:S(2)}) collective-permute-start(bf16[128,3072]{1,0:T(8,128)(2,1)S(1)} %broadcast_select_fusion), channel_id=1, source_target_pairs={{0,64},{32,480},{64,128},{96,32},{128,192},{160,96},{192,256},{224... | collective-permute-start | bytes 2359304 | tf_op jit(solution)/shard_map/ppermute | solution.py:134
  86.7 16.0 %collective-permute-start.10 = (bf16[128,3072]{1,0:T(8,128)(2,1)}, bf16[128,3072]{1,0:T(8,128)(2,1)}, u32[]{:S(2)}, u32[]{:S(2)}) collective-permute-start(bf16[128,3072]{1,0:T(8,128)(2,1)} %collective-permute-done.2.refs_3_), channel_id=1, source_target_pairs={{0,32},{32,0},{64,96},{96,64},{128,160},{160,128},{192,224},{224,1... | collective-permute-start | bytes 2359304 | tf_op jit(solution)/shard_map/ppermute | solution.py:133
  88.6 14.1 %collective-permute-start.11 = (bf16[128,3072]{1,0:T(8,128)(2,1)}, bf16[128,3072]{1,0:T(8,128)(2,1)}, u32[]{:S(2)}, u32[]{:S(2)}) collective-permute-start(bf16[128,3072]{1,0:T(8,128)(2,1)} %collective-permute-done.3.refs_4_), channel_id=1, source_target_pairs={{0,32},{32,0},{64,96},{96,64},{128,160},{160,128},{192,224},{224,1... | collective-permute-start | bytes 2359304 | tf_op jit(solution)/shard_map/ppermute | solution.py:133
  91.1 11.7 %collective-permute-start.12 = (bf16[128,3072]{1,0:T(8,128)(2,1)S(1)}, bf16[128,3072]{1,0:T(8,128)(2,1)}, u32[]{:S(2)}, u32[]{:S(2)}) collective-permute-start(bf16[128,3072]{1,0:T(8,128)(2,1)S(1)} %collective-permute-done.4.refs_5_), channel_id=1, source_target_pairs={{0,32},{32,0},{64,96},{96,64},{128,160},{160,128},{192,224},{224,1... | collective-permute-start | bytes 2359304 | tf_op jit(solution)/shard_map/ppermute | solution.py:133
  93.9 8.8 %collective-permute-start.13 = (bf16[128,3072]{1,0:T(8,128)(2,1)S(1)}, bf16[128,3072]{1,0:T(8,128)(2,1)}, u32[]{:S(2)}, u32[]{:S(2)}) collective-permute-start(bf16[128,3072]{1,0:T(8,128)(2,1)S(1)} %collective-permute-done.5.refs_6_), channel_id=1, source_target_pairs={{0,32},{32,0},{64,96},{96,64},{128,160},{160,128},{192,224},{224,1... | collective-permute-start | bytes 2359304 | tf_op jit(solution)/shard_map/ppermute | solution.py:133
  99.5 4.5 %collective-permute-start.14 = (bf16[128,3072]{1,0:T(8,128)(2,1)}, bf16[128,3072]{1,0:T(8,128)(2,1)}, u32[]{:S(2)}, u32[]{:S(2)}) collective-permute-start(bf16[128,3072]{1,0:T(8,128)(2,1)} %collective-permute-done.6.refs_7_), channel_id=1, source_target_pairs={{0,32},{32,0},{64,96},{96,64},{128,160},{160,128},{192,224},{224,1... | collective-permute-start | bytes 2359304 | tf_op jit(solution)/shard_map/ppermute | solution.py:133
  104.0 9.7 %copy-start.1 = (bf16[1,1024,64]{1,2,0:T(8,128)(2,1)S(1)}, bf16[1,1024,64]{1,2,0:T(8,128)(2,1)}, u32[]{:S(2)}) copy-start(bf16[1,1024,64]{1,2,0:T(8,128)(2,1)} %param.18) | copy-start | bytes 393220
  128.5 3.9 %collective-permute-start.15 = (bf16[8,288,128]{2,1,0:T(8,128)(2,1)S(1)}, bf16[8,288,128]{2,1,0:T(8,128)(2,1)S(1)}, u32[]{:S(2)}, u32[]{:S(2)}) collective-permute-start(bf16[8,288,128]{2,1,0:T(8,128)(2,1)S(1)} %get-tuple-element.7), channel_id=1, source_target_pairs={{0,32},{32,0},{64,96},{96,64},{128,160},{160,128},{192,224},{224,1... | collective-permute-start | bytes 1769480 | tf_op jit(solution)/shard_map/ppermute | solution.py:425
  (2 other events, 2.8 us)
